TPU v7x, 32 devices: a whole 2x2x4 slice. The times are simulated.
32 devices in a mesh: layers: 2 (over x), col: 16 (over z, y, core).
Axes of the slice: x: 2, y: 2, z: 4, core: 2. Of those that a mesh axis runs over, the one named last changes fastest.
Arguments:
- dense_weight: float32 [64, 16384], P('layers', 'col'), parts along dimension 0, may hold values from -6 to 6
- start_weight: float32 [64, 16384], P('layers', 'col'), parts along dimension 0, may hold values from -6 to 6
- keep_mask: int32 [64, 16384], P('layers', 'col'), parts along dimension 0, may hold values 0 or 1
- tile_plan: int32 [1056, 2], P(('layers', 'col')), parts along dimension 0, may hold values from 0 to 31, as said below
- hess_tiles: float32 [1056, 512, 512], P(('layers', 'col')), parts along dimension 0, as said below
Outputs:
- weights_out: float32 [64, 16384], P('layers', 'col'), parts along dimension 0
- velocity_out: float32 [64, 16384], P('layers', 'col'), parts along dimension 0
There are 2 independent parts, one for each index of `layers`. A program takes and returns all parts, laid end to end along the dimension named above; each array names one. Nothing has to cross between parts.
Inputs may be any that keep to these rules, and one draw needn't show every extreme that they name: `tile_plan`: each live slot names a tile (a, b) with a >= b, and each of the 32 (33) / 2 lower-triangle tiles is named by exactly one slot; the other slots name (0, 0). `hess_tiles`: the tiles of a symmetric positive definite matrix at the places that tile_plan names; slots that name no tile hold zeros.
All inputs are finite; a program needn't handle non-finite values. No bound on the sum of `keep_mask` on one device may be relied on, other than what follows from the above.
Results may differ from a plain program's by a relative error of at most 0.0001.
Values sent between devices are 32-bit elements; how exact they have to be, the bound alone decides.
No kernel may reach another device: no remote copies, remote signals or barrier semaphores. Data moves between devices by JAX's collectives and lax.ppermute only.
A program may use at most 64 MiB of HBM per device.

v0:
```python
import jax
import jax.numpy as jnp
from jax import lax
from jax.sharding import PartitionSpec as P

ITERS = 2


step_size = 0.15
momentum = 0.6


def add_term(acc, piece, source, target, tile, flipped, allowed):
    order = tile.shape[1]
    span = piece.shape[1]
    tile_dim = 1 if flipped else 0
    relative = source * order
    valid = allowed & (relative >= 0) & (relative < span)

    def apply_term(total):
        block = lax.dynamic_slice_in_dim(piece, jnp.clip(relative, 0, span - order), order, 1)
        contrib = lax.dot_general(
            block,
            tile,
            (((1,), (tile_dim,)), ((), ())),
            precision=lax.Precision.HIGHEST,
            preferred_element_type=jnp.float32,
        )
        current = lax.dynamic_slice_in_dim(total, target * order, order, 1)
        return lax.dynamic_update_slice_in_dim(total, current + contrib, target * order, 1)

    def keep_total(total):
        return total

    return lax.cond(valid, apply_term, keep_total, acc)


def tile_terms(carry, piece, tile_plan, hess_tiles):

    def one_slot(slot, acc):
        row_block = tile_plan[slot, 0]
        col_block = tile_plan[slot, 1]
        tile = hess_tiles[slot]
        acc = add_term(acc, piece, row_block, col_block, tile, False, jnp.bool_(True))
        acc = add_term(acc, piece, col_block, row_block, tile, True, row_block != col_block)
        return acc

    return lax.fori_loop(0, tile_plan.shape[0], one_slot, carry)


def body(dense_weight, start_weight, keep_mask, tile_plan, hess_tiles):
    keep = keep_mask.astype(jnp.float32)
    weights = start_weight
    velocity = jnp.zeros(start_weight.shape, jnp.float32)
    full_width = dense_weight.shape[1] * lax.axis_size("col")
    for step in range(ITERS):
        error = weights - dense_weight
        empty = jnp.zeros((dense_weight.shape[0], full_width), jnp.float32)
        whole = lax.all_gather(error, "col", axis=1, tiled=True)
        partial_grad = tile_terms(empty, whole, tile_plan, hess_tiles)
        gradient = lax.psum_scatter(partial_grad, "col", scatter_dimension=1, tiled=True)
        velocity = momentum * velocity + gradient
        weights = keep * (weights - step_size * velocity)
    return (weights, velocity)


def solution(mesh):
    placed = (
        P("layers", "col"),
        P("layers", "col"),
        P("layers", "col"),
        P(("layers", "col"), None),
        P(("layers", "col"), None, None),
    )
    return jax.shard_map(
        body,
        mesh=mesh,
        in_specs=placed,
        out_specs=(P("layers", "col"), P("layers", "col")),
        check_vma=False,
    )
```

profile of v0, /device:TPU:0, one launch (start us, length us, event | category | flops | bytes accessed | tf_op | source)
XLA Modules:
  0.0 841.8 jit_solution(4746795135078019642)
XLA Ops:
  8.9 46.0 %all-gather.3.cloned.1.call-done = f32[32,16384]{1,0:T(8,128)} async-done(((f32[32,1024]{1,0:T(8,128)}), f32[32,16384]{1,0:T(8,128)}) %all-gather.3.cloned.1.call-update) | async-done | bytes 2097168 | tf_op jit(solution)/shard_map/all_gather | solution.py:59
  55.1 298.4 %while.32 = (s32[]{:T(128)}, f32[32,16384]{1,0:T(8,128)S(1)}, s32[33,2]{0,1:T(2,128)S(1)}, f32[33,512,512]{2,1,0:T(8,128)}, f32[32,16384]{1,0:T(8,128)}, /*index=5*/s32[]{:T(128)}, s32[]{:T(128)}, s32[]{:T(128)}, s32[]{:T(128)}) while((s32[]{:T(128)}, f32[32,16384]{1,0:T(8,128)S(1)}, s32[33,2]{0,1:T(2,128)S(1)}, f32[33,512,512]{2,1,0:T(8,128)}, ...), condition=%wide.region_5.6_spmd, body=%wide.region_0.5_spmd.sunk | while | flops 201359392 | bytes 4587977 | solution.py:48
  61.9 2.6 conditional.9
  71.3 2.6 conditional.9
  80.8 2.6 conditional.9
  97.0 2.6 conditional.9
  120.1 2.6 conditional.9
  129.5 2.6 conditional.9
  145.8 2.6 conditional.9
  155.2 2.6 conditional.9
  164.7 2.6 conditional.9
  174.1 2.6 conditional.9
  284.7 2.6 conditional.9
  294.2 2.6 conditional.9
  303.6 2.6 conditional.9
  313.1 2.6 conditional.9
  322.5 2.6 conditional.9
  331.9 2.6 conditional.9
  341.4 2.6 conditional.9
  350.8 2.6 conditional.9
  354.9 71.8 %reduce-scatter.3.cloned.1.call-done = f32[32,1024]{1,0:T(8,128)} async-done(((f32[32,16384]{1,0:T(8,128)}), f32[32,1024]{1,0:T(8,128)}) %reduce-scatter.3.cloned.1.call-update) | async-done | bytes 131088 | tf_op jit(solution)/shard_map/reduce_scatter | solution.py:61
  428.3 41.8 %all-gather.5.cloned.1.call-done = f32[32,16384]{1,0:T(8,128)} async-done(((f32[32,1024]{1,0:T(8,128)}), f32[32,16384]{1,0:T(8,128)}) %all-gather.5.cloned.1.call-update) | async-done | bytes 2097168 | tf_op jit(solution)/shard_map/all_gather | solution.py:59
  470.3 290.5 %while.33 = (s32[]{:T(128)}, f32[32,16384]{1,0:T(8,128)S(1)}, s32[33,2]{0,1:T(2,128)S(1)}, f32[33,512,512]{2,1,0:T(8,128)}, f32[32,16384]{1,0:T(8,128)}, /*index=5*/s32[]{:T(128)}, s32[]{:T(128)}, s32[]{:T(128)}, s32[]{:T(128)}) while((s32[]{:T(128)}, f32[32,16384]{1,0:T(8,128)S(1)}, s32[33,2]{0,1:T(2,128)S(1)}, f32[33,512,512]{2,1,0:T(8,128)}, ...), condition=%wide.region_12.13_spmd, body=%wide.region_7.12_spmd.sunk | while | flops 201359392 | bytes 4587977 | solution.py:48
  762.1 71.5 %reduce-scatter.5.cloned.1.call-done = f32[32,1024]{1,0:T(8,128)} async-done(((f32[32,16384]{1,0:T(8,128)}), f32[32,1024]{1,0:T(8,128)}) %reduce-scatter.5.cloned.1.call-update) | async-done | bytes 131088 | tf_op jit(solution)/shard_map/reduce_scatter | solution.py:61
  (395 shorter events, 597.5 us)
Async XLA Ops:
  7.2 47.9 %copy-start.6 = (s32[33,2]{0,1:T(2,128)S(1)}, s32[33,2]{0,1:T(2,128)}, u32[]{:S(2)}) copy-start(s32[33,2]{0,1:T(2,128)} %param.20) | copy-start | bytes 796
  7.2 47.8 %all-gather.3.cloned.1.call-start = ((), (), s32[]{:S(2)}) async-start(), calls=%async_computation.2 | async-start | bytes 2228224 | tf_op jit(solution)/shard_map/all_gather | solution.py:59
  8.9 417.8 %reduce-scatter.3.cloned.1.call-start = ((), (), s32[]{:S(2)}) async-start(), calls=%async_computation.3 | async-start | bytes 2228224 | tf_op jit(solution)/shard_map/reduce_scatter | solution.py:61
  353.5 1.3 copy-start.1
  353.5 73.2 %copy-start.2 = (f32[32,1024]{1,0:T(8,128)S(1)}, f32[32,1024]{1,0:T(8,128)}, u32[]{:S(2)}) copy-start(f32[32,1024]{1,0:T(8,128)} %param.18) | copy-start | bytes 393220
  353.5 73.2 %copy-start.3 = (f32[32,1024]{1,0:T(8,128)S(1)}, f32[32,1024]{1,0:T(8,128)}, u32[]{:S(2)}) copy-start(f32[32,1024]{1,0:T(8,128)} %param.17) | copy-start | bytes 393220
  353.5 73.2 %copy-start.4 = (s32[32,1024]{1,0:T(8,128)S(1)}, s32[32,1024]{1,0:T(8,128)}, u32[]{:S(2)}) copy-start(s32[32,1024]{1,0:T(8,128)} %param.19) | copy-start | bytes 393220
  354.8 115.3 %all-gather.5.cloned.1.call-start = ((), (), s32[]{:S(2)}) async-start(), calls=%async_computation.4 | async-start | bytes 2228224 | tf_op jit(solution)/shard_map/all_gather | solution.py:59
  428.3 405.3 %reduce-scatter.5.cloned.1.call-start = ((), (), s32[]{:S(2)}) async-start(), calls=%async_computation.5 | async-start | bytes 2228224 | tf_op jit(solution)/shard_map/reduce_scatter | solution.py:61
  760.8 1.3 copy-start
  760.8 72.8 %copy-start.5 = (f32[32,1024]{1,0:T(8,128)S(1)}, f32[32,1024]{1,0:T(8,128)}, u32[]{:S(2)}) copy-start(f32[32,1024]{1,0:T(8,128)} %reduce-scatter.3.cloned.1.call-done) | copy-start | bytes 393220
Sparse Core Ops, SparseCore 0:
  10.8 44.1 all-gather.2
  354.9 71.6 reduce-scatter.2
  429.6 40.4 all-gather.4
  762.2 71.3 reduce-scatter.4
where the time goes:
time: 855 us; the launch traced here: 842 us
  loops' own time  248 us (29%)
  waiting for transfers between devices  231 us (27%)
  matrix products  216 us (25%)
  local copies, waits for them, and re-layouts  128 us (15%)
  between operations  13.9 us (2%)
    dot_general x122, matrix products, apply_term(): lax.dot_general(block, tile, (((1,), (tile_dim,)), ((), ())), precision=l...  216 us
    another operation x2, loops' own time, tile_terms(): return lax.fori_loop(0, tile_plan.shape[0], one_slot, carry)  168 us
    reduce_scatter x2, waiting for transfers between devices, body(): lax.psum_scatter(partial_grad, 'col', scatter_dimension=1, tiled=True)  143 us
    all_gather x2, waiting for transfers between devices, body(): whole = lax.all_gather(error, 'col', axis=1, tiled=True)  87.8 us
    squeeze x66, local copies, waits for them, and re-layouts, one_slot(): tile = hess_tiles[slot]  85.8 us
    another operation x132, loops' own time, add_term(): return lax.cond(valid, apply_term, keep_total, acc)  79.8 us
    dynamic_slice x66, local copies, waits for them, and re-layouts, one_slot(): col_block = tile_plan[slot, 1]  39.7 us
  transfers between devices with their start and end apart: 4, of which 4 were waited for; matrix products, arithmetic and copies ran while one was open for 0% of the time, Pallas kernels for 0%

commit v1 on v0

v1 whole, which is shorter than its diff:
```python
import functools

import jax
import jax.numpy as jnp
from jax import lax
from jax.experimental import pallas as pl
from jax.experimental.pallas import tpu as pltpu
from jax.sharding import PartitionSpec as P

ITERS = 2
MIB = 2**20

step_size = 0.15
momentum = 0.6

IN_VMEM = pl.BlockSpec(memory_space=pltpu.VMEM)


def stages_of(count):
    bits = [1 << i for i in range(count.bit_length() - 1)]
    near, far = bits[:2], bits[2:]
    groups = [far[i : i + 2] for i in range(0, len(far), 2)]
    return groups[::-1] + [[b] for b in near[::-1]]


def masks_of(group):
    masks = [0]
    for bit in group:
        masks += [m | bit for m in masks]
    return masks[1:]


def swap(x, mask):
    count = lax.axis_size("col")
    return lax.ppermute(x, "col", [(i, i ^ mask) for i in range(count)])


def gather(own):
    pieces = {0: own}
    for group in stages_of(lax.axis_size("col")):
        held = list(pieces)
        for mask in reversed(masks_of(group)):
            for p in held:
                pieces[p | mask] = swap(pieces[p], mask)
    return [pieces[p] for p in range(len(pieces))]


def scatter_sum(parts):
    held = dict(enumerate(parts))
    for group in reversed(stages_of(len(parts))):
        masks = masks_of(group)
        every = sum(group)
        kept = [p for p in held if not p & every]
        terms = {p: [held[p]] for p in kept}
        for p in reversed(kept):
            for mask in reversed(masks):
                terms[p].append(swap(held[p | mask], mask))
        if kept == [0]:
            return terms[0]
        held = {p: sum(terms[p][1:], terms[p][0]) for p in kept}


def split_kernel(tile_ref, split_ref):
    step = pl.program_id(0)
    for j in range(tile_ref.shape[0]):
        tile = tile_ref[j]
        high = tile.astype(jnp.bfloat16)
        slot = step * tile_ref.shape[0] + j
        split_ref[slot, 0] = high
        split_ref[slot, 1] = (tile - high.astype(jnp.float32)).astype(jnp.bfloat16)


def split_tiles(tiles):
    slots, order, _ = tiles.shape
    together = 3 if slots % 3 == 0 else 1
    return pl.pallas_call(
        split_kernel,
        grid=(slots // together,),
        in_specs=[pl.BlockSpec((together, order, order), lambda i: (i, 0, 0))],
        out_specs=IN_VMEM,
        out_shape=pltpu.VMEM((slots, 2, order, order), jnp.bfloat16),
        compiler_params=pltpu.CompilerParams(vmem_limit_bytes=16 * MIB),
        cost_estimate=pl.CostEstimate(flops=0, bytes_accessed=slots * order * order * 4, transcendentals=0),
        name="split_tiles",
    )(tiles)


def places(owner, order, width):
    if width >= order:
        each = width // order
        return [(slice(j * order, (j + 1) * order), owner * each + j, slice(None)) for j in range(each)]
    each = order // width
    start = pl.multiple_of(lax.rem(owner, each) * width, width)
    return [(slice(None), lax.div(owner, each), pl.ds(start, width))]


def product_kernel(count, plan, split, *refs):
    ins, outs, (err, acc) = refs[:count], refs[count : 2 * count], refs[2 * count :]
    blocks, rows, order = acc.shape
    width = ins[0].shape[1]
    me = lax.axis_index("col")
    for p in range(count):
        for part, block, columns in places(me ^ p, order, width):
            piece = ins[p][:, part]
            high = piece.astype(jnp.bfloat16)
            err[block, :rows, columns] = high
            err[block, rows:, columns] = (piece - high.astype(jnp.float32)).astype(jnp.bfloat16)
    acc[...] = jnp.zeros(acc.shape, jnp.float32)

    def one_slot(slot, carry):
        row_block = plan[slot, 0]
        col_block = plan[slot, 1]
        high = split[slot, 0]
        low = split[slot, 1]
        for source, target, dim, live in (
            (row_block, col_block, 0, None),
            (col_block, row_block, 1, row_block != col_block),
        ):
            dims = (((1,), (dim,)), ((), ()))
            both = err[source]
            lead = lax.dot_general(both, high, dims, preferred_element_type=jnp.float32)
            rest = lax.dot_general(both[:rows], low, dims, preferred_element_type=jnp.float32)
            term = lead[:rows] + (lead[rows:] + rest)
            if live is not None:
                term = jnp.where(live, term, 0.0)
            acc[target] += term
        return carry

    lax.fori_loop(0, split.shape[0], one_slot, 0, unroll=3)
    for p in range(count):
        for part, block, columns in places(me ^ p, order, width):
            outs[p][:, part] = acc[block, :, columns]


def product(plan, split, pieces):
    slots, _, order, _ = split.shape
    count = len(pieces)
    rows, width = pieces[0].shape
    blocks = count * width // order
    return pl.pallas_call(
        functools.partial(product_kernel, count),
        in_specs=[pl.BlockSpec(memory_space=pltpu.SMEM)] + [IN_VMEM] * (1 + count),
        out_specs=[IN_VMEM] * count,
        out_shape=[jax.ShapeDtypeStruct((rows, width), jnp.float32)] * count,
        scratch_shapes=[
            pltpu.VMEM((blocks, 2 * rows, order), jnp.bfloat16),
            pltpu.VMEM((blocks, rows, order), jnp.float32),
        ],
        compiler_params=pltpu.CompilerParams(vmem_limit_bytes=16 * MIB),
        cost_estimate=pl.CostEstimate(
            flops=slots * 12 * rows * order * order, bytes_accessed=8 * blocks * rows * order, transcendentals=0
        ),
        name="hessian_product",
    )(plan, pltpu.with_memory_space_constraint(split, pltpu.VMEM), *pieces)


def body(dense_weight, start_weight, keep_mask, tile_plan, hess_tiles):
    keep = keep_mask.astype(jnp.float32)
    weights = start_weight
    velocity = jnp.zeros(start_weight.shape, jnp.float32)
    split = split_tiles(hess_tiles)
    for step in range(ITERS):
        pieces = gather(weights - dense_weight)
        terms = scatter_sum(product(tile_plan, split, pieces))
        gradient = sum(terms[1:], terms[0])
        velocity = momentum * velocity + gradient
        weights = keep * (weights - step_size * velocity)
    return (weights, velocity)


def solution(mesh):
    placed = (
        P("layers", "col"),
        P("layers", "col"),
        P("layers", "col"),
        P(("layers", "col"), None),
        P(("layers", "col"), None, None),
    )
    return jax.shard_map(
        body,
        mesh=mesh,
        in_specs=placed,
        out_specs=(P("layers", "col"), P("layers", "col")),
        check_vma=False,
    )
```

time: 855 us -> 156 us (0.18); the launches traced: 842 us -> 155 us
  loops' own time: 248 us -> 0 us
  matrix products: 216 us -> 0 us
  waiting for transfers between devices: 231 us -> 55.6 us
  local copies, waits for them, and re-layouts: 128 us -> 0.79 us
  Pallas kernels: 0 us -> 52.3 us
  starting transfers between devices: 0.16 us -> 43.6 us
  between operations: 13.9 us -> 0.94 us
    another operation x134 -> x0, loops' own time: 248 us -> none  [the longest x2 168 us: tile_terms(): return lax.fori_loop(0, tile_plan.shape[0], one_slot, carry)]
    dot_general x122 -> x0, matrix products: 216 us -> none  [apply_term(): lax.dot_general(block, tile, (((1,), (tile_dim,)), ((), ())), precision=l...]
    reduce_scatter x2 -> x0, waiting for transfers between devices: 143 us -> none  [body(): lax.psum_scatter(partial_grad, 'col', scatter_dimension=1, tiled=True)]
    all_gather x2 -> x0, waiting for transfers between devices: 87.8 us -> none  [body(): whole = lax.all_gather(error, 'col', axis=1, tiled=True)]
    squeeze x66 -> x0, local copies, waits for them, and re-layouts: 85.8 us -> none  [one_slot(): tile = hess_tiles[slot]]
    ppermute x0 -> x60, waiting for transfers between devices: none -> 55.6 us  [swap(): return lax.ppermute(x, 'col', [(i, i ^ mask) for i in range(count)])]
    pallas_call x0 -> x3, Pallas kernels: none -> 52.3 us  [the longest x2 37.5 us: product(): pl.pallas_call(functools.partial(product_kernel, count), in_specs=[pl.Blo...]
    ppermute x0 -> x60, starting transfers between devices: none -> 43.6 us  [swap(): return lax.ppermute(x, 'col', [(i, i ^ mask) for i in range(count)])]
  transfers between devices with their start and end apart: 4 -> 60, of which waited for: 4 -> 18; matrix products, arithmetic and copies ran while one was open for 0% -> 1% of each run, Pallas kernels for 0% -> 9%
where the time goes in v1:
time: 156 us; the launch traced here: 155 us
  waiting for transfers between devices  55.6 us (36%)
  Pallas kernels  52.3 us (34%)
  starting transfers between devices  43.6 us (28%)
  other arithmetic  2.15 us (1%)
    ppermute x60, waiting for transfers between devices, swap(): return lax.ppermute(x, 'col', [(i, i ^ mask) for i in range(count)])  55.6 us
    ppermute x60, starting transfers between devices, swap(): return lax.ppermute(x, 'col', [(i, i ^ mask) for i in range(count)])  43.6 us
    pallas_call x2, Pallas kernels, product(): pl.pallas_call(functools.partial(product_kernel, count), in_specs=[pl.Blo...  37.5 us
    pallas_call x1, Pallas kernels, split_tiles(): pl.pallas_call(split_kernel, grid=(slots // together,), in_specs=[pl.Bloc...  14.7 us
  transfers between devices with their start and end apart: 60, of which 18 were waited for; matrix products, arithmetic and copies ran while one was open for 1% of the time, Pallas kernels for 9%

profile of v1, /device:TPU:0, one launch (start us, length us, event | category | flops | bytes accessed | tf_op | source)
XLA Modules:
  0.0 155.3 jit_solution(2132620473119237683)
XLA Ops:
  1.6 5.1 %collective-permute-start.11 = (f32[32,1024]{1,0:T(8,128)S(1)}, f32[32,1024]{1,0:T(8,128)S(1)}, u32[]{:S(2)}, u32[]{:S(2)}) collective-permute-start(f32[32,1024]{1,0:T(8,128)S(1)} %sub.12.refs_0_), channel_id=1, source_target_pairs={{0,12},{1,13},{2,14},{3,15},{4,8},{5,9},{6,10},{7,11},{8,4},{9,5},... | collective-permute-start | bytes 393224 | tf_op jit(solution)/shard_map/ppermute | solution.py:35
  9.0 2.1 %collective-permute-done.11.refs_12_ = f32[32,1024]{1,0:T(8,128)S(1)} collective-permute-done((f32[32,1024]{1,0:T(8,128)S(1)}, f32[32,1024]{1,0:T(8,128)S(1)}, u32[]{:S(2)}, u32[]{:S(2)}) %collective-permute-start.11) | collective-permute-done | bytes 131104 | tf_op jit(solution)/shard_map/ppermute | solution.py:35
  12.9 4.9 %collective-permute-done.7.refs_8_ = f32[32,1024]{1,0:T(8,128)S(1)} collective-permute-done((f32[32,1024]{1,0:T(8,128)S(1)}, f32[32,1024]{1,0:T(8,128)S(1)}, u32[]{:S(2)}, u32[]{:S(2)}) %collective-permute-start.7) | collective-permute-done | bytes 131104 | tf_op jit(solution)/shard_map/ppermute | solution.py:35
  20.6 3.5 %collective-permute-done.9.refs_10_ = f32[32,1024]{1,0:T(8,128)S(1)} collective-permute-done((f32[32,1024]{1,0:T(8,128)S(1)}, f32[32,1024]{1,0:T(8,128)S(1)}, u32[]{:S(2)}, u32[]{:S(2)}) %collective-permute-start.9) | collective-permute-done | bytes 131104 | tf_op jit(solution)/shard_map/ppermute | solution.py:35
  27.3 14.7 %split_tiles.1.split = bf16[33,2,512,512]{3,2,1,0:T(8,128)(2,1)S(1)} custom-call(f32[33,512,512]{2,1,0:T(8,128)} %tile_ref.1), custom_call_target="tpu_custom_call" | custom-call | bytes 34603008 | tf_op jit(solution)/shard_map/split_tiles/pallas_call | solution.py:76
  42.1 18.8 %hessian_product.2 = (f32[32,1024]{1,0:T(8,128)S(1)}, f32[32,1024]{1,0:T(8,128)S(1)}, f32[32,1024]{1,0:T(8,128)S(1)}, f32[32,1024]{1,0:T(8,128)S(1)}, f32[32,102...) custom-call(s32[33,2]{1,0:T(8,128)S(1)} %copy.7.plan, ...), custom_call_target="tpu_custom_call" | custom-call | flops 3321888768 | bytes 4194304 | tf_op jit(solution)/shard_map/hessian_product/pallas_call | solution.py:140
  65.5 3.1 %collective-permute-done.20 = f32[32,1024]{1,0:T(8,128)S(1)} collective-permute-done((f32[32,1024]{1,0:T(8,128)S(1)}, f32[32,1024]{1,0:T(8,128)S(1)}, u32[]{:S(2)}, u32[]{:S(2)}) %collective-permute-start.20) | collective-permute-done | bytes 131104 | tf_op jit(solution)/shard_map/ppermute | solution.py:35
  70.7 4.3 %collective-permute-done.24 = f32[32,1024]{1,0:T(8,128)S(1)} collective-permute-done((f32[32,1024]{1,0:T(8,128)S(1)}, f32[32,1024]{1,0:T(8,128)S(1)}, u32[]{:S(2)}, u32[]{:S(2)}) %collective-permute-start.24) | collective-permute-done | bytes 131104 | tf_op jit(solution)/shard_map/ppermute | solution.py:35
  75.0 2.5 %collective-permute-start.21 = (f32[32,1024]{1,0:T(8,128)S(1)}, f32[32,1024]{1,0:T(8,128)S(1)}, u32[]{:S(2)}, u32[]{:S(2)}) collective-permute-start(f32[32,1024]{1,0:T(8,128)S(1)} %add_add_fusion.7), channel_id=1, source_target_pairs={{0,12},{1,13},{2,14},{3,15},{4,8},{5,9},{6,10},{7,11},{8,4},{9,5},... | collective-permute-start | bytes 393224 | tf_op jit(solution)/shard_map/ppermute | solution.py:35
  77.7 1.9 %collective-permute-start.29 = (f32[32,1024]{1,0:T(8,128)S(1)}, f32[32,1024]{1,0:T(8,128)S(1)}, u32[]{:S(2)}, u32[]{:S(2)}) collective-permute-start(f32[32,1024]{1,0:T(8,128)S(1)} %add_add_fusion.4), channel_id=1, source_target_pairs={{0,4},{1,5},{2,6},{3,7},{4,0},{5,1},{6,2},{7,3},{8,12},{9,13},{10,... | collective-permute-start | bytes 393224 | tf_op jit(solution)/shard_map/ppermute | solution.py:35
  79.6 3.5 %collective-permute-done.21 = f32[32,1024]{1,0:T(8,128)S(1)} collective-permute-done((f32[32,1024]{1,0:T(8,128)S(1)}, f32[32,1024]{1,0:T(8,128)S(1)}, u32[]{:S(2)}, u32[]{:S(2)}) %collective-permute-start.21) | collective-permute-done | bytes 131104 | tf_op jit(solution)/shard_map/ppermute | solution.py:35
  83.1 4.2 %collective-permute-done.25 = f32[32,1024]{1,0:T(8,128)S(1)} collective-permute-done((f32[32,1024]{1,0:T(8,128)S(1)}, f32[32,1024]{1,0:T(8,128)S(1)}, u32[]{:S(2)}, u32[]{:S(2)}) %collective-permute-start.25) | collective-permute-done | bytes 131104 | tf_op jit(solution)/shard_map/ppermute | solution.py:35
  87.4 3.0 %collective-permute-start.41 = (f32[32,1024]{1,0:T(8,128)S(1)}, f32[32,1024]{1,0:T(8,128)S(1)}, u32[]{:S(2)}, u32[]{:S(2)}) collective-permute-start(f32[32,1024]{1,0:T(8,128)S(1)} %get-tuple-element.68.refs_0_), channel_id=1, source_target_pairs={{0,12},{1,13},{2,14},{3,15},{4,8},{5,9},{6,10},{7,11},{8,4},{9,5},... | collective-permute-start | bytes 393224 | tf_op jit(solution)/shard_map/ppermute | solution.py:35
  92.7 3.0 %collective-permute-done.41.refs_12_ = f32[32,1024]{1,0:T(8,128)S(1)} collective-permute-done((f32[32,1024]{1,0:T(8,128)S(1)}, f32[32,1024]{1,0:T(8,128)S(1)}, u32[]{:S(2)}, u32[]{:S(2)}) %collective-permute-start.41) | collective-permute-done | bytes 131104 | tf_op jit(solution)/shard_map/ppermute | solution.py:35
  96.5 3.8 %collective-permute-done.37.refs_8_ = f32[32,1024]{1,0:T(8,128)S(1)} collective-permute-done((f32[32,1024]{1,0:T(8,128)S(1)}, f32[32,1024]{1,0:T(8,128)S(1)}, u32[]{:S(2)}, u32[]{:S(2)}) %collective-permute-start.37) | collective-permute-done | bytes 131104 | tf_op jit(solution)/shard_map/ppermute | solution.py:35
  103.2 3.5 %collective-permute-done.39.refs_10_ = f32[32,1024]{1,0:T(8,128)S(1)} collective-permute-done((f32[32,1024]{1,0:T(8,128)S(1)}, f32[32,1024]{1,0:T(8,128)S(1)}, u32[]{:S(2)}, u32[]{:S(2)}) %collective-permute-start.39) | collective-permute-done | bytes 131104 | tf_op jit(solution)/shard_map/ppermute | solution.py:35
  107.2 1.9 %collective-permute-done.35.refs_6_ = f32[32,1024]{1,0:T(8,128)S(1)} collective-permute-done((f32[32,1024]{1,0:T(8,128)S(1)}, f32[32,1024]{1,0:T(8,128)S(1)}, u32[]{:S(2)}, u32[]{:S(2)}) %collective-permute-start.35) | collective-permute-done | bytes 131104 | tf_op jit(solution)/shard_map/ppermute | solution.py:35
  110.5 18.7 %hessian_product.3 = (f32[32,1024]{1,0:T(8,128)S(1)}, f32[32,1024]{1,0:T(8,128)S(1)}, f32[32,1024]{1,0:T(8,128)S(1)}, f32[32,1024]{1,0:T(8,128)S(1)}, f32[32,102...) custom-call(s32[33,2]{1,0:T(8,128)S(1)} %copy.7.plan, ...), custom_call_target="tpu_custom_call" | custom-call | flops 3321888768 | bytes 4194304 | tf_op jit(solution)/shard_map/hessian_product/pallas_call | solution.py:140
  133.6 3.5 %collective-permute-done.50 = f32[32,1024]{1,0:T(8,128)S(1)} collective-permute-done((f32[32,1024]{1,0:T(8,128)S(1)}, f32[32,1024]{1,0:T(8,128)S(1)}, u32[]{:S(2)}, u32[]{:S(2)}) %collective-permute-start.50) | collective-permute-done | bytes 131104 | tf_op jit(solution)/shard_map/ppermute | solution.py:35
  137.1 2.1 %collective-permute-start.58 = (f32[32,1024]{1,0:T(8,128)S(1)}, f32[32,1024]{1,0:T(8,128)S(1)}, u32[]{:S(2)}, u32[]{:S(2)}) collective-permute-start(f32[32,1024]{1,0:T(8,128)S(1)} %add.120), channel_id=1, source_target_pairs={{0,2},{1,3},{2,0},{3,1},{4,6},{5,7},{6,4},{7,5},{8,10},{9,11},{10,... | collective-permute-start | bytes 393224 | tf_op jit(solution)/shard_map/ppermute | solution.py:35
  139.2 4.1 %collective-permute-done.54 = f32[32,1024]{1,0:T(8,128)S(1)} collective-permute-done((f32[32,1024]{1,0:T(8,128)S(1)}, f32[32,1024]{1,0:T(8,128)S(1)}, u32[]{:S(2)}, u32[]{:S(2)}) %collective-permute-start.54) | collective-permute-done | bytes 131104 | tf_op jit(solution)/shard_map/ppermute | solution.py:35
  145.8 2.1 %collective-permute-start.59 = (f32[32,1024]{1,0:T(8,128)S(1)}, f32[32,1024]{1,0:T(8,128)S(1)}, u32[]{:S(2)}, u32[]{:S(2)}) collective-permute-start(f32[32,1024]{1,0:T(8,128)S(1)} %add_add_fusion.1), channel_id=1, source_target_pairs={{0,4},{1,5},{2,6},{3,7},{4,0},{5,1},{6,2},{7,3},{8,12},{9,13},{10,... | collective-permute-start | bytes 393224 | tf_op jit(solution)/shard_map/ppermute | solution.py:35
  147.9 2.7 %collective-permute-done.51 = f32[32,1024]{1,0:T(8,128)S(1)} collective-permute-done((f32[32,1024]{1,0:T(8,128)S(1)}, f32[32,1024]{1,0:T(8,128)S(1)}, u32[]{:S(2)}, u32[]{:S(2)}) %collective-permute-start.51) | collective-permute-done | bytes 131104 | tf_op jit(solution)/shard_map/ppermute | solution.py:35
  150.6 4.0 %collective-permute-done.55 = f32[32,1024]{1,0:T(8,128)S(1)} collective-permute-done((f32[32,1024]{1,0:T(8,128)S(1)}, f32[32,1024]{1,0:T(8,128)S(1)}, u32[]{:S(2)}, u32[]{:S(2)}) %collective-permute-start.55) | collective-permute-done | bytes 131104 | tf_op jit(solution)/shard_map/ppermute | solution.py:35
  (123 shorter events, 33.3 us)
Async XLA Ops:
  1.6 9.5 %collective-permute-start.11 = (f32[32,1024]{1,0:T(8,128)S(1)}, f32[32,1024]{1,0:T(8,128)S(1)}, u32[]{:S(2)}, u32[]{:S(2)}) collective-permute-start(f32[32,1024]{1,0:T(8,128)S(1)} %sub.12.refs_0_), channel_id=1, source_target_pairs={{0,12},{1,13},{2,14},{3,15},{4,8},{5,9},{6,10},{7,11},{8,4},{9,5},... | collective-permute-start | bytes 393224 | tf_op jit(solution)/shard_map/ppermute | solution.py:35
  6.7 11.1 %collective-permute-start.7 = (f32[32,1024]{1,0:T(8,128)S(1)}, f32[32,1024]{1,0:T(8,128)S(1)}, u32[]{:S(2)}, u32[]{:S(2)}) collective-permute-start(f32[32,1024]{1,0:T(8,128)S(1)} %sub.12.refs_0_), channel_id=1, source_target_pairs={{0,8},{1,9},{2,10},{3,11},{4,12},{5,13},{6,14},{7,15},{8,0},{9,1},... | collective-permute-start | bytes 393224 | tf_op jit(solution)/shard_map/ppermute | solution.py:35
  6.7 11.1 %collective-permute-start.3 = (f32[32,1024]{1,0:T(8,128)S(1)}, f32[32,1024]{1,0:T(8,128)S(1)}, u32[]{:S(2)}, u32[]{:S(2)}) collective-permute-start(f32[32,1024]{1,0:T(8,128)S(1)} %sub.12.refs_0_), channel_id=1, source_target_pairs={{0,4},{1,5},{2,6},{3,7},{4,0},{5,1},{6,2},{7,3},{8,12},{9,13},{10,... | collective-permute-start | bytes 393224 | tf_op jit(solution)/shard_map/ppermute | solution.py:35
  7.4 12.0 %collective-permute-start.1 = (f32[32,1024]{1,0:T(8,128)S(1)}, f32[32,1024]{1,0:T(8,128)S(1)}, u32[]{:S(2)}, u32[]{:S(2)}) collective-permute-start(f32[32,1024]{1,0:T(8,128)S(1)} %sub.12.refs_0_), channel_id=1, source_target_pairs={{0,2},{1,3},{2,0},{3,1},{4,6},{5,7},{6,4},{7,5},{8,10},{9,11},{10,... | collective-permute-start | bytes 393224 | tf_op jit(solution)/shard_map/ppermute | solution.py:35
  9.0 10.5 %collective-permute-start = (f32[32,1024]{1,0:T(8,128)S(1)}, f32[32,1024]{1,0:T(8,128)S(1)}, u32[]{:S(2)}, u32[]{:S(2)}) collective-permute-start(f32[32,1024]{1,0:T(8,128)S(1)} %sub.12.refs_0_), channel_id=1, source_target_pairs={{0,1},{1,0},{2,3},{3,2},{4,5},{5,4},{6,7},{7,6},{8,9},{9,8},{10,11... | collective-permute-start | bytes 393224 | tf_op jit(solution)/shard_map/ppermute | solution.py:35
  11.2 8.9 %collective-permute-start.13 = (f32[32,1024]{1,0:T(8,128)S(1)}, f32[32,1024]{1,0:T(8,128)S(1)}, u32[]{:S(2)}, u32[]{:S(2)}) collective-permute-start(f32[32,1024]{1,0:T(8,128)S(1)} %collective-permute-done.11.refs_12_), channel_id=1, source_target_pairs={{0,2},{1,3},{2,0},{3,1},{4,6},{5,7},{6,4},{7,5},{8,10},{9,11},{10,... | collective-permute-start | bytes 393224 | tf_op jit(solution)/shard_map/ppermute | solution.py:35
  20.1 22.0 %collective-permute-start.4 = (f32[32,1024]{1,0:T(8,128)S(1)}, f32[32,1024]{1,0:T(8,128)S(1)}, u32[]{:S(2)}, u32[]{:S(2)}) collective-permute-start(f32[32,1024]{1,0:T(8,128)S(1)} %collective-permute-done.3.refs_4_), channel_id=1, source_target_pairs={{0,1},{1,0},{2,3},{3,2},{4,5},{5,4},{6,7},{7,6},{8,9},{9,8},{10,11... | collective-permute-start | bytes 393224 | tf_op jit(solution)/shard_map/ppermute | solution.py:35
  20.1 22.0 %collective-permute-start.2 = (f32[32,1024]{1,0:T(8,128)S(1)}, f32[32,1024]{1,0:T(8,128)S(1)}, u32[]{:S(2)}, u32[]{:S(2)}) collective-permute-start(f32[32,1024]{1,0:T(8,128)S(1)} %collective-permute-done.1.refs_2_), channel_id=1, source_target_pairs={{0,1},{1,0},{2,3},{3,2},{4,5},{5,4},{6,7},{7,6},{8,9},{9,8},{10,11... | collective-permute-start | bytes 393224 | tf_op jit(solution)/shard_map/ppermute | solution.py:35
  24.1 18.0 %collective-permute-start.14 = (f32[32,1024]{1,0:T(8,128)S(1)}, f32[32,1024]{1,0:T(8,128)S(1)}, u32[]{:S(2)}, u32[]{:S(2)}) collective-permute-start(f32[32,1024]{1,0:T(8,128)S(1)} %collective-permute-done.13.refs_14_), channel_id=1, source_target_pairs={{0,1},{1,0},{2,3},{3,2},{4,5},{5,4},{6,7},{7,6},{8,9},{9,8},{10,11... | collective-permute-start | bytes 393224 | tf_op jit(solution)/shard_map/ppermute | solution.py:35
  24.1 18.0 %collective-permute-start.10 = (f32[32,1024]{1,0:T(8,128)S(1)}, f32[32,1024]{1,0:T(8,128)S(1)}, u32[]{:S(2)}, u32[]{:S(2)}) collective-permute-start(f32[32,1024]{1,0:T(8,128)S(1)} %collective-permute-done.9.refs_10_), channel_id=1, source_target_pairs={{0,1},{1,0},{2,3},{3,2},{4,5},{5,4},{6,7},{7,6},{8,9},{9,8},{10,11... | collective-permute-start | bytes 393224 | tf_op jit(solution)/shard_map/ppermute | solution.py:35
  26.5 15.6 %collective-permute-start.6 = (f32[32,1024]{1,0:T(8,128)S(1)}, f32[32,1024]{1,0:T(8,128)S(1)}, u32[]{:S(2)}, u32[]{:S(2)}) collective-permute-start(f32[32,1024]{1,0:T(8,128)S(1)} %collective-permute-done.5.refs_6_), channel_id=1, source_target_pairs={{0,1},{1,0},{2,3},{3,2},{4,5},{5,4},{6,7},{7,6},{8,9},{9,8},{10,11... | collective-permute-start | bytes 393224 | tf_op jit(solution)/shard_map/ppermute | solution.py:35
  64.1 15.5 %collective-permute-start.15 = (f32[32,1024]{1,0:T(8,128)S(1)}, f32[32,1024]{1,0:T(8,128)S(1)}, u32[]{:S(2)}, u32[]{:S(2)}) collective-permute-start(f32[32,1024]{1,0:T(8,128)S(1)} %get-tuple-element.35), channel_id=1, source_target_pairs={{0,1},{1,0},{2,3},{3,2},{4,5},{5,4},{6,7},{7,6},{8,9},{9,8},{10,11... | collective-permute-start | bytes 393224 | tf_op jit(solution)/shard_map/ppermute | solution.py:35
  64.8 12.7 %collective-permute-start.26 = (f32[32,1024]{1,0:T(8,128)S(1)}, f32[32,1024]{1,0:T(8,128)S(1)}, u32[]{:S(2)}, u32[]{:S(2)}) collective-permute-start(f32[32,1024]{1,0:T(8,128)S(1)} %get-tuple-element.47), channel_id=1, source_target_pairs={{0,1},{1,0},{2,3},{3,2},{4,5},{5,4},{6,7},{7,6},{8,9},{9,8},{10,11... | collective-permute-start | bytes 393224 | tf_op jit(solution)/shard_map/ppermute | solution.py:35
  64.9 14.7 %collective-permute-start.17 = (f32[32,1024]{1,0:T(8,128)S(1)}, f32[32,1024]{1,0:T(8,128)S(1)}, u32[]{:S(2)}, u32[]{:S(2)}) collective-permute-start(f32[32,1024]{1,0:T(8,128)S(1)} %add.94), channel_id=1, source_target_pairs={{0,2},{1,3},{2,0},{3,1},{4,6},{5,7},{6,4},{7,5},{8,10},{9,11},{10,... | collective-permute-start | bytes 393224 | tf_op jit(solution)/shard_map/ppermute | solution.py:35
  77.5 9.7 %collective-permute-start.25 = (f32[32,1024]{1,0:T(8,128)S(1)}, f32[32,1024]{1,0:T(8,128)S(1)}, u32[]{:S(2)}, u32[]{:S(2)}) collective-permute-start(f32[32,1024]{1,0:T(8,128)S(1)} %add_add_fusion.6), channel_id=1, source_target_pairs={{0,8},{1,9},{2,10},{3,11},{4,12},{5,13},{6,14},{7,15},{8,0},{9,1},... | collective-permute-start | bytes 393224 | tf_op jit(solution)/shard_map/ppermute | solution.py:35
  77.7 9.6 %collective-permute-start.29 = (f32[32,1024]{1,0:T(8,128)S(1)}, f32[32,1024]{1,0:T(8,128)S(1)}, u32[]{:S(2)}, u32[]{:S(2)}) collective-permute-start(f32[32,1024]{1,0:T(8,128)S(1)} %add_add_fusion.4), channel_id=1, source_target_pairs={{0,4},{1,5},{2,6},{3,7},{4,0},{5,1},{6,2},{7,3},{8,12},{9,13},{10,... | collective-permute-start | bytes 393224 | tf_op jit(solution)/shard_map/ppermute | solution.py:35
  90.4 10.0 %collective-permute-start.37 = (f32[32,1024]{1,0:T(8,128)S(1)}, f32[32,1024]{1,0:T(8,128)S(1)}, u32[]{:S(2)}, u32[]{:S(2)}) collective-permute-start(f32[32,1024]{1,0:T(8,128)S(1)} %get-tuple-element.68.refs_0_), channel_id=1, source_target_pairs={{0,8},{1,9},{2,10},{3,11},{4,12},{5,13},{6,14},{7,15},{8,0},{9,1},... | collective-permute-start | bytes 393224 | tf_op jit(solution)/shard_map/ppermute | solution.py:35
  90.4 10.0 %collective-permute-start.33 = (f32[32,1024]{1,0:T(8,128)S(1)}, f32[32,1024]{1,0:T(8,128)S(1)}, u32[]{:S(2)}, u32[]{:S(2)}) collective-permute-start(f32[32,1024]{1,0:T(8,128)S(1)} %get-tuple-element.68.refs_0_), channel_id=1, source_target_pairs={{0,4},{1,5},{2,6},{3,7},{4,0},{5,1},{6,2},{7,3},{8,12},{9,13},{10,... | collective-permute-start | bytes 393224 | tf_op jit(solution)/shard_map/ppermute | solution.py:35
  91.8 9.1 %collective-permute-start.31 = (f32[32,1024]{1,0:T(8,128)S(1)}, f32[32,1024]{1,0:T(8,128)S(1)}, u32[]{:S(2)}, u32[]{:S(2)}) collective-permute-start(f32[32,1024]{1,0:T(8,128)S(1)} %get-tuple-element.68.refs_0_), channel_id=1, source_target_pairs={{0,2},{1,3},{2,0},{3,1},{4,6},{5,7},{6,4},{7,5},{8,10},{9,11},{10,... | collective-permute-start | bytes 393224 | tf_op jit(solution)/shard_map/ppermute | solution.py:35
  131.2 16.7 %collective-permute-start.45 = (f32[32,1024]{1,0:T(8,128)S(1)}, f32[32,1024]{1,0:T(8,128)S(1)}, u32[]{:S(2)}, u32[]{:S(2)}) collective-permute-start(f32[32,1024]{1,0:T(8,128)S(1)} %get-tuple-element.51), channel_id=1, source_target_pairs={{0,1},{1,0},{2,3},{3,2},{4,5},{5,4},{6,7},{7,6},{8,9},{9,8},{10,11... | collective-permute-start | bytes 393224 | tf_op jit(solution)/shard_map/ppermute | solution.py:35
  131.8 13.0 %collective-permute-start.56 = (f32[32,1024]{1,0:T(8,128)S(1)}, f32[32,1024]{1,0:T(8,128)S(1)}, u32[]{:S(2)}, u32[]{:S(2)}) collective-permute-start(f32[32,1024]{1,0:T(8,128)S(1)} %get-tuple-element.63), channel_id=1, source_target_pairs={{0,1},{1,0},{2,3},{3,2},{4,5},{5,4},{6,7},{7,6},{8,9},{9,8},{10,11... | collective-permute-start | bytes 393224 | tf_op jit(solution)/shard_map/ppermute | solution.py:35
  132.0 16.0 %collective-permute-start.47 = (f32[32,1024]{1,0:T(8,128)S(1)}, f32[32,1024]{1,0:T(8,128)S(1)}, u32[]{:S(2)}, u32[]{:S(2)}) collective-permute-start(f32[32,1024]{1,0:T(8,128)S(1)} %add.109), channel_id=1, source_target_pairs={{0,2},{1,3},{2,0},{3,1},{4,6},{5,7},{6,4},{7,5},{8,10},{9,11},{10,... | collective-permute-start | bytes 393224 | tf_op jit(solution)/shard_map/ppermute | solution.py:35
  137.1 8.7 %collective-permute-start.58 = (f32[32,1024]{1,0:T(8,128)S(1)}, f32[32,1024]{1,0:T(8,128)S(1)}, u32[]{:S(2)}, u32[]{:S(2)}) collective-permute-start(f32[32,1024]{1,0:T(8,128)S(1)} %add.120), channel_id=1, source_target_pairs={{0,2},{1,3},{2,0},{3,1},{4,6},{5,7},{6,4},{7,5},{8,10},{9,11},{10,... | collective-permute-start | bytes 393224 | tf_op jit(solution)/shard_map/ppermute | solution.py:35
  144.9 9.7 %collective-permute-start.55 = (f32[32,1024]{1,0:T(8,128)S(1)}, f32[32,1024]{1,0:T(8,128)S(1)}, u32[]{:S(2)}, u32[]{:S(2)}) collective-permute-start(f32[32,1024]{1,0:T(8,128)S(1)} %add_add_fusion.2), channel_id=1, source_target_pairs={{0,8},{1,9},{2,10},{3,11},{4,12},{5,13},{6,14},{7,15},{8,0},{9,1},... | collective-permute-start | bytes 393224 | tf_op jit(solution)/shard_map/ppermute | solution.py:35
  (39 other events, 310.1 us)

commit v2 on v0

v2 whole, which is shorter than its diff:
```python
import functools

import jax
import jax.numpy as jnp
from jax import lax
from jax.experimental import pallas as pl
from jax.experimental.pallas import tpu as pltpu
from jax.sharding import PartitionSpec as P

ITERS = 2
MIB = 2**20
SCOPED = 24 * MIB
DEPTH = 3

step_size = 0.15
momentum = 0.6

IN_VMEM = pl.BlockSpec(memory_space=pltpu.VMEM)
IN_SMEM = pl.BlockSpec(memory_space=pltpu.SMEM)

CORE, HALF = 1, 2


def swap(x, mask):
    count = lax.axis_size("col")
    return lax.ppermute(x, "col", [(i, i ^ mask) for i in range(count)])


def far_bits(count):
    return [1 << i for i in range(2, count.bit_length() - 1)]


def far_pieces(count):
    return list(range(0, count, 4))


def gather(own):
    count = lax.axis_size("col")
    pieces = {0: own}
    for bit in reversed(far_bits(count)):
        for p in list(pieces):
            pieces[p | bit] = swap(pieces[p], bit)
    for p in sorted(pieces, key=lambda p: p.bit_count()):
        pieces[p | HALF] = swap(pieces[p], HALF)
    order = sorted(pieces, key=lambda p: p.bit_count())
    arrays = [([p], pieces[p][None]) for p in order]
    for start in range(0, len(order), 4):
        some = order[start : start + 4]
        arrays.append(([p | CORE for p in some], swap(jnp.stack([pieces[p] for p in some]), CORE)))
    return arrays


def scatter_sum(kept_half, sent_half, kept_own, sent_own):
    count = lax.axis_size("col")
    far = far_pieces(count)
    half = kept_half + swap(sent_half, CORE)
    crossed = {p: swap(half[j], HALF) for j, p in reversed(list(enumerate(far)))}
    own = kept_own + swap(sent_own, CORE)
    held = {p: own[j] + crossed[p] for j, p in enumerate(far)}
    for bit in far_bits(count):
        for p in sorted((p for p in held if p & bit), reverse=True):
            held[p ^ bit] += swap(held.pop(p), bit)
    return held[0]


def places(owner, order, width):
    if width >= order:
        each = width // order
        return [(slice(j * order, (j + 1) * order), owner * each + j, slice(None)) for j in range(each)]
    each = order // width
    start = pl.multiple_of(lax.rem(owner, each) * width, width)
    return [(slice(None), lax.div(owner, each), pl.ds(start, width))]


def take_pieces(held, pieces, err, order):
    me = lax.axis_index("col")
    _, rows, width = pieces[0].shape
    for places_held, ref in zip(held, pieces, strict=True):
        for i, p in enumerate(places_held):
            for part, block, columns in places(me ^ p, order, width):
                piece = ref[i, :, part]
                high = piece.astype(jnp.bfloat16)
                err[block, :rows, columns] = high
                err[block, rows:, columns] = (piece - high.astype(jnp.float32)).astype(jnp.bfloat16)


def give_sums(acc, outs, count, width, order):
    me = lax.axis_index("col")
    for out, offset in zip(outs, (HALF, HALF | CORE, 0, CORE), strict=True):
        for j, p in enumerate(far_pieces(count)):
            for part, block, columns in places(me ^ (p | offset), order, width):
                out[j, :, part] = acc[block, :, columns]


def add_products(row_block, col_block, high, low, err, acc):
    rows = acc.shape[1]
    for source, target, dim in ((row_block, col_block, 0), (col_block, row_block, 1)):
        dims = (((1,), (dim,)), ((), ()))
        both = err[source]
        lead = lax.dot_general(both, high, dims, preferred_element_type=jnp.float32)
        rest = lax.dot_general(both[:rows], low, dims, preferred_element_type=jnp.float32)
        term = lead[:rows] + (lead[rows:] + rest)
        if dim:
            term = jnp.where(row_block != col_block, term, 0.0)
        acc[target] += term


def product_kernel(held, width, together, plan, tiles, *refs):
    pieces = refs[: len(held)]
    *outs, err, acc, ring, arrived = refs[len(held) :]
    slots, order, _ = tiles.shape
    count = acc.shape[0] * order // width
    steps = slots // together
    depth = ring.shape[0]

    def fetch(step):
        at = lax.rem(step, depth)
        return pltpu.make_async_copy(tiles.at[pl.ds(step * together, together)], ring.at[at], arrived.at[at])

    for step in range(min(depth, steps)):
        fetch(step).start()
    take_pieces(held, pieces, err, order)
    acc[...] = jnp.zeros(acc.shape, jnp.float32)

    def one_step(step, carry):
        fetch(step).wait()
        for j in range(together):
            slot = step * together + j
            tile = ring[lax.rem(step, depth), j]
            high = tile.astype(jnp.bfloat16)
            low = (tile - high.astype(jnp.float32)).astype(jnp.bfloat16)
            add_products(plan[slot, 0], plan[slot, 1], high, low, err, acc)

        @pl.when(step + depth < steps)
        def _():
            fetch(step + depth).start()

        return carry

    lax.fori_loop(0, steps, one_step, 0)
    give_sums(acc, outs, count, width, order)


def product(plan, tiles, arrays):
    slots, order, _ = tiles.shape
    held = [p for p, _ in arrays]
    count = sum(len(p) for p in held)
    _, rows, width = arrays[0][1].shape
    blocks = count * width // order
    together = 3 if slots % 3 == 0 else 1
    some = jax.ShapeDtypeStruct((count // 4, rows, width), jnp.float32)
    return pl.pallas_call(
        functools.partial(product_kernel, held, width, together),
        in_specs=[IN_SMEM, pl.BlockSpec(memory_space=pl.ANY)] + [IN_VMEM] * len(held),
        out_specs=[IN_VMEM] * 4,
        out_shape=[some] * 4,
        scratch_shapes=[
            pltpu.VMEM((blocks, 2 * rows, order), jnp.bfloat16),
            pltpu.VMEM((blocks, rows, order), jnp.float32),
            pltpu.VMEM((DEPTH, together, order, order), jnp.float32),
            pltpu.SemaphoreType.DMA((DEPTH,)),
        ],
        compiler_params=pltpu.CompilerParams(vmem_limit_bytes=SCOPED),
        cost_estimate=pl.CostEstimate(
            flops=slots * 12 * rows * order * order, bytes_accessed=slots * order * order * 4, transcendentals=0
        ),
        name="product",
    )(plan, tiles, *[x for _, x in arrays])


def body(dense_weight, start_weight, keep_mask, tile_plan, hess_tiles):
    keep = keep_mask.astype(jnp.float32)
    weights = start_weight
    velocity = jnp.zeros(start_weight.shape, jnp.float32)
    for step in range(ITERS):
        terms = product(tile_plan, hess_tiles, gather(weights - dense_weight))
        gradient = scatter_sum(*terms)
        velocity = momentum * velocity + gradient
        weights = keep * (weights - step_size * velocity)
    return (weights, velocity)


def solution(mesh):
    placed = (
        P("layers", "col"),
        P("layers", "col"),
        P("layers", "col"),
        P(("layers", "col"), None),
        P(("layers", "col"), None, None),
    )
    return jax.shard_map(
        body,
        mesh=mesh,
        in_specs=placed,
        out_specs=(P("layers", "col"), P("layers", "col")),
        check_vma=False,
    )
```

time: 855 us -> 144 us (0.17); the launches traced: 842 us -> 143 us
  loops' own time: 248 us -> 0 us
  matrix products: 216 us -> 0 us
  waiting for transfers between devices: 231 us -> 51.3 us
  local copies, waits for them, and re-layouts: 128 us -> 0.87 us
  starting transfers between devices: 0.16 us -> 45.6 us
  Pallas kernels: 0 us -> 41.8 us
  between operations: 13.9 us -> 0.83 us
    another operation x134 -> x0, loops' own time: 248 us -> none  [the longest x2 168 us: tile_terms(): return lax.fori_loop(0, tile_plan.shape[0], one_slot, carry)]
    dot_general x122 -> x0, matrix products: 216 us -> none  [apply_term(): lax.dot_general(block, tile, (((1,), (tile_dim,)), ((), ())), precision=l...]
    reduce_scatter x2 -> x0, waiting for transfers between devices: 143 us -> none  [body(): lax.psum_scatter(partial_grad, 'col', scatter_dimension=1, tiled=True)]
    all_gather x2 -> x0, waiting for transfers between devices: 87.8 us -> none  [body(): whole = lax.all_gather(error, 'col', axis=1, tiled=True)]
    squeeze x66 -> x2, local copies, waits for them, and re-layouts: 85.8 us -> 0.09 us  [scatter_sum(): half[j]]
    ppermute x0 -> x36, waiting for transfers between devices: none -> 51.3 us  [swap(): return lax.ppermute(x, 'col', [(i, i ^ mask) for i in range(count)])]
    ppermute x0 -> x36, starting transfers between devices: none -> 45.6 us  [swap(): return lax.ppermute(x, 'col', [(i, i ^ mask) for i in range(count)])]
    pallas_call x0 -> x2, Pallas kernels: none -> 41.8 us  [product(): pl.pallas_call(functools.partial(product_kernel, held, width, together),...]
  transfers between devices with their start and end apart: 4 -> 36, of which waited for: 4 -> 21; matrix products, arithmetic and copies ran while one was open for 0% -> 1% of each run, Pallas kernels for 0% -> 0%
where the time goes in v2:
time: 144 us; the launch traced here: 143 us
  waiting for transfers between devices  51.3 us (36%)
  starting transfers between devices  45.6 us (32%)
  Pallas kernels  41.8 us (29%)
  other arithmetic  3.13 us (2%)
    ppermute x36, waiting for transfers between devices, swap(): return lax.ppermute(x, 'col', [(i, i ^ mask) for i in range(count)])  51.3 us
    ppermute x36, starting transfers between devices, swap(): return lax.ppermute(x, 'col', [(i, i ^ mask) for i in range(count)])  45.6 us
    pallas_call x2, Pallas kernels, product(): pl.pallas_call(functools.partial(product_kernel, held, width, together),...  41.8 us
  transfers between devices with their start and end apart: 36, of which 21 were waited for; matrix products, arithmetic and copies ran while one was open for 1% of the time, Pallas kernels for 0%

profile of v2, /device:TPU:0, one launch (start us, length us, event | category | flops | bytes accessed | tf_op | source)
XLA Modules:
  0.0 143.5 jit_solution(12674094773728317729)
XLA Ops:
  1.7 4.1 %collective-permute-start = (f32[32,1024]{1,0:T(8,128)S(1)}, f32[32,1024]{1,0:T(8,128)S(1)}, u32[]{:S(2)}, u32[]{:S(2)}) collective-permute-start(f32[32,1024]{1,0:T(8,128)S(1)} %sub.12), channel_id=1, source_target_pairs={{0,8},{1,9},{2,10},{3,11},{4,12},{5,13},{6,14},{7,15},{8,0},{9,1},... | collective-permute-start | bytes 393224 | tf_op jit(solution)/shard_map/ppermute | solution.py:26
  5.8 1.6 %collective-permute-start.1 = (f32[32,1024]{1,0:T(8,128)S(1)}, f32[32,1024]{1,0:T(8,128)S(1)}, u32[]{:S(2)}, u32[]{:S(2)}) collective-permute-start(f32[32,1024]{1,0:T(8,128)S(1)} %sub.12), channel_id=1, source_target_pairs={{0,4},{1,5},{2,6},{3,7},{4,0},{5,1},{6,2},{7,3},{8,12},{9,13},{10,... | collective-permute-start | bytes 393224 | tf_op jit(solution)/shard_map/ppermute | solution.py:26
  7.4 4.8 %collective-permute-done = f32[32,1024]{1,0:T(8,128)S(1)} collective-permute-done((f32[32,1024]{1,0:T(8,128)S(1)}, f32[32,1024]{1,0:T(8,128)S(1)}, u32[]{:S(2)}, u32[]{:S(2)}) %collective-permute-start) | collective-permute-done | bytes 131104 | tf_op jit(solution)/shard_map/ppermute | solution.py:26
  19.3 5.5 %collective-permute-done.5 = f32[32,1024]{1,0:T(8,128)S(1)} collective-permute-done((f32[32,1024]{1,0:T(8,128)S(1)}, f32[32,1024]{1,0:T(8,128)S(1)}, u32[]{:S(2)}, u32[]{:S(2)}) %collective-permute-start.5) | collective-permute-done | bytes 131104 | tf_op jit(solution)/shard_map/ppermute | solution.py:26
  29.3 20.9 %product.2 = (f32[4,32,1024]{2,1,0:T(8,128)S(1)}, f32[4,32,1024]{2,1,0:T(8,128)S(1)}, f32[4,32,1024]{2,1,0:T(8,128)S(1)}, f32[4,32,1024]{2,1,0:T(8,128)S(1)}) custom-call(s32[33,2]{1,0:T(8,128)S(1)} %copy.7.plan, f32[33,512,512]{2,1,0:T(8,128)} %tiles.3, f32[1,32,1024]{2,1,0:T(8,128)S(1)} %bitcast.83, f32[1,32,1024]{2,1,0:T(8,128)S(1)} %bitcast.85, ...), custom_call_target="tpu_custom_call" | custom-call | flops 3321888768 | bytes 34603008 | tf_op jit(solution)/shard_map/product/pallas_call | solution.py:152
  52.3 1.6 %collective-permute-start.15 = (f32[32,1024]{1,0:T(8,128)S(1)}, f32[32,1024]{1,0:T(8,128)S(1)}, u32[]{:S(2)}, u32[]{:S(2)}) collective-permute-start(f32[32,1024]{1,0:T(8,128)S(1)} %get-tuple-element.29), channel_id=1, source_target_pairs={{0,2},{1,3},{2,0},{3,1},{4,6},{5,7},{6,4},{7,5},{8,10},{9,11},{10,... | collective-permute-start | bytes 393224 | tf_op jit(solution)/shard_map/ppermute | solution.py:26
  56.0 2.7 %collective-permute-done.15 = f32[32,1024]{1,0:T(8,128)S(1)} collective-permute-done((f32[32,1024]{1,0:T(8,128)S(1)}, f32[32,1024]{1,0:T(8,128)S(1)}, u32[]{:S(2)}, u32[]{:S(2)}) %collective-permute-start.15) | collective-permute-done | bytes 131104 | tf_op jit(solution)/shard_map/ppermute | solution.py:26
  58.8 2.8 %collective-permute-done.12 = f32[32,1024]{1,0:T(8,128)S(1)} collective-permute-done((f32[32,1024]{1,0:T(8,128)S(1)}, f32[32,1024]{1,0:T(8,128)S(1)}, u32[]{:S(2)}, u32[]{:S(2)}) %collective-permute-start.12) | collective-permute-done | bytes 131104 | tf_op jit(solution)/shard_map/ppermute | solution.py:26
  63.5 1.8 %collective-permute-start.13 = (f32[32,1024]{1,0:T(8,128)S(1)}, f32[32,1024]{1,0:T(8,128)S(1)}, u32[]{:S(2)}, u32[]{:S(2)}) collective-permute-start(f32[32,1024]{1,0:T(8,128)S(1)} %get-tuple-element.32), channel_id=1, source_target_pairs={{0,4},{1,5},{2,6},{3,7},{4,0},{5,1},{6,2},{7,3},{8,12},{9,13},{10,... | collective-permute-start | bytes 393224 | tf_op jit(solution)/shard_map/ppermute | solution.py:26
  65.2 1.7 %collective-permute-done.16 = f32[32,1024]{1,0:T(8,128)S(1)} collective-permute-done((f32[32,1024]{1,0:T(8,128)S(1)}, f32[32,1024]{1,0:T(8,128)S(1)}, u32[]{:S(2)}, u32[]{:S(2)}) %collective-permute-start.16) | collective-permute-done | bytes 131104 | tf_op jit(solution)/shard_map/ppermute | solution.py:26
  67.0 4.6 %collective-permute-start.17 = (f32[32,1024]{1,0:T(8,128)S(1)}, f32[32,1024]{1,0:T(8,128)S(1)}, u32[]{:S(2)}, u32[]{:S(2)}) collective-permute-start(f32[32,1024]{1,0:T(8,128)S(1)} %fusion.10), channel_id=1, source_target_pairs={{0,8},{1,9},{2,10},{3,11},{4,12},{5,13},{6,14},{7,15},{8,0},{9,1},... | collective-permute-start | bytes 393224 | tf_op jit(solution)/shard_map/ppermute | solution.py:26
  71.6 6.1 %collective-permute-done.17 = f32[32,1024]{1,0:T(8,128)S(1)} collective-permute-done((f32[32,1024]{1,0:T(8,128)S(1)}, f32[32,1024]{1,0:T(8,128)S(1)}, u32[]{:S(2)}, u32[]{:S(2)}) %collective-permute-start.17) | collective-permute-done | bytes 131104 | tf_op jit(solution)/shard_map/ppermute | solution.py:26
  79.0 3.8 %collective-permute-start.19 = (f32[32,1024]{1,0:T(8,128)S(1)}, f32[32,1024]{1,0:T(8,128)S(1)}, u32[]{:S(2)}, u32[]{:S(2)}) collective-permute-start(f32[32,1024]{1,0:T(8,128)S(1)} %get-tuple-element.20), channel_id=1, source_target_pairs={{0,4},{1,5},{2,6},{3,7},{4,0},{5,1},{6,2},{7,3},{8,12},{9,13},{10,... | collective-permute-start | bytes 393224 | tf_op jit(solution)/shard_map/ppermute | solution.py:26
  83.8 2.4 %collective-permute-start.21 = (f32[32,1024]{1,0:T(8,128)S(1)}, f32[32,1024]{1,0:T(8,128)S(1)}, u32[]{:S(2)}, u32[]{:S(2)}) collective-permute-start(f32[32,1024]{1,0:T(8,128)S(1)} %collective-permute-done.18), channel_id=1, source_target_pairs={{0,4},{1,5},{2,6},{3,7},{4,0},{5,1},{6,2},{7,3},{8,12},{9,13},{10,... | collective-permute-start | bytes 393224 | tf_op jit(solution)/shard_map/ppermute | solution.py:26
  86.3 1.9 %collective-permute-start.22 = (f32[32,1024]{1,0:T(8,128)S(1)}, f32[32,1024]{1,0:T(8,128)S(1)}, u32[]{:S(2)}, u32[]{:S(2)}) collective-permute-start(f32[32,1024]{1,0:T(8,128)S(1)} %collective-permute-done.18), channel_id=1, source_target_pairs={{0,2},{1,3},{2,0},{3,1},{4,6},{5,7},{6,4},{7,5},{8,10},{9,11},{10,... | collective-permute-start | bytes 393224 | tf_op jit(solution)/shard_map/ppermute | solution.py:26
  89.1 2.0 %collective-permute-start.24 = (f32[32,1024]{1,0:T(8,128)S(1)}, f32[32,1024]{1,0:T(8,128)S(1)}, u32[]{:S(2)}, u32[]{:S(2)}) collective-permute-start(f32[32,1024]{1,0:T(8,128)S(1)} %collective-permute-done.21), channel_id=1, source_target_pairs={{0,2},{1,3},{2,0},{3,1},{4,6},{5,7},{6,4},{7,5},{8,10},{9,11},{10,... | collective-permute-start | bytes 393224 | tf_op jit(solution)/shard_map/ppermute | solution.py:26
  91.3 2.7 %collective-permute-done.23 = f32[32,1024]{1,0:T(8,128)S(1)} collective-permute-done((f32[32,1024]{1,0:T(8,128)S(1)}, f32[32,1024]{1,0:T(8,128)S(1)}, u32[]{:S(2)}, u32[]{:S(2)}) %collective-permute-start.23) | collective-permute-done | bytes 131104 | tf_op jit(solution)/shard_map/ppermute | solution.py:26
  95.5 1.9 %collective-permute-done.26.refs_9_ = f32[4,32,1024]{2,1,0:T(8,128)S(1)} collective-permute-done((f32[4,32,1024]{2,1,0:T(8,128)S(1)}, f32[4,32,1024]{2,1,0:T(8,128)S(1)}, u32[]{:S(2)}, u32[]{:S(2)}) %collective-permute-start.26) | collective-permute-done | bytes 524320 | tf_op jit(solution)/shard_map/ppermute | solution.py:26
  97.4 20.9 %product.3 = (f32[4,32,1024]{2,1,0:T(8,128)S(1)}, f32[4,32,1024]{2,1,0:T(8,128)S(1)}, f32[4,32,1024]{2,1,0:T(8,128)S(1)}, f32[4,32,1024]{2,1,0:T(8,128)S(1)}) custom-call(s32[33,2]{1,0:T(8,128)S(1)} %copy.7.plan, f32[33,512,512]{2,1,0:T(8,128)} %tiles.3, f32[1,32,1024]{2,1,0:T(8,128)S(1)} %bitcast.81, f32[1,32,1024]{2,1,0:T(8,128)S(1)} %bitcast.87, ...), custom_call_target="tpu_custom_call" | custom-call | flops 3321888768 | bytes 34603008 | tf_op jit(solution)/shard_map/product/pallas_call | solution.py:152
  123.3 3.5 %collective-permute-done.33 = f32[32,1024]{1,0:T(8,128)S(1)} collective-permute-done((f32[32,1024]{1,0:T(8,128)S(1)}, f32[32,1024]{1,0:T(8,128)S(1)}, u32[]{:S(2)}, u32[]{:S(2)}) %collective-permute-start.33) | collective-permute-done | bytes 131104 | tf_op jit(solution)/shard_map/ppermute | solution.py:26
  126.8 2.8 %collective-permute-done.30 = f32[32,1024]{1,0:T(8,128)S(1)} collective-permute-done((f32[32,1024]{1,0:T(8,128)S(1)}, f32[32,1024]{1,0:T(8,128)S(1)}, u32[]{:S(2)}, u32[]{:S(2)}) %collective-permute-start.30) | collective-permute-done | bytes 131104 | tf_op jit(solution)/shard_map/ppermute | solution.py:26
  132.5 2.6 %collective-permute-done.34 = f32[32,1024]{1,0:T(8,128)S(1)} collective-permute-done((f32[32,1024]{1,0:T(8,128)S(1)}, f32[32,1024]{1,0:T(8,128)S(1)}, u32[]{:S(2)}, u32[]{:S(2)}) %collective-permute-start.34) | collective-permute-done | bytes 131104 | tf_op jit(solution)/shard_map/ppermute | solution.py:26
  135.1 3.7 %collective-permute-start.35 = (f32[32,1024]{1,0:T(8,128)S(1)}, f32[32,1024]{1,0:T(8,128)S(1)}, u32[]{:S(2)}, u32[]{:S(2)}) collective-permute-start(f32[32,1024]{1,0:T(8,128)S(1)} %fusion.2), channel_id=1, source_target_pairs={{0,8},{1,9},{2,10},{3,11},{4,12},{5,13},{6,14},{7,15},{8,0},{9,1},... | collective-permute-start | bytes 393224 | tf_op jit(solution)/shard_map/ppermute | solution.py:26
  138.9 3.8 %collective-permute-done.35 = f32[32,1024]{1,0:T(8,128)S(1)} collective-permute-done((f32[32,1024]{1,0:T(8,128)S(1)}, f32[32,1024]{1,0:T(8,128)S(1)}, u32[]{:S(2)}, u32[]{:S(2)}) %collective-permute-start.35) | collective-permute-done | bytes 131104 | tf_op jit(solution)/shard_map/ppermute | solution.py:26
  (74 shorter events, 32.3 us)
Async XLA Ops:
  1.7 10.5 %collective-permute-start = (f32[32,1024]{1,0:T(8,128)S(1)}, f32[32,1024]{1,0:T(8,128)S(1)}, u32[]{:S(2)}, u32[]{:S(2)}) collective-permute-start(f32[32,1024]{1,0:T(8,128)S(1)} %sub.12), channel_id=1, source_target_pairs={{0,8},{1,9},{2,10},{3,11},{4,12},{5,13},{6,14},{7,15},{8,0},{9,1},... | collective-permute-start | bytes 393224 | tf_op jit(solution)/shard_map/ppermute | solution.py:26
  5.8 9.1 %collective-permute-start.1 = (f32[32,1024]{1,0:T(8,128)S(1)}, f32[32,1024]{1,0:T(8,128)S(1)}, u32[]{:S(2)}, u32[]{:S(2)}) collective-permute-start(f32[32,1024]{1,0:T(8,128)S(1)} %sub.12), channel_id=1, source_target_pairs={{0,4},{1,5},{2,6},{3,7},{4,0},{5,1},{6,2},{7,3},{8,12},{9,13},{10,... | collective-permute-start | bytes 393224 | tf_op jit(solution)/shard_map/ppermute | solution.py:26
  12.8 6.4 %collective-permute-start.2 = (f32[32,1024]{1,0:T(8,128)S(1)}, f32[32,1024]{1,0:T(8,128)S(1)}, u32[]{:S(2)}, u32[]{:S(2)}) collective-permute-start(f32[32,1024]{1,0:T(8,128)S(1)} %sub.12), channel_id=1, source_target_pairs={{0,2},{1,3},{2,0},{3,1},{4,6},{5,7},{6,4},{7,5},{8,10},{9,11},{10,... | collective-permute-start | bytes 393224 | tf_op jit(solution)/shard_map/ppermute | solution.py:26
  14.3 10.5 %collective-permute-start.4 = (f32[32,1024]{1,0:T(8,128)S(1)}, f32[32,1024]{1,0:T(8,128)S(1)}, u32[]{:S(2)}, u32[]{:S(2)}) collective-permute-start(f32[32,1024]{1,0:T(8,128)S(1)} %collective-permute-done), channel_id=1, source_target_pairs={{0,2},{1,3},{2,0},{3,1},{4,6},{5,7},{6,4},{7,5},{8,10},{9,11},{10,... | collective-permute-start | bytes 393224 | tf_op jit(solution)/shard_map/ppermute | solution.py:26
  14.9 10.0 %collective-permute-start.5 = (f32[32,1024]{1,0:T(8,128)S(1)}, f32[32,1024]{1,0:T(8,128)S(1)}, u32[]{:S(2)}, u32[]{:S(2)}) collective-permute-start(f32[32,1024]{1,0:T(8,128)S(1)} %collective-permute-done.1), channel_id=1, source_target_pairs={{0,2},{1,3},{2,0},{3,1},{4,6},{5,7},{6,4},{7,5},{8,10},{9,11},{10,... | collective-permute-start | bytes 393224 | tf_op jit(solution)/shard_map/ppermute | solution.py:26
  17.2 9.2 %collective-permute-start.6 = (f32[32,1024]{1,0:T(8,128)S(1)}, f32[32,1024]{1,0:T(8,128)S(1)}, u32[]{:S(2)}, u32[]{:S(2)}) collective-permute-start(f32[32,1024]{1,0:T(8,128)S(1)} %collective-permute-done.3), channel_id=1, source_target_pairs={{0,2},{1,3},{2,0},{3,1},{4,6},{5,7},{6,4},{7,5},{8,10},{9,11},{10,... | collective-permute-start | bytes 393224 | tf_op jit(solution)/shard_map/ppermute | solution.py:26
  19.3 8.7 %collective-permute-start.7 = (f32[4,32,1024]{2,1,0:T(8,128)S(1)}, f32[4,32,1024]{2,1,0:T(8,128)S(1)}, u32[]{:S(2)}, u32[]{:S(2)}) collective-permute-start(f32[4,32,1024]{2,1,0:T(8,128)S(1)} %pad_maximum_fusion), channel_id=1, source_target_pairs={{0,1},{1,0},{2,3},{3,2},{4,5},{5,4},{6,7},{7,6},{8,9},{9,8},{10,11... | collective-permute-start | bytes 1572872 | tf_op jit(solution)/shard_map/ppermute | solution.py:26
  52.3 6.4 %collective-permute-start.15 = (f32[32,1024]{1,0:T(8,128)S(1)}, f32[32,1024]{1,0:T(8,128)S(1)}, u32[]{:S(2)}, u32[]{:S(2)}) collective-permute-start(f32[32,1024]{1,0:T(8,128)S(1)} %get-tuple-element.29), channel_id=1, source_target_pairs={{0,2},{1,3},{2,0},{3,1},{4,6},{5,7},{6,4},{7,5},{8,10},{9,11},{10,... | collective-permute-start | bytes 393224 | tf_op jit(solution)/shard_map/ppermute | solution.py:26
  53.9 7.6 %collective-permute-start.12 = (f32[32,1024]{1,0:T(8,128)S(1)}, f32[32,1024]{1,0:T(8,128)S(1)}, u32[]{:S(2)}, u32[]{:S(2)}) collective-permute-start(f32[32,1024]{1,0:T(8,128)S(1)} %get-tuple-element.31), channel_id=1, source_target_pairs={{0,2},{1,3},{2,0},{3,1},{4,6},{5,7},{6,4},{7,5},{8,10},{9,11},{10,... | collective-permute-start | bytes 393224 | tf_op jit(solution)/shard_map/ppermute | solution.py:26
  54.4 10.8 %collective-permute-start.14 = (f32[32,1024]{1,0:T(8,128)S(1)}, f32[32,1024]{1,0:T(8,128)S(1)}, u32[]{:S(2)}, u32[]{:S(2)}) collective-permute-start(f32[32,1024]{1,0:T(8,128)S(1)} %get-tuple-element.30), channel_id=1, source_target_pairs={{0,2},{1,3},{2,0},{3,1},{4,6},{5,7},{6,4},{7,5},{8,10},{9,11},{10,... | collective-permute-start | bytes 393224 | tf_op jit(solution)/shard_map/ppermute | solution.py:26
  62.0 9.6 %collective-permute-start.11 = (f32[32,1024]{1,0:T(8,128)S(1)}, f32[32,1024]{1,0:T(8,128)S(1)}, u32[]{:S(2)}, u32[]{:S(2)}) collective-permute-start(f32[32,1024]{1,0:T(8,128)S(1)} %get-tuple-element.28), channel_id=1, source_target_pairs={{0,2},{1,3},{2,0},{3,1},{4,6},{5,7},{6,4},{7,5},{8,10},{9,11},{10,... | collective-permute-start | bytes 393224 | tf_op jit(solution)/shard_map/ppermute | solution.py:26
  63.5 8.1 %collective-permute-start.13 = (f32[32,1024]{1,0:T(8,128)S(1)}, f32[32,1024]{1,0:T(8,128)S(1)}, u32[]{:S(2)}, u32[]{:S(2)}) collective-permute-start(f32[32,1024]{1,0:T(8,128)S(1)} %get-tuple-element.32), channel_id=1, source_target_pairs={{0,4},{1,5},{2,6},{3,7},{4,0},{5,1},{6,2},{7,3},{8,12},{9,13},{10,... | collective-permute-start | bytes 393224 | tf_op jit(solution)/shard_map/ppermute | solution.py:26
  67.0 10.7 %collective-permute-start.17 = (f32[32,1024]{1,0:T(8,128)S(1)}, f32[32,1024]{1,0:T(8,128)S(1)}, u32[]{:S(2)}, u32[]{:S(2)}) collective-permute-start(f32[32,1024]{1,0:T(8,128)S(1)} %fusion.10), channel_id=1, source_target_pairs={{0,8},{1,9},{2,10},{3,11},{4,12},{5,13},{6,14},{7,15},{8,0},{9,1},... | collective-permute-start | bytes 393224 | tf_op jit(solution)/shard_map/ppermute | solution.py:26
  77.8 6.0 %collective-permute-start.18 = (f32[32,1024]{1,0:T(8,128)S(1)}, f32[32,1024]{1,0:T(8,128)S(1)}, u32[]{:S(2)}, u32[]{:S(2)}) collective-permute-start(f32[32,1024]{1,0:T(8,128)S(1)} %get-tuple-element.20), channel_id=1, source_target_pairs={{0,8},{1,9},{2,10},{3,11},{4,12},{5,13},{6,14},{7,15},{8,0},{9,1},... | collective-permute-start | bytes 393224 | tf_op jit(solution)/shard_map/ppermute | solution.py:26
  79.0 9.2 %collective-permute-start.19 = (f32[32,1024]{1,0:T(8,128)S(1)}, f32[32,1024]{1,0:T(8,128)S(1)}, u32[]{:S(2)}, u32[]{:S(2)}) collective-permute-start(f32[32,1024]{1,0:T(8,128)S(1)} %get-tuple-element.20), channel_id=1, source_target_pairs={{0,4},{1,5},{2,6},{3,7},{4,0},{5,1},{6,2},{7,3},{8,12},{9,13},{10,... | collective-permute-start | bytes 393224 | tf_op jit(solution)/shard_map/ppermute | solution.py:26
  86.3 7.7 %collective-permute-start.22 = (f32[32,1024]{1,0:T(8,128)S(1)}, f32[32,1024]{1,0:T(8,128)S(1)}, u32[]{:S(2)}, u32[]{:S(2)}) collective-permute-start(f32[32,1024]{1,0:T(8,128)S(1)} %collective-permute-done.18), channel_id=1, source_target_pairs={{0,2},{1,3},{2,0},{3,1},{4,6},{5,7},{6,4},{7,5},{8,10},{9,11},{10,... | collective-permute-start | bytes 393224 | tf_op jit(solution)/shard_map/ppermute | solution.py:26
  88.2 5.7 %collective-permute-start.23 = (f32[32,1024]{1,0:T(8,128)S(1)}, f32[32,1024]{1,0:T(8,128)S(1)}, u32[]{:S(2)}, u32[]{:S(2)}) collective-permute-start(f32[32,1024]{1,0:T(8,128)S(1)} %collective-permute-done.19), channel_id=1, source_target_pairs={{0,2},{1,3},{2,0},{3,1},{4,6},{5,7},{6,4},{7,5},{8,10},{9,11},{10,... | collective-permute-start | bytes 393224 | tf_op jit(solution)/shard_map/ppermute | solution.py:26
  89.1 6.2 %collective-permute-start.24 = (f32[32,1024]{1,0:T(8,128)S(1)}, f32[32,1024]{1,0:T(8,128)S(1)}, u32[]{:S(2)}, u32[]{:S(2)}) collective-permute-start(f32[32,1024]{1,0:T(8,128)S(1)} %collective-permute-done.21), channel_id=1, source_target_pairs={{0,2},{1,3},{2,0},{3,1},{4,6},{5,7},{6,4},{7,5},{8,10},{9,11},{10,... | collective-permute-start | bytes 393224 | tf_op jit(solution)/shard_map/ppermute | solution.py:26
  120.4 6.4 %collective-permute-start.33 = (f32[32,1024]{1,0:T(8,128)S(1)}, f32[32,1024]{1,0:T(8,128)S(1)}, u32[]{:S(2)}, u32[]{:S(2)}) collective-permute-start(f32[32,1024]{1,0:T(8,128)S(1)} %get-tuple-element.23), channel_id=1, source_target_pairs={{0,2},{1,3},{2,0},{3,1},{4,6},{5,7},{6,4},{7,5},{8,10},{9,11},{10,... | collective-permute-start | bytes 393224 | tf_op jit(solution)/shard_map/ppermute | solution.py:26
  121.2 8.4 %collective-permute-start.30 = (f32[32,1024]{1,0:T(8,128)S(1)}, f32[32,1024]{1,0:T(8,128)S(1)}, u32[]{:S(2)}, u32[]{:S(2)}) collective-permute-start(f32[32,1024]{1,0:T(8,128)S(1)} %get-tuple-element.25), channel_id=1, source_target_pairs={{0,2},{1,3},{2,0},{3,1},{4,6},{5,7},{6,4},{7,5},{8,10},{9,11},{10,... | collective-permute-start | bytes 393224 | tf_op jit(solution)/shard_map/ppermute | solution.py:26
  122.5 10.0 %collective-permute-start.32 = (f32[32,1024]{1,0:T(8,128)S(1)}, f32[32,1024]{1,0:T(8,128)S(1)}, u32[]{:S(2)}, u32[]{:S(2)}) collective-permute-start(f32[32,1024]{1,0:T(8,128)S(1)} %get-tuple-element.24), channel_id=1, source_target_pairs={{0,2},{1,3},{2,0},{3,1},{4,6},{5,7},{6,4},{7,5},{8,10},{9,11},{10,... | collective-permute-start | bytes 393224 | tf_op jit(solution)/shard_map/ppermute | solution.py:26
  130.5 8.4 %collective-permute-start.29 = (f32[32,1024]{1,0:T(8,128)S(1)}, f32[32,1024]{1,0:T(8,128)S(1)}, u32[]{:S(2)}, u32[]{:S(2)}) collective-permute-start(f32[32,1024]{1,0:T(8,128)S(1)} %get-tuple-element.22), channel_id=1, source_target_pairs={{0,2},{1,3},{2,0},{3,1},{4,6},{5,7},{6,4},{7,5},{8,10},{9,11},{10,... | collective-permute-start | bytes 393224 | tf_op jit(solution)/shard_map/ppermute | solution.py:26
  131.7 7.1 %collective-permute-start.31 = (f32[32,1024]{1,0:T(8,128)S(1)}, f32[32,1024]{1,0:T(8,128)S(1)}, u32[]{:S(2)}, u32[]{:S(2)}) collective-permute-start(f32[32,1024]{1,0:T(8,128)S(1)} %get-tuple-element.26), channel_id=1, source_target_pairs={{0,4},{1,5},{2,6},{3,7},{4,0},{5,1},{6,2},{7,3},{8,12},{9,13},{10,... | collective-permute-start | bytes 393224 | tf_op jit(solution)/shard_map/ppermute | solution.py:26
  135.1 7.6 %collective-permute-start.35 = (f32[32,1024]{1,0:T(8,128)S(1)}, f32[32,1024]{1,0:T(8,128)S(1)}, u32[]{:S(2)}, u32[]{:S(2)}) collective-permute-start(f32[32,1024]{1,0:T(8,128)S(1)} %fusion.2), channel_id=1, source_target_pairs={{0,8},{1,9},{2,10},{3,11},{4,12},{5,13},{6,14},{7,15},{8,0},{9,1},... | collective-permute-start | bytes 393224 | tf_op jit(solution)/shard_map/ppermute | solution.py:26
  (15 other events, 279.9 us)

commit v3 on v2

--- a/solution.py
+++ b/solution.py
@@ -18,20 +18,28 @@
 IN_VMEM = pl.BlockSpec(memory_space=pltpu.VMEM)
 IN_SMEM = pl.BlockSpec(memory_space=pltpu.SMEM)
 
-CORE, HALF = 1, 2
+CORE = 1
+NEAR = (2, 4)
+
+
+def near_masks(count):
+    masks = [0]
+    for bit in NEAR:
+        masks += [m | bit for m in masks if bit < count]
+    return masks[1:]
+
+
+def far_bits(count):
+    return [1 << i for i in range(1, count.bit_length() - 1) if 1 << i not in NEAR]
+
+
+def sum_groups(count):
+    return [list(range(count // 2, count, 2)), list(range(0, count // 2, 2))]
 
 
 def swap(x, mask):
     count = lax.axis_size("col")
     return lax.ppermute(x, "col", [(i, i ^ mask) for i in range(count)])
-
-
-def far_bits(count):
-    return [1 << i for i in range(2, count.bit_length() - 1)]
-
-
-def far_pieces(count):
-    return list(range(0, count, 4))
 
 
 def gather(own):
@@ -40,8 +48,9 @@
     for bit in reversed(far_bits(count)):
         for p in list(pieces):
             pieces[p | bit] = swap(pieces[p], bit)
-    for p in sorted(pieces, key=lambda p: p.bit_count()):
-        pieces[p | HALF] = swap(pieces[p], HALF)
+    for p in sorted(pieces):
+        for mask in near_masks(count):
+            pieces[p | mask] = swap(pieces[p], mask)
     order = sorted(pieces, key=lambda p: p.bit_count())
     arrays = [([p], pieces[p][None]) for p in order]
     for start in range(0, len(order), 4):
@@ -50,13 +59,16 @@
     return arrays
 
 
-def scatter_sum(kept_half, sent_half, kept_own, sent_own):
+def scatter_sum(sums):
     count = lax.axis_size("col")
-    far = far_pieces(count)
-    half = kept_half + swap(sent_half, CORE)
-    crossed = {p: swap(half[j], HALF) for j, p in reversed(list(enumerate(far)))}
-    own = kept_own + swap(sent_own, CORE)
-    held = {p: own[j] + crossed[p] for j, p in enumerate(far)}
+    held = {}
+    for group, kept, sent in zip(sum_groups(count), sums[::2], sums[1::2], strict=True):
+        whole = kept + swap(sent, CORE)
+        held |= {p: whole[j] for j, p in enumerate(group)}
+    masks = near_masks(count)
+    for p in sorted((p for p in held if not p & sum(NEAR)), reverse=True):
+        for mask in reversed(masks):
+            held[p] += swap(held.pop(p | mask), mask)
     for bit in far_bits(count):
         for p in sorted((p for p in held if p & bit), reverse=True):
             held[p ^ bit] += swap(held.pop(p), bit)
@@ -86,10 +98,11 @@
 
 def give_sums(acc, outs, count, width, order):
     me = lax.axis_index("col")
-    for out, offset in zip(outs, (HALF, HALF | CORE, 0, CORE), strict=True):
-        for j, p in enumerate(far_pieces(count)):
-            for part, block, columns in places(me ^ (p | offset), order, width):
-                out[j, :, part] = acc[block, :, columns]
+    for g, group in enumerate(sum_groups(count)):
+        for core in (0, CORE):
+            for j, p in enumerate(group):
+                for part, block, columns in places(me ^ (p | core), order, width):
+                    outs[2 * g + core][j, :, part] = acc[block, :, columns]
 
 
 def add_products(row_block, col_block, high, low, err, acc):
@@ -174,7 +187,7 @@
     velocity = jnp.zeros(start_weight.shape, jnp.float32)
     for step in range(ITERS):
         terms = product(tile_plan, hess_tiles, gather(weights - dense_weight))
-        gradient = scatter_sum(*terms)
+        gradient = scatter_sum(terms)
         velocity = momentum * velocity + gradient
         weights = keep * (weights - step_size * velocity)
     return (weights, velocity)

time: 144 us -> 128 us (0.89)
  starting transfers between devices: 45.6 us -> 37.2 us
  waiting for transfers between devices: 51.3 us -> 44 us
    ppermute x36, starting transfers between devices: 45.6 us -> 37.2 us  [swap(): return lax.ppermute(x, 'col', [(i, i ^ mask) for i in range(count)])]
    ppermute x36, waiting for transfers between devices: 51.3 us -> 44 us  [swap(): return lax.ppermute(x, 'col', [(i, i ^ mask) for i in range(count)])]
  transfers between devices with their start and end apart: 36 -> 36, of which waited for: 21 -> 25; matrix products, arithmetic and copies ran while one was open for 1% -> 2% of each run, Pallas kernels for 0% -> 0%
where the time goes in v3:
time: 128 us
  waiting for transfers between devices  44 us (34%)
  Pallas kernels  41.8 us (33%)
  starting transfers between devices  37.2 us (29%)
  other arithmetic  3.1 us (2%)
    ppermute x36, waiting for transfers between devices, swap(): return lax.ppermute(x, 'col', [(i, i ^ mask) for i in range(count)])  44 us
    pallas_call x2, Pallas kernels, product(): pl.pallas_call(functools.partial(product_kernel, held, width, together),...  41.8 us
    ppermute x36, starting transfers between devices, swap(): return lax.ppermute(x, 'col', [(i, i ^ mask) for i in range(count)])  37.2 us
  transfers between devices with their start and end apart: 36, of which 25 were waited for; matrix products, arithmetic and copies ran while one was open for 2% of the time, Pallas kernels for 0%

profile of v3, /device:TPU:0, one launch (start us, length us, event | category | flops | bytes accessed | tf_op | source)
XLA Modules:
  0.0 127.8 jit_solution(14830125914149744496)
XLA Ops:
  1.7 4.1 %collective-permute-start = (f32[32,1024]{1,0:T(8,128)S(1)}, f32[32,1024]{1,0:T(8,128)S(1)}, u32[]{:S(2)}, u32[]{:S(2)}) collective-permute-start(f32[32,1024]{1,0:T(8,128)S(1)} %sub.12), channel_id=1, source_target_pairs={{0,8},{1,9},{2,10},{3,11},{4,12},{5,13},{6,14},{7,15},{8,0},{9,1},... | collective-permute-start | bytes 393224 | tf_op jit(solution)/shard_map/ppermute | solution.py:42
  5.8 1.6 %collective-permute-start.2 = (f32[32,1024]{1,0:T(8,128)S(1)}, f32[32,1024]{1,0:T(8,128)S(1)}, u32[]{:S(2)}, u32[]{:S(2)}) collective-permute-start(f32[32,1024]{1,0:T(8,128)S(1)} %sub.12), channel_id=1, source_target_pairs={{0,4},{1,5},{2,6},{3,7},{4,0},{5,1},{6,2},{7,3},{8,12},{9,13},{10,... | collective-permute-start | bytes 393224 | tf_op jit(solution)/shard_map/ppermute | solution.py:42
  7.4 1.5 %collective-permute-start.1 = (f32[32,1024]{1,0:T(8,128)S(1)}, f32[32,1024]{1,0:T(8,128)S(1)}, u32[]{:S(2)}, u32[]{:S(2)}) collective-permute-start(f32[32,1024]{1,0:T(8,128)S(1)} %sub.12), channel_id=1, source_target_pairs={{0,2},{1,3},{2,0},{3,1},{4,6},{5,7},{6,4},{7,5},{8,10},{9,11},{10,... | collective-permute-start | bytes 393224 | tf_op jit(solution)/shard_map/ppermute | solution.py:42
  9.3 2.9 %collective-permute-done = f32[32,1024]{1,0:T(8,128)S(1)} collective-permute-done((f32[32,1024]{1,0:T(8,128)S(1)}, f32[32,1024]{1,0:T(8,128)S(1)}, u32[]{:S(2)}, u32[]{:S(2)}) %collective-permute-start) | collective-permute-done | bytes 131104 | tf_op jit(solution)/shard_map/ppermute | solution.py:42
  12.2 1.6 %collective-permute-start.6 = (f32[32,1024]{1,0:T(8,128)S(1)}, f32[32,1024]{1,0:T(8,128)S(1)}, u32[]{:S(2)}, u32[]{:S(2)}) collective-permute-start(f32[32,1024]{1,0:T(8,128)S(1)} %collective-permute-done), channel_id=1, source_target_pairs={{0,6},{1,7},{2,4},{3,5},{4,2},{5,3},{6,0},{7,1},{8,14},{9,15},{10,... | collective-permute-start | bytes 393224 | tf_op jit(solution)/shard_map/ppermute | solution.py:42
  17.2 2.8 %collective-permute-done.6 = f32[32,1024]{1,0:T(8,128)S(1)} collective-permute-done((f32[32,1024]{1,0:T(8,128)S(1)}, f32[32,1024]{1,0:T(8,128)S(1)}, u32[]{:S(2)}, u32[]{:S(2)}) %collective-permute-start.6) | collective-permute-done | bytes 131104 | tf_op jit(solution)/shard_map/ppermute | solution.py:42
  24.8 20.9 %product.2 = (f32[4,32,1024]{2,1,0:T(8,128)S(1)}, f32[4,32,1024]{2,1,0:T(8,128)S(1)}, f32[4,32,1024]{2,1,0:T(8,128)S(1)}, f32[4,32,1024]{2,1,0:T(8,128)S(1)}) custom-call(s32[33,2]{1,0:T(8,128)S(1)} %copy.7.plan, f32[33,512,512]{2,1,0:T(8,128)} %tiles.3, f32[1,32,1024]{2,1,0:T(8,128)S(1)} %bitcast.83, f32[1,32,1024]{2,1,0:T(8,128)S(1)} %bitcast.85, ...), custom_call_target="tpu_custom_call" | custom-call | flops 3321888768 | bytes 34603008 | tf_op jit(solution)/shard_map/product/pallas_call | solution.py:165
  52.9 1.5 %collective-permute-start.12 = (f32[32,1024]{1,0:T(8,128)S(1)}, f32[32,1024]{1,0:T(8,128)S(1)}, u32[]{:S(2)}, u32[]{:S(2)}) collective-permute-start(f32[32,1024]{1,0:T(8,128)S(1)} %get-tuple-element.29), channel_id=1, source_target_pairs={{0,2},{1,3},{2,0},{3,1},{4,6},{5,7},{6,4},{7,5},{8,10},{9,11},{10,... | collective-permute-start | bytes 393224 | tf_op jit(solution)/shard_map/ppermute | solution.py:42
  56.5 1.5 %collective-permute-done.16 = f32[32,1024]{1,0:T(8,128)S(1)} collective-permute-done((f32[32,1024]{1,0:T(8,128)S(1)}, f32[32,1024]{1,0:T(8,128)S(1)}, u32[]{:S(2)}, u32[]{:S(2)}) %collective-permute-start.16) | collective-permute-done | bytes 131104 | tf_op jit(solution)/shard_map/ppermute | solution.py:42
  58.0 2.4 %collective-permute-start.17 = (f32[32,1024]{1,0:T(8,128)S(1)}, f32[32,1024]{1,0:T(8,128)S(1)}, u32[]{:S(2)}, u32[]{:S(2)}) collective-permute-start(f32[32,1024]{1,0:T(8,128)S(1)} %fusion.10), channel_id=1, source_target_pairs={{0,8},{1,9},{2,10},{3,11},{4,12},{5,13},{6,14},{7,15},{8,0},{9,1},... | collective-permute-start | bytes 393224 | tf_op jit(solution)/shard_map/ppermute | solution.py:42
  60.8 1.9 %collective-permute-done.12 = f32[32,1024]{1,0:T(8,128)S(1)} collective-permute-done((f32[32,1024]{1,0:T(8,128)S(1)}, f32[32,1024]{1,0:T(8,128)S(1)}, u32[]{:S(2)}, u32[]{:S(2)}) %collective-permute-start.12) | collective-permute-done | bytes 131104 | tf_op jit(solution)/shard_map/ppermute | solution.py:42
  62.9 4.1 %collective-permute-done.17 = f32[32,1024]{1,0:T(8,128)S(1)} collective-permute-done((f32[32,1024]{1,0:T(8,128)S(1)}, f32[32,1024]{1,0:T(8,128)S(1)}, u32[]{:S(2)}, u32[]{:S(2)}) %collective-permute-start.17) | collective-permute-done | bytes 131104 | tf_op jit(solution)/shard_map/ppermute | solution.py:42
  67.2 2.8 %collective-permute-start.20 = (f32[32,1024]{1,0:T(8,128)S(1)}, f32[32,1024]{1,0:T(8,128)S(1)}, u32[]{:S(2)}, u32[]{:S(2)}) collective-permute-start(f32[32,1024]{1,0:T(8,128)S(1)} %get-tuple-element.20), channel_id=1, source_target_pairs={{0,4},{1,5},{2,6},{3,7},{4,0},{5,1},{6,2},{7,3},{8,12},{9,13},{10,... | collective-permute-start | bytes 393224 | tf_op jit(solution)/shard_map/ppermute | solution.py:42
  71.4 2.7 %collective-permute-done.18 = f32[32,1024]{1,0:T(8,128)S(1)} collective-permute-done((f32[32,1024]{1,0:T(8,128)S(1)}, f32[32,1024]{1,0:T(8,128)S(1)}, u32[]{:S(2)}, u32[]{:S(2)}) %collective-permute-start.18) | collective-permute-done | bytes 131104 | tf_op jit(solution)/shard_map/ppermute | solution.py:42
  78.6 2.6 %collective-permute-done.24 = f32[32,1024]{1,0:T(8,128)S(1)} collective-permute-done((f32[32,1024]{1,0:T(8,128)S(1)}, f32[32,1024]{1,0:T(8,128)S(1)}, u32[]{:S(2)}, u32[]{:S(2)}) %collective-permute-start.24) | collective-permute-done | bytes 131104 | tf_op jit(solution)/shard_map/ppermute | solution.py:42
  81.3 1.9 %collective-permute-done.23 = f32[32,1024]{1,0:T(8,128)S(1)} collective-permute-done((f32[32,1024]{1,0:T(8,128)S(1)}, f32[32,1024]{1,0:T(8,128)S(1)}, u32[]{:S(2)}, u32[]{:S(2)}) %collective-permute-start.23) | collective-permute-done | bytes 131104 | tf_op jit(solution)/shard_map/ppermute | solution.py:42
  83.3 1.9 %collective-permute-done.26.refs_9_ = f32[4,32,1024]{2,1,0:T(8,128)S(1)} collective-permute-done((f32[4,32,1024]{2,1,0:T(8,128)S(1)}, f32[4,32,1024]{2,1,0:T(8,128)S(1)}, u32[]{:S(2)}, u32[]{:S(2)}) %collective-permute-start.26) | collective-permute-done | bytes 524320 | tf_op jit(solution)/shard_map/ppermute | solution.py:42
  85.2 20.9 %product.3 = (f32[4,32,1024]{2,1,0:T(8,128)S(1)}, f32[4,32,1024]{2,1,0:T(8,128)S(1)}, f32[4,32,1024]{2,1,0:T(8,128)S(1)}, f32[4,32,1024]{2,1,0:T(8,128)S(1)}) custom-call(s32[33,2]{1,0:T(8,128)S(1)} %copy.7.plan, f32[33,512,512]{2,1,0:T(8,128)} %tiles.3, f32[1,32,1024]{2,1,0:T(8,128)S(1)} %bitcast.81, f32[1,32,1024]{2,1,0:T(8,128)S(1)} %bitcast.87, ...), custom_call_target="tpu_custom_call" | custom-call | flops 3321888768 | bytes 34603008 | tf_op jit(solution)/shard_map/product/pallas_call | solution.py:165
  110.1 1.6 %collective-permute-start.33 = (f32[32,1024]{1,0:T(8,128)S(1)}, f32[32,1024]{1,0:T(8,128)S(1)}, u32[]{:S(2)}, u32[]{:S(2)}) collective-permute-start(f32[32,1024]{1,0:T(8,128)S(1)} %get-tuple-element.27), channel_id=1, source_target_pairs={{0,4},{1,5},{2,6},{3,7},{4,0},{5,1},{6,2},{7,3},{8,12},{9,13},{10,... | collective-permute-start | bytes 393224 | tf_op jit(solution)/shard_map/ppermute | solution.py:42
  113.8 1.8 %collective-permute-done.32 = f32[32,1024]{1,0:T(8,128)S(1)} collective-permute-done((f32[32,1024]{1,0:T(8,128)S(1)}, f32[32,1024]{1,0:T(8,128)S(1)}, u32[]{:S(2)}, u32[]{:S(2)}) %collective-permute-start.32) | collective-permute-done | bytes 131104 | tf_op jit(solution)/shard_map/ppermute | solution.py:42
  115.5 2.9 %collective-permute-done.34 = f32[32,1024]{1,0:T(8,128)S(1)} collective-permute-done((f32[32,1024]{1,0:T(8,128)S(1)}, f32[32,1024]{1,0:T(8,128)S(1)}, u32[]{:S(2)}, u32[]{:S(2)}) %collective-permute-start.34) | collective-permute-done | bytes 131104 | tf_op jit(solution)/shard_map/ppermute | solution.py:42
  119.6 3.1 %collective-permute-done.28 = f32[32,1024]{1,0:T(8,128)S(1)} collective-permute-done((f32[32,1024]{1,0:T(8,128)S(1)}, f32[32,1024]{1,0:T(8,128)S(1)}, u32[]{:S(2)}, u32[]{:S(2)}) %collective-permute-start.28) | collective-permute-done | bytes 131104 | tf_op jit(solution)/shard_map/ppermute | solution.py:42
  123.0 2.0 %collective-permute-done.29 = f32[32,1024]{1,0:T(8,128)S(1)} collective-permute-done((f32[32,1024]{1,0:T(8,128)S(1)}, f32[32,1024]{1,0:T(8,128)S(1)}, u32[]{:S(2)}, u32[]{:S(2)}) %collective-permute-start.29) | collective-permute-done | bytes 131104 | tf_op jit(solution)/shard_map/ppermute | solution.py:42
  125.1 2.0 %collective-permute-done.35 = f32[32,1024]{1,0:T(8,128)S(1)} collective-permute-done((f32[32,1024]{1,0:T(8,128)S(1)}, f32[32,1024]{1,0:T(8,128)S(1)}, u32[]{:S(2)}, u32[]{:S(2)}) %collective-permute-start.35) | collective-permute-done | bytes 131104 | tf_op jit(solution)/shard_map/ppermute | solution.py:42
  (74 shorter events, 34.1 us)
Async XLA Ops:
  1.7 10.5 %collective-permute-start = (f32[32,1024]{1,0:T(8,128)S(1)}, f32[32,1024]{1,0:T(8,128)S(1)}, u32[]{:S(2)}, u32[]{:S(2)}) collective-permute-start(f32[32,1024]{1,0:T(8,128)S(1)} %sub.12), channel_id=1, source_target_pairs={{0,8},{1,9},{2,10},{3,11},{4,12},{5,13},{6,14},{7,15},{8,0},{9,1},... | collective-permute-start | bytes 393224 | tf_op jit(solution)/shard_map/ppermute | solution.py:42
  5.8 9.4 %collective-permute-start.2 = (f32[32,1024]{1,0:T(8,128)S(1)}, f32[32,1024]{1,0:T(8,128)S(1)}, u32[]{:S(2)}, u32[]{:S(2)}) collective-permute-start(f32[32,1024]{1,0:T(8,128)S(1)} %sub.12), channel_id=1, source_target_pairs={{0,4},{1,5},{2,6},{3,7},{4,0},{5,1},{6,2},{7,3},{8,12},{9,13},{10,... | collective-permute-start | bytes 393224 | tf_op jit(solution)/shard_map/ppermute | solution.py:42
  7.4 8.3 %collective-permute-start.1 = (f32[32,1024]{1,0:T(8,128)S(1)}, f32[32,1024]{1,0:T(8,128)S(1)}, u32[]{:S(2)}, u32[]{:S(2)}) collective-permute-start(f32[32,1024]{1,0:T(8,128)S(1)} %sub.12), channel_id=1, source_target_pairs={{0,2},{1,3},{2,0},{3,1},{4,6},{5,7},{6,4},{7,5},{8,10},{9,11},{10,... | collective-permute-start | bytes 393224 | tf_op jit(solution)/shard_map/ppermute | solution.py:42
  8.9 8.3 %collective-permute-start.3 = (f32[32,1024]{1,0:T(8,128)S(1)}, f32[32,1024]{1,0:T(8,128)S(1)}, u32[]{:S(2)}, u32[]{:S(2)}) collective-permute-start(f32[32,1024]{1,0:T(8,128)S(1)} %sub.12), channel_id=1, source_target_pairs={{0,6},{1,7},{2,4},{3,5},{4,2},{5,3},{6,0},{7,1},{8,14},{9,15},{10,... | collective-permute-start | bytes 393224 | tf_op jit(solution)/shard_map/ppermute | solution.py:42
  12.2 7.7 %collective-permute-start.6 = (f32[32,1024]{1,0:T(8,128)S(1)}, f32[32,1024]{1,0:T(8,128)S(1)}, u32[]{:S(2)}, u32[]{:S(2)}) collective-permute-start(f32[32,1024]{1,0:T(8,128)S(1)} %collective-permute-done), channel_id=1, source_target_pairs={{0,6},{1,7},{2,4},{3,5},{4,2},{5,3},{6,0},{7,1},{8,14},{9,15},{10,... | collective-permute-start | bytes 393224 | tf_op jit(solution)/shard_map/ppermute | solution.py:42
  15.7 7.7 %collective-permute-start.7 = (f32[4,32,1024]{2,1,0:T(8,128)S(1)}, f32[4,32,1024]{2,1,0:T(8,128)S(1)}, u32[]{:S(2)}, u32[]{:S(2)}) collective-permute-start(f32[4,32,1024]{2,1,0:T(8,128)S(1)} %pad_maximum_fusion), channel_id=1, source_target_pairs={{0,1},{1,0},{2,3},{3,2},{4,5},{5,4},{6,7},{7,6},{8,9},{9,8},{10,11... | collective-permute-start | bytes 1572872 | tf_op jit(solution)/shard_map/ppermute | solution.py:42
  47.8 7.3 %collective-permute-start.14 = (f32[32,1024]{1,0:T(8,128)S(1)}, f32[32,1024]{1,0:T(8,128)S(1)}, u32[]{:S(2)}, u32[]{:S(2)}) collective-permute-start(f32[32,1024]{1,0:T(8,128)S(1)} %get-tuple-element.31), channel_id=1, source_target_pairs={{0,6},{1,7},{2,4},{3,5},{4,2},{5,3},{6,0},{7,1},{8,14},{9,15},{10,... | collective-permute-start | bytes 393224 | tf_op jit(solution)/shard_map/ppermute | solution.py:42
  49.2 8.8 %collective-permute-start.16 = (f32[32,1024]{1,0:T(8,128)S(1)}, f32[32,1024]{1,0:T(8,128)S(1)}, u32[]{:S(2)}, u32[]{:S(2)}) collective-permute-start(f32[32,1024]{1,0:T(8,128)S(1)} %get-tuple-element.32), channel_id=1, source_target_pairs={{0,2},{1,3},{2,0},{3,1},{4,6},{5,7},{6,4},{7,5},{8,10},{9,11},{10,... | collective-permute-start | bytes 393224 | tf_op jit(solution)/shard_map/ppermute | solution.py:42
  50.7 7.3 %collective-permute-start.15 = (f32[32,1024]{1,0:T(8,128)S(1)}, f32[32,1024]{1,0:T(8,128)S(1)}, u32[]{:S(2)}, u32[]{:S(2)}) collective-permute-start(f32[32,1024]{1,0:T(8,128)S(1)} %get-tuple-element.33), channel_id=1, source_target_pairs={{0,4},{1,5},{2,6},{3,7},{4,0},{5,1},{6,2},{7,3},{8,12},{9,13},{10,... | collective-permute-start | bytes 393224 | tf_op jit(solution)/shard_map/ppermute | solution.py:42
  51.4 9.3 %collective-permute-start.10 = (f32[32,1024]{1,0:T(8,128)S(1)}, f32[32,1024]{1,0:T(8,128)S(1)}, u32[]{:S(2)}, u32[]{:S(2)}) collective-permute-start(f32[32,1024]{1,0:T(8,128)S(1)} %get-tuple-element.28), channel_id=1, source_target_pairs={{0,6},{1,7},{2,4},{3,5},{4,2},{5,3},{6,0},{7,1},{8,14},{9,15},{10,... | collective-permute-start | bytes 393224 | tf_op jit(solution)/shard_map/ppermute | solution.py:42
  52.9 9.8 %collective-permute-start.12 = (f32[32,1024]{1,0:T(8,128)S(1)}, f32[32,1024]{1,0:T(8,128)S(1)}, u32[]{:S(2)}, u32[]{:S(2)}) collective-permute-start(f32[32,1024]{1,0:T(8,128)S(1)} %get-tuple-element.29), channel_id=1, source_target_pairs={{0,2},{1,3},{2,0},{3,1},{4,6},{5,7},{6,4},{7,5},{8,10},{9,11},{10,... | collective-permute-start | bytes 393224 | tf_op jit(solution)/shard_map/ppermute | solution.py:42
  55.1 7.8 %collective-permute-start.11 = (f32[32,1024]{1,0:T(8,128)S(1)}, f32[32,1024]{1,0:T(8,128)S(1)}, u32[]{:S(2)}, u32[]{:S(2)}) collective-permute-start(f32[32,1024]{1,0:T(8,128)S(1)} %get-tuple-element.30), channel_id=1, source_target_pairs={{0,4},{1,5},{2,6},{3,7},{4,0},{5,1},{6,2},{7,3},{8,12},{9,13},{10,... | collective-permute-start | bytes 393224 | tf_op jit(solution)/shard_map/ppermute | solution.py:42
  58.0 9.0 %collective-permute-start.17 = (f32[32,1024]{1,0:T(8,128)S(1)}, f32[32,1024]{1,0:T(8,128)S(1)}, u32[]{:S(2)}, u32[]{:S(2)}) collective-permute-start(f32[32,1024]{1,0:T(8,128)S(1)} %fusion.10), channel_id=1, source_target_pairs={{0,8},{1,9},{2,10},{3,11},{4,12},{5,13},{6,14},{7,15},{8,0},{9,1},... | collective-permute-start | bytes 393224 | tf_op jit(solution)/shard_map/ppermute | solution.py:42
  67.2 9.4 %collective-permute-start.20 = (f32[32,1024]{1,0:T(8,128)S(1)}, f32[32,1024]{1,0:T(8,128)S(1)}, u32[]{:S(2)}, u32[]{:S(2)}) collective-permute-start(f32[32,1024]{1,0:T(8,128)S(1)} %get-tuple-element.20), channel_id=1, source_target_pairs={{0,4},{1,5},{2,6},{3,7},{4,0},{5,1},{6,2},{7,3},{8,12},{9,13},{10,... | collective-permute-start | bytes 393224 | tf_op jit(solution)/shard_map/ppermute | solution.py:42
  70.0 7.7 %collective-permute-start.19 = (f32[32,1024]{1,0:T(8,128)S(1)}, f32[32,1024]{1,0:T(8,128)S(1)}, u32[]{:S(2)}, u32[]{:S(2)}) collective-permute-start(f32[32,1024]{1,0:T(8,128)S(1)} %get-tuple-element.20), channel_id=1, source_target_pairs={{0,2},{1,3},{2,0},{3,1},{4,6},{5,7},{6,4},{7,5},{8,10},{9,11},{10,... | collective-permute-start | bytes 393224 | tf_op jit(solution)/shard_map/ppermute | solution.py:42
  71.3 7.3 %collective-permute-start.21 = (f32[32,1024]{1,0:T(8,128)S(1)}, f32[32,1024]{1,0:T(8,128)S(1)}, u32[]{:S(2)}, u32[]{:S(2)}) collective-permute-start(f32[32,1024]{1,0:T(8,128)S(1)} %get-tuple-element.20), channel_id=1, source_target_pairs={{0,6},{1,7},{2,4},{3,5},{4,2},{5,3},{6,0},{7,1},{8,14},{9,15},{10,... | collective-permute-start | bytes 393224 | tf_op jit(solution)/shard_map/ppermute | solution.py:42
  75.2 8.0 %collective-permute-start.23 = (f32[32,1024]{1,0:T(8,128)S(1)}, f32[32,1024]{1,0:T(8,128)S(1)}, u32[]{:S(2)}, u32[]{:S(2)}) collective-permute-start(f32[32,1024]{1,0:T(8,128)S(1)} %collective-permute-done.18), channel_id=1, source_target_pairs={{0,4},{1,5},{2,6},{3,7},{4,0},{5,1},{6,2},{7,3},{8,12},{9,13},{10,... | collective-permute-start | bytes 393224 | tf_op jit(solution)/shard_map/ppermute | solution.py:42
  108.2 7.4 %collective-permute-start.32 = (f32[32,1024]{1,0:T(8,128)S(1)}, f32[32,1024]{1,0:T(8,128)S(1)}, u32[]{:S(2)}, u32[]{:S(2)}) collective-permute-start(f32[32,1024]{1,0:T(8,128)S(1)} %get-tuple-element.25), channel_id=1, source_target_pairs={{0,6},{1,7},{2,4},{3,5},{4,2},{5,3},{6,0},{7,1},{8,14},{9,15},{10,... | collective-permute-start | bytes 393224 | tf_op jit(solution)/shard_map/ppermute | solution.py:42
  109.3 9.1 %collective-permute-start.34 = (f32[32,1024]{1,0:T(8,128)S(1)}, f32[32,1024]{1,0:T(8,128)S(1)}, u32[]{:S(2)}, u32[]{:S(2)}) collective-permute-start(f32[32,1024]{1,0:T(8,128)S(1)} %get-tuple-element.26), channel_id=1, source_target_pairs={{0,2},{1,3},{2,0},{3,1},{4,6},{5,7},{6,4},{7,5},{8,10},{9,11},{10,... | collective-permute-start | bytes 393224 | tf_op jit(solution)/shard_map/ppermute | solution.py:42
  110.1 8.3 %collective-permute-start.33 = (f32[32,1024]{1,0:T(8,128)S(1)}, f32[32,1024]{1,0:T(8,128)S(1)}, u32[]{:S(2)}, u32[]{:S(2)}) collective-permute-start(f32[32,1024]{1,0:T(8,128)S(1)} %get-tuple-element.27), channel_id=1, source_target_pairs={{0,4},{1,5},{2,6},{3,7},{4,0},{5,1},{6,2},{7,3},{8,12},{9,13},{10,... | collective-permute-start | bytes 393224 | tf_op jit(solution)/shard_map/ppermute | solution.py:42
  111.8 10.8 %collective-permute-start.28 = (f32[32,1024]{1,0:T(8,128)S(1)}, f32[32,1024]{1,0:T(8,128)S(1)}, u32[]{:S(2)}, u32[]{:S(2)}) collective-permute-start(f32[32,1024]{1,0:T(8,128)S(1)} %get-tuple-element.22), channel_id=1, source_target_pairs={{0,6},{1,7},{2,4},{3,5},{4,2},{5,3},{6,0},{7,1},{8,14},{9,15},{10,... | collective-permute-start | bytes 393224 | tf_op jit(solution)/shard_map/ppermute | solution.py:42
  113.0 10.0 %collective-permute-start.30 = (f32[32,1024]{1,0:T(8,128)S(1)}, f32[32,1024]{1,0:T(8,128)S(1)}, u32[]{:S(2)}, u32[]{:S(2)}) collective-permute-start(f32[32,1024]{1,0:T(8,128)S(1)} %get-tuple-element.23), channel_id=1, source_target_pairs={{0,2},{1,3},{2,0},{3,1},{4,6},{5,7},{6,4},{7,5},{8,10},{9,11},{10,... | collective-permute-start | bytes 393224 | tf_op jit(solution)/shard_map/ppermute | solution.py:42
  115.5 9.5 %collective-permute-start.29 = (f32[32,1024]{1,0:T(8,128)S(1)}, f32[32,1024]{1,0:T(8,128)S(1)}, u32[]{:S(2)}, u32[]{:S(2)}) collective-permute-start(f32[32,1024]{1,0:T(8,128)S(1)} %get-tuple-element.24), channel_id=1, source_target_pairs={{0,4},{1,5},{2,6},{3,7},{4,0},{5,1},{6,2},{7,3},{8,12},{9,13},{10,... | collective-permute-start | bytes 393224 | tf_op jit(solution)/shard_map/ppermute | solution.py:42
  118.4 8.6 %collective-permute-start.35 = (f32[32,1024]{1,0:T(8,128)S(1)}, f32[32,1024]{1,0:T(8,128)S(1)}, u32[]{:S(2)}, u32[]{:S(2)}) collective-permute-start(f32[32,1024]{1,0:T(8,128)S(1)} %fusion.2), channel_id=1, source_target_pairs={{0,8},{1,9},{2,10},{3,11},{4,12},{5,13},{6,14},{7,15},{8,0},{9,1},... | collective-permute-start | bytes 393224 | tf_op jit(solution)/shard_map/ppermute | solution.py:42
  (15 other events, 257.9 us)

commit v4 on v3

--- a/solution.py
+++ b/solution.py
@@ -10,7 +10,7 @@
 ITERS = 2
 MIB = 2**20
 SCOPED = 24 * MIB
-DEPTH = 3
+DEPTH = 6
 
 step_size = 0.15
 momentum = 0.6
@@ -105,52 +105,76 @@
                     outs[2 * g + core][j, :, part] = acc[block, :, columns]
 
 
-def add_products(row_block, col_block, high, low, err, acc):
+def add_products(row_block, col_block, ready, err, acc):
     rows = acc.shape[1]
-    for source, target, dim in ((row_block, col_block, 0), (col_block, row_block, 1)):
-        dims = (((1,), (dim,)), ((), ()))
+
+    def term(source, at):
         both = err[source]
-        lead = lax.dot_general(both, high, dims, preferred_element_type=jnp.float32)
-        rest = lax.dot_general(both[:rows], low, dims, preferred_element_type=jnp.float32)
-        term = lead[:rows] + (lead[rows:] + rest)
-        if dim:
-            term = jnp.where(row_block != col_block, term, 0.0)
-        acc[target] += term
-
-
-def product_kernel(held, width, together, plan, tiles, *refs):
+        lead = jnp.dot(both, ready[at], preferred_element_type=jnp.float32)
+        rest = jnp.dot(both[:rows], ready[at + 1], preferred_element_type=jnp.float32)
+        return lead[:rows] + (lead[rows:] + rest)
+
+    acc[col_block] += term(row_block, 0)
+    acc[row_block] += jnp.where(row_block != col_block, term(col_block, 2), 0.0)
+
+
+def split_tile(tile, ready):
+    for at, x in ((0, tile), (2, tile.T)):
+        high = x.astype(jnp.bfloat16)
+        ready[at] = high
+        ready[at + 1] = (x - high.astype(jnp.float32)).astype(jnp.bfloat16)
+
+
+def product_kernel(held, width, plan, tiles, *refs):
     pieces = refs[: len(held)]
-    *outs, err, acc, ring, arrived = refs[len(held) :]
+    *outs, err, acc, ring, arrived, even, odd = refs[len(held) :]
     slots, order, _ = tiles.shape
     count = acc.shape[0] * order // width
-    steps = slots // together
     depth = ring.shape[0]
 
-    def fetch(step):
-        at = lax.rem(step, depth)
-        return pltpu.make_async_copy(tiles.at[pl.ds(step * together, together)], ring.at[at], arrived.at[at])
-
-    for step in range(min(depth, steps)):
-        fetch(step).start()
+    def fetch(slot):
+        at = lax.rem(slot, depth)
+        return pltpu.make_async_copy(tiles.at[slot], ring.at[at], arrived.at[at])
+
+    def refill(slot):
+        @pl.when(slot + depth < slots)
+        def _():
+            fetch(slot + depth).start()
+
+    def prepare(slot, ready):
+        split_tile(ring[lax.rem(slot, depth)], ready)
+
+    def multiply(slot, ready):
+        add_products(plan[slot, 0], plan[slot, 1], ready, err, acc)
+
+    for slot in range(min(depth, slots)):
+        fetch(slot).start()
     take_pieces(held, pieces, err, order)
     acc[...] = jnp.zeros(acc.shape, jnp.float32)
-
-    def one_step(step, carry):
-        fetch(step).wait()
-        for j in range(together):
-            slot = step * together + j
-            tile = ring[lax.rem(step, depth), j]
-            high = tile.astype(jnp.bfloat16)
-            low = (tile - high.astype(jnp.float32)).astype(jnp.bfloat16)
-            add_products(plan[slot, 0], plan[slot, 1], high, low, err, acc)
-
-        @pl.when(step + depth < steps)
-        def _():
-            fetch(step + depth).start()
-
+    fetch(0).wait()
+    prepare(0, even)
+    refill(0)
+
+    def two_slots(step, carry):
+        slot = 2 * step
+        fetch(slot + 1).wait()
+        fetch(slot + 2).wait()
+        prepare(slot + 1, odd)
+        multiply(slot, even)
+        prepare(slot + 2, even)
+        multiply(slot + 1, odd)
+        refill(slot + 1)
+        refill(slot + 2)
         return carry
 
-    lax.fori_loop(0, steps, one_step, 0)
+    lax.fori_loop(0, (slots - 1) // 2, two_slots, 0)
+    if slots % 2:
+        multiply(slots - 1, even)
+    else:
+        fetch(slots - 1).wait()
+        prepare(slots - 1, odd)
+        multiply(slots - 2, even)
+        multiply(slots - 1, odd)
     give_sums(acc, outs, count, width, order)
 
 
@@ -160,18 +184,19 @@
     count = sum(len(p) for p in held)
     _, rows, width = arrays[0][1].shape
     blocks = count * width // order
-    together = 3 if slots % 3 == 0 else 1
     some = jax.ShapeDtypeStruct((count // 4, rows, width), jnp.float32)
     return pl.pallas_call(
-        functools.partial(product_kernel, held, width, together),
+        functools.partial(product_kernel, held, width),
         in_specs=[IN_SMEM, pl.BlockSpec(memory_space=pl.ANY)] + [IN_VMEM] * len(held),
         out_specs=[IN_VMEM] * 4,
         out_shape=[some] * 4,
         scratch_shapes=[
             pltpu.VMEM((blocks, 2 * rows, order), jnp.bfloat16),
             pltpu.VMEM((blocks, rows, order), jnp.float32),
-            pltpu.VMEM((DEPTH, together, order, order), jnp.float32),
+            pltpu.VMEM((DEPTH, order, order), jnp.float32),
             pltpu.SemaphoreType.DMA((DEPTH,)),
+            pltpu.VMEM((4, order, order), jnp.bfloat16),
+            pltpu.VMEM((4, order, order), jnp.bfloat16),
         ],
         compiler_params=pltpu.CompilerParams(vmem_limit_bytes=SCOPED),
         cost_estimate=pl.CostEstimate(

time: 128 us -> 121 us (0.945)
  Pallas kernels: 41.8 us -> 34.7 us
    pallas_call x2, Pallas kernels: 41.8 us -> 34.7 us  [product(): pl.pallas_call(functools.partial(product_kernel, held, width), in_specs=[...]
where the time goes in v4:
time: 121 us
  waiting for transfers between devices  44 us (36%)
  starting transfers between devices  37.2 us (31%)
  Pallas kernels  34.7 us (29%)
  other arithmetic  3.1 us (3%)
    ppermute x36, waiting for transfers between devices, swap(): return lax.ppermute(x, 'col', [(i, i ^ mask) for i in range(count)])  44 us
    ppermute x36, starting transfers between devices, swap(): return lax.ppermute(x, 'col', [(i, i ^ mask) for i in range(count)])  37.2 us
    pallas_call x2, Pallas kernels, product(): pl.pallas_call(functools.partial(product_kernel, held, width), in_specs=[...  34.7 us
  transfers between devices with their start and end apart: 36, of which 25 were waited for; matrix products, arithmetic and copies ran while one was open for 2% of the time, Pallas kernels for 0%

profile of v4, /device:TPU:0, one launch (start us, length us, event | category | flops | bytes accessed | tf_op | source)
XLA Modules:
  0.0 120.8 jit_solution(9415237633778660929)
XLA Ops:
  1.7 4.1 %collective-permute-start = (f32[32,1024]{1,0:T(8,128)S(1)}, f32[32,1024]{1,0:T(8,128)S(1)}, u32[]{:S(2)}, u32[]{:S(2)}) collective-permute-start(f32[32,1024]{1,0:T(8,128)S(1)} %sub.12), channel_id=1, source_target_pairs={{0,8},{1,9},{2,10},{3,11},{4,12},{5,13},{6,14},{7,15},{8,0},{9,1},... | collective-permute-start | bytes 393224 | tf_op jit(solution)/shard_map/ppermute | solution.py:42
  5.8 1.6 %collective-permute-start.2 = (f32[32,1024]{1,0:T(8,128)S(1)}, f32[32,1024]{1,0:T(8,128)S(1)}, u32[]{:S(2)}, u32[]{:S(2)}) collective-permute-start(f32[32,1024]{1,0:T(8,128)S(1)} %sub.12), channel_id=1, source_target_pairs={{0,4},{1,5},{2,6},{3,7},{4,0},{5,1},{6,2},{7,3},{8,12},{9,13},{10,... | collective-permute-start | bytes 393224 | tf_op jit(solution)/shard_map/ppermute | solution.py:42
  7.4 1.5 %collective-permute-start.1 = (f32[32,1024]{1,0:T(8,128)S(1)}, f32[32,1024]{1,0:T(8,128)S(1)}, u32[]{:S(2)}, u32[]{:S(2)}) collective-permute-start(f32[32,1024]{1,0:T(8,128)S(1)} %sub.12), channel_id=1, source_target_pairs={{0,2},{1,3},{2,0},{3,1},{4,6},{5,7},{6,4},{7,5},{8,10},{9,11},{10,... | collective-permute-start | bytes 393224 | tf_op jit(solution)/shard_map/ppermute | solution.py:42
  9.3 2.9 %collective-permute-done = f32[32,1024]{1,0:T(8,128)S(1)} collective-permute-done((f32[32,1024]{1,0:T(8,128)S(1)}, f32[32,1024]{1,0:T(8,128)S(1)}, u32[]{:S(2)}, u32[]{:S(2)}) %collective-permute-start) | collective-permute-done | bytes 131104 | tf_op jit(solution)/shard_map/ppermute | solution.py:42
  12.2 1.6 %collective-permute-start.6 = (f32[32,1024]{1,0:T(8,128)S(1)}, f32[32,1024]{1,0:T(8,128)S(1)}, u32[]{:S(2)}, u32[]{:S(2)}) collective-permute-start(f32[32,1024]{1,0:T(8,128)S(1)} %collective-permute-done), channel_id=1, source_target_pairs={{0,6},{1,7},{2,4},{3,5},{4,2},{5,3},{6,0},{7,1},{8,14},{9,15},{10,... | collective-permute-start | bytes 393224 | tf_op jit(solution)/shard_map/ppermute | solution.py:42
  17.2 2.8 %collective-permute-done.6 = f32[32,1024]{1,0:T(8,128)S(1)} collective-permute-done((f32[32,1024]{1,0:T(8,128)S(1)}, f32[32,1024]{1,0:T(8,128)S(1)}, u32[]{:S(2)}, u32[]{:S(2)}) %collective-permute-start.6) | collective-permute-done | bytes 131104 | tf_op jit(solution)/shard_map/ppermute | solution.py:42
  24.8 17.4 %product.2 = (f32[4,32,1024]{2,1,0:T(8,128)S(1)}, f32[4,32,1024]{2,1,0:T(8,128)S(1)}, f32[4,32,1024]{2,1,0:T(8,128)S(1)}, f32[4,32,1024]{2,1,0:T(8,128)S(1)}) custom-call(s32[33,2]{1,0:T(8,128)S(1)} %copy.7.plan, f32[33,512,512]{2,1,0:T(8,128)} %tiles.3, f32[1,32,1024]{2,1,0:T(8,128)S(1)} %bitcast.83, f32[1,32,1024]{2,1,0:T(8,128)S(1)} %bitcast.85, ...), custom_call_target="tpu_custom_call" | custom-call | flops 3321888768 | bytes 34603008 | tf_op jit(solution)/shard_map/product/pallas_call | solution.py:188
  49.4 1.5 %collective-permute-start.12 = (f32[32,1024]{1,0:T(8,128)S(1)}, f32[32,1024]{1,0:T(8,128)S(1)}, u32[]{:S(2)}, u32[]{:S(2)}) collective-permute-start(f32[32,1024]{1,0:T(8,128)S(1)} %get-tuple-element.29), channel_id=1, source_target_pairs={{0,2},{1,3},{2,0},{3,1},{4,6},{5,7},{6,4},{7,5},{8,10},{9,11},{10,... | collective-permute-start | bytes 393224 | tf_op jit(solution)/shard_map/ppermute | solution.py:42
  53.0 1.5 %collective-permute-done.16 = f32[32,1024]{1,0:T(8,128)S(1)} collective-permute-done((f32[32,1024]{1,0:T(8,128)S(1)}, f32[32,1024]{1,0:T(8,128)S(1)}, u32[]{:S(2)}, u32[]{:S(2)}) %collective-permute-start.16) | collective-permute-done | bytes 131104 | tf_op jit(solution)/shard_map/ppermute | solution.py:42
  54.5 2.4 %collective-permute-start.17 = (f32[32,1024]{1,0:T(8,128)S(1)}, f32[32,1024]{1,0:T(8,128)S(1)}, u32[]{:S(2)}, u32[]{:S(2)}) collective-permute-start(f32[32,1024]{1,0:T(8,128)S(1)} %fusion.10), channel_id=1, source_target_pairs={{0,8},{1,9},{2,10},{3,11},{4,12},{5,13},{6,14},{7,15},{8,0},{9,1},... | collective-permute-start | bytes 393224 | tf_op jit(solution)/shard_map/ppermute | solution.py:42
  57.2 1.9 %collective-permute-done.12 = f32[32,1024]{1,0:T(8,128)S(1)} collective-permute-done((f32[32,1024]{1,0:T(8,128)S(1)}, f32[32,1024]{1,0:T(8,128)S(1)}, u32[]{:S(2)}, u32[]{:S(2)}) %collective-permute-start.12) | collective-permute-done | bytes 131104 | tf_op jit(solution)/shard_map/ppermute | solution.py:42
  59.3 4.1 %collective-permute-done.17 = f32[32,1024]{1,0:T(8,128)S(1)} collective-permute-done((f32[32,1024]{1,0:T(8,128)S(1)}, f32[32,1024]{1,0:T(8,128)S(1)}, u32[]{:S(2)}, u32[]{:S(2)}) %collective-permute-start.17) | collective-permute-done | bytes 131104 | tf_op jit(solution)/shard_map/ppermute | solution.py:42
  63.7 2.8 %collective-permute-start.20 = (f32[32,1024]{1,0:T(8,128)S(1)}, f32[32,1024]{1,0:T(8,128)S(1)}, u32[]{:S(2)}, u32[]{:S(2)}) collective-permute-start(f32[32,1024]{1,0:T(8,128)S(1)} %get-tuple-element.20), channel_id=1, source_target_pairs={{0,4},{1,5},{2,6},{3,7},{4,0},{5,1},{6,2},{7,3},{8,12},{9,13},{10,... | collective-permute-start | bytes 393224 | tf_op jit(solution)/shard_map/ppermute | solution.py:42
  67.9 2.7 %collective-permute-done.18 = f32[32,1024]{1,0:T(8,128)S(1)} collective-permute-done((f32[32,1024]{1,0:T(8,128)S(1)}, f32[32,1024]{1,0:T(8,128)S(1)}, u32[]{:S(2)}, u32[]{:S(2)}) %collective-permute-start.18) | collective-permute-done | bytes 131104 | tf_op jit(solution)/shard_map/ppermute | solution.py:42
  75.1 2.6 %collective-permute-done.24 = f32[32,1024]{1,0:T(8,128)S(1)} collective-permute-done((f32[32,1024]{1,0:T(8,128)S(1)}, f32[32,1024]{1,0:T(8,128)S(1)}, u32[]{:S(2)}, u32[]{:S(2)}) %collective-permute-start.24) | collective-permute-done | bytes 131104 | tf_op jit(solution)/shard_map/ppermute | solution.py:42
  77.7 1.9 %collective-permute-done.23 = f32[32,1024]{1,0:T(8,128)S(1)} collective-permute-done((f32[32,1024]{1,0:T(8,128)S(1)}, f32[32,1024]{1,0:T(8,128)S(1)}, u32[]{:S(2)}, u32[]{:S(2)}) %collective-permute-start.23) | collective-permute-done | bytes 131104 | tf_op jit(solution)/shard_map/ppermute | solution.py:42
  79.8 1.9 %collective-permute-done.26.refs_9_ = f32[4,32,1024]{2,1,0:T(8,128)S(1)} collective-permute-done((f32[4,32,1024]{2,1,0:T(8,128)S(1)}, f32[4,32,1024]{2,1,0:T(8,128)S(1)}, u32[]{:S(2)}, u32[]{:S(2)}) %collective-permute-start.26) | collective-permute-done | bytes 524320 | tf_op jit(solution)/shard_map/ppermute | solution.py:42
  81.7 17.4 %product.3 = (f32[4,32,1024]{2,1,0:T(8,128)S(1)}, f32[4,32,1024]{2,1,0:T(8,128)S(1)}, f32[4,32,1024]{2,1,0:T(8,128)S(1)}, f32[4,32,1024]{2,1,0:T(8,128)S(1)}) custom-call(s32[33,2]{1,0:T(8,128)S(1)} %copy.7.plan, f32[33,512,512]{2,1,0:T(8,128)} %tiles.3, f32[1,32,1024]{2,1,0:T(8,128)S(1)} %bitcast.81, f32[1,32,1024]{2,1,0:T(8,128)S(1)} %bitcast.87, ...), custom_call_target="tpu_custom_call" | custom-call | flops 3321888768 | bytes 34603008 | tf_op jit(solution)/shard_map/product/pallas_call | solution.py:188
  103.0 1.6 %collective-permute-start.33 = (f32[32,1024]{1,0:T(8,128)S(1)}, f32[32,1024]{1,0:T(8,128)S(1)}, u32[]{:S(2)}, u32[]{:S(2)}) collective-permute-start(f32[32,1024]{1,0:T(8,128)S(1)} %get-tuple-element.27), channel_id=1, source_target_pairs={{0,4},{1,5},{2,6},{3,7},{4,0},{5,1},{6,2},{7,3},{8,12},{9,13},{10,... | collective-permute-start | bytes 393224 | tf_op jit(solution)/shard_map/ppermute | solution.py:42
  106.7 1.8 %collective-permute-done.32 = f32[32,1024]{1,0:T(8,128)S(1)} collective-permute-done((f32[32,1024]{1,0:T(8,128)S(1)}, f32[32,1024]{1,0:T(8,128)S(1)}, u32[]{:S(2)}, u32[]{:S(2)}) %collective-permute-start.32) | collective-permute-done | bytes 131104 | tf_op jit(solution)/shard_map/ppermute | solution.py:42
  108.5 2.9 %collective-permute-done.34 = f32[32,1024]{1,0:T(8,128)S(1)} collective-permute-done((f32[32,1024]{1,0:T(8,128)S(1)}, f32[32,1024]{1,0:T(8,128)S(1)}, u32[]{:S(2)}, u32[]{:S(2)}) %collective-permute-start.34) | collective-permute-done | bytes 131104 | tf_op jit(solution)/shard_map/ppermute | solution.py:42
  112.5 3.0 %collective-permute-done.28 = f32[32,1024]{1,0:T(8,128)S(1)} collective-permute-done((f32[32,1024]{1,0:T(8,128)S(1)}, f32[32,1024]{1,0:T(8,128)S(1)}, u32[]{:S(2)}, u32[]{:S(2)}) %collective-permute-start.28) | collective-permute-done | bytes 131104 | tf_op jit(solution)/shard_map/ppermute | solution.py:42
  116.0 2.0 %collective-permute-done.29 = f32[32,1024]{1,0:T(8,128)S(1)} collective-permute-done((f32[32,1024]{1,0:T(8,128)S(1)}, f32[32,1024]{1,0:T(8,128)S(1)}, u32[]{:S(2)}, u32[]{:S(2)}) %collective-permute-start.29) | collective-permute-done | bytes 131104 | tf_op jit(solution)/shard_map/ppermute | solution.py:42
  118.0 2.0 %collective-permute-done.35 = f32[32,1024]{1,0:T(8,128)S(1)} collective-permute-done((f32[32,1024]{1,0:T(8,128)S(1)}, f32[32,1024]{1,0:T(8,128)S(1)}, u32[]{:S(2)}, u32[]{:S(2)}) %collective-permute-start.35) | collective-permute-done | bytes 131104 | tf_op jit(solution)/shard_map/ppermute | solution.py:42
  (74 shorter events, 34.1 us)
Async XLA Ops:
  1.7 10.5 %collective-permute-start = (f32[32,1024]{1,0:T(8,128)S(1)}, f32[32,1024]{1,0:T(8,128)S(1)}, u32[]{:S(2)}, u32[]{:S(2)}) collective-permute-start(f32[32,1024]{1,0:T(8,128)S(1)} %sub.12), channel_id=1, source_target_pairs={{0,8},{1,9},{2,10},{3,11},{4,12},{5,13},{6,14},{7,15},{8,0},{9,1},... | collective-permute-start | bytes 393224 | tf_op jit(solution)/shard_map/ppermute | solution.py:42
  5.8 9.4 %collective-permute-start.2 = (f32[32,1024]{1,0:T(8,128)S(1)}, f32[32,1024]{1,0:T(8,128)S(1)}, u32[]{:S(2)}, u32[]{:S(2)}) collective-permute-start(f32[32,1024]{1,0:T(8,128)S(1)} %sub.12), channel_id=1, source_target_pairs={{0,4},{1,5},{2,6},{3,7},{4,0},{5,1},{6,2},{7,3},{8,12},{9,13},{10,... | collective-permute-start | bytes 393224 | tf_op jit(solution)/shard_map/ppermute | solution.py:42
  7.4 8.3 %collective-permute-start.1 = (f32[32,1024]{1,0:T(8,128)S(1)}, f32[32,1024]{1,0:T(8,128)S(1)}, u32[]{:S(2)}, u32[]{:S(2)}) collective-permute-start(f32[32,1024]{1,0:T(8,128)S(1)} %sub.12), channel_id=1, source_target_pairs={{0,2},{1,3},{2,0},{3,1},{4,6},{5,7},{6,4},{7,5},{8,10},{9,11},{10,... | collective-permute-start | bytes 393224 | tf_op jit(solution)/shard_map/ppermute | solution.py:42
  8.9 8.3 %collective-permute-start.3 = (f32[32,1024]{1,0:T(8,128)S(1)}, f32[32,1024]{1,0:T(8,128)S(1)}, u32[]{:S(2)}, u32[]{:S(2)}) collective-permute-start(f32[32,1024]{1,0:T(8,128)S(1)} %sub.12), channel_id=1, source_target_pairs={{0,6},{1,7},{2,4},{3,5},{4,2},{5,3},{6,0},{7,1},{8,14},{9,15},{10,... | collective-permute-start | bytes 393224 | tf_op jit(solution)/shard_map/ppermute | solution.py:42
  12.2 7.7 %collective-permute-start.6 = (f32[32,1024]{1,0:T(8,128)S(1)}, f32[32,1024]{1,0:T(8,128)S(1)}, u32[]{:S(2)}, u32[]{:S(2)}) collective-permute-start(f32[32,1024]{1,0:T(8,128)S(1)} %collective-permute-done), channel_id=1, source_target_pairs={{0,6},{1,7},{2,4},{3,5},{4,2},{5,3},{6,0},{7,1},{8,14},{9,15},{10,... | collective-permute-start | bytes 393224 | tf_op jit(solution)/shard_map/ppermute | solution.py:42
  15.7 7.7 %collective-permute-start.7 = (f32[4,32,1024]{2,1,0:T(8,128)S(1)}, f32[4,32,1024]{2,1,0:T(8,128)S(1)}, u32[]{:S(2)}, u32[]{:S(2)}) collective-permute-start(f32[4,32,1024]{2,1,0:T(8,128)S(1)} %pad_maximum_fusion), channel_id=1, source_target_pairs={{0,1},{1,0},{2,3},{3,2},{4,5},{5,4},{6,7},{7,6},{8,9},{9,8},{10,11... | collective-permute-start | bytes 1572872 | tf_op jit(solution)/shard_map/ppermute | solution.py:42
  44.2 7.3 %collective-permute-start.14 = (f32[32,1024]{1,0:T(8,128)S(1)}, f32[32,1024]{1,0:T(8,128)S(1)}, u32[]{:S(2)}, u32[]{:S(2)}) collective-permute-start(f32[32,1024]{1,0:T(8,128)S(1)} %get-tuple-element.31), channel_id=1, source_target_pairs={{0,6},{1,7},{2,4},{3,5},{4,2},{5,3},{6,0},{7,1},{8,14},{9,15},{10,... | collective-permute-start | bytes 393224 | tf_op jit(solution)/shard_map/ppermute | solution.py:42
  45.7 8.8 %collective-permute-start.16 = (f32[32,1024]{1,0:T(8,128)S(1)}, f32[32,1024]{1,0:T(8,128)S(1)}, u32[]{:S(2)}, u32[]{:S(2)}) collective-permute-start(f32[32,1024]{1,0:T(8,128)S(1)} %get-tuple-element.32), channel_id=1, source_target_pairs={{0,2},{1,3},{2,0},{3,1},{4,6},{5,7},{6,4},{7,5},{8,10},{9,11},{10,... | collective-permute-start | bytes 393224 | tf_op jit(solution)/shard_map/ppermute | solution.py:42
  47.2 7.3 %collective-permute-start.15 = (f32[32,1024]{1,0:T(8,128)S(1)}, f32[32,1024]{1,0:T(8,128)S(1)}, u32[]{:S(2)}, u32[]{:S(2)}) collective-permute-start(f32[32,1024]{1,0:T(8,128)S(1)} %get-tuple-element.33), channel_id=1, source_target_pairs={{0,4},{1,5},{2,6},{3,7},{4,0},{5,1},{6,2},{7,3},{8,12},{9,13},{10,... | collective-permute-start | bytes 393224 | tf_op jit(solution)/shard_map/ppermute | solution.py:42
  47.9 9.3 %collective-permute-start.10 = (f32[32,1024]{1,0:T(8,128)S(1)}, f32[32,1024]{1,0:T(8,128)S(1)}, u32[]{:S(2)}, u32[]{:S(2)}) collective-permute-start(f32[32,1024]{1,0:T(8,128)S(1)} %get-tuple-element.28), channel_id=1, source_target_pairs={{0,6},{1,7},{2,4},{3,5},{4,2},{5,3},{6,0},{7,1},{8,14},{9,15},{10,... | collective-permute-start | bytes 393224 | tf_op jit(solution)/shard_map/ppermute | solution.py:42
  49.4 9.8 %collective-permute-start.12 = (f32[32,1024]{1,0:T(8,128)S(1)}, f32[32,1024]{1,0:T(8,128)S(1)}, u32[]{:S(2)}, u32[]{:S(2)}) collective-permute-start(f32[32,1024]{1,0:T(8,128)S(1)} %get-tuple-element.29), channel_id=1, source_target_pairs={{0,2},{1,3},{2,0},{3,1},{4,6},{5,7},{6,4},{7,5},{8,10},{9,11},{10,... | collective-permute-start | bytes 393224 | tf_op jit(solution)/shard_map/ppermute | solution.py:42
  51.6 7.8 %collective-permute-start.11 = (f32[32,1024]{1,0:T(8,128)S(1)}, f32[32,1024]{1,0:T(8,128)S(1)}, u32[]{:S(2)}, u32[]{:S(2)}) collective-permute-start(f32[32,1024]{1,0:T(8,128)S(1)} %get-tuple-element.30), channel_id=1, source_target_pairs={{0,4},{1,5},{2,6},{3,7},{4,0},{5,1},{6,2},{7,3},{8,12},{9,13},{10,... | collective-permute-start | bytes 393224 | tf_op jit(solution)/shard_map/ppermute | solution.py:42
  54.5 9.0 %collective-permute-start.17 = (f32[32,1024]{1,0:T(8,128)S(1)}, f32[32,1024]{1,0:T(8,128)S(1)}, u32[]{:S(2)}, u32[]{:S(2)}) collective-permute-start(f32[32,1024]{1,0:T(8,128)S(1)} %fusion.10), channel_id=1, source_target_pairs={{0,8},{1,9},{2,10},{3,11},{4,12},{5,13},{6,14},{7,15},{8,0},{9,1},... | collective-permute-start | bytes 393224 | tf_op jit(solution)/shard_map/ppermute | solution.py:42
  63.7 9.4 %collective-permute-start.20 = (f32[32,1024]{1,0:T(8,128)S(1)}, f32[32,1024]{1,0:T(8,128)S(1)}, u32[]{:S(2)}, u32[]{:S(2)}) collective-permute-start(f32[32,1024]{1,0:T(8,128)S(1)} %get-tuple-element.20), channel_id=1, source_target_pairs={{0,4},{1,5},{2,6},{3,7},{4,0},{5,1},{6,2},{7,3},{8,12},{9,13},{10,... | collective-permute-start | bytes 393224 | tf_op jit(solution)/shard_map/ppermute | solution.py:42
  66.4 7.7 %collective-permute-start.19 = (f32[32,1024]{1,0:T(8,128)S(1)}, f32[32,1024]{1,0:T(8,128)S(1)}, u32[]{:S(2)}, u32[]{:S(2)}) collective-permute-start(f32[32,1024]{1,0:T(8,128)S(1)} %get-tuple-element.20), channel_id=1, source_target_pairs={{0,2},{1,3},{2,0},{3,1},{4,6},{5,7},{6,4},{7,5},{8,10},{9,11},{10,... | collective-permute-start | bytes 393224 | tf_op jit(solution)/shard_map/ppermute | solution.py:42
  67.8 7.3 %collective-permute-start.21 = (f32[32,1024]{1,0:T(8,128)S(1)}, f32[32,1024]{1,0:T(8,128)S(1)}, u32[]{:S(2)}, u32[]{:S(2)}) collective-permute-start(f32[32,1024]{1,0:T(8,128)S(1)} %get-tuple-element.20), channel_id=1, source_target_pairs={{0,6},{1,7},{2,4},{3,5},{4,2},{5,3},{6,0},{7,1},{8,14},{9,15},{10,... | collective-permute-start | bytes 393224 | tf_op jit(solution)/shard_map/ppermute | solution.py:42
  71.6 8.0 %collective-permute-start.23 = (f32[32,1024]{1,0:T(8,128)S(1)}, f32[32,1024]{1,0:T(8,128)S(1)}, u32[]{:S(2)}, u32[]{:S(2)}) collective-permute-start(f32[32,1024]{1,0:T(8,128)S(1)} %collective-permute-done.18), channel_id=1, source_target_pairs={{0,4},{1,5},{2,6},{3,7},{4,0},{5,1},{6,2},{7,3},{8,12},{9,13},{10,... | collective-permute-start | bytes 393224 | tf_op jit(solution)/shard_map/ppermute | solution.py:42
  101.1 7.3 %collective-permute-start.32 = (f32[32,1024]{1,0:T(8,128)S(1)}, f32[32,1024]{1,0:T(8,128)S(1)}, u32[]{:S(2)}, u32[]{:S(2)}) collective-permute-start(f32[32,1024]{1,0:T(8,128)S(1)} %get-tuple-element.25), channel_id=1, source_target_pairs={{0,6},{1,7},{2,4},{3,5},{4,2},{5,3},{6,0},{7,1},{8,14},{9,15},{10,... | collective-permute-start | bytes 393224 | tf_op jit(solution)/shard_map/ppermute | solution.py:42
  102.3 9.1 %collective-permute-start.34 = (f32[32,1024]{1,0:T(8,128)S(1)}, f32[32,1024]{1,0:T(8,128)S(1)}, u32[]{:S(2)}, u32[]{:S(2)}) collective-permute-start(f32[32,1024]{1,0:T(8,128)S(1)} %get-tuple-element.26), channel_id=1, source_target_pairs={{0,2},{1,3},{2,0},{3,1},{4,6},{5,7},{6,4},{7,5},{8,10},{9,11},{10,... | collective-permute-start | bytes 393224 | tf_op jit(solution)/shard_map/ppermute | solution.py:42
  103.0 8.3 %collective-permute-start.33 = (f32[32,1024]{1,0:T(8,128)S(1)}, f32[32,1024]{1,0:T(8,128)S(1)}, u32[]{:S(2)}, u32[]{:S(2)}) collective-permute-start(f32[32,1024]{1,0:T(8,128)S(1)} %get-tuple-element.27), channel_id=1, source_target_pairs={{0,4},{1,5},{2,6},{3,7},{4,0},{5,1},{6,2},{7,3},{8,12},{9,13},{10,... | collective-permute-start | bytes 393224 | tf_op jit(solution)/shard_map/ppermute | solution.py:42
  104.8 10.8 %collective-permute-start.28 = (f32[32,1024]{1,0:T(8,128)S(1)}, f32[32,1024]{1,0:T(8,128)S(1)}, u32[]{:S(2)}, u32[]{:S(2)}) collective-permute-start(f32[32,1024]{1,0:T(8,128)S(1)} %get-tuple-element.22), channel_id=1, source_target_pairs={{0,6},{1,7},{2,4},{3,5},{4,2},{5,3},{6,0},{7,1},{8,14},{9,15},{10,... | collective-permute-start | bytes 393224 | tf_op jit(solution)/shard_map/ppermute | solution.py:42
  105.9 10.0 %collective-permute-start.30 = (f32[32,1024]{1,0:T(8,128)S(1)}, f32[32,1024]{1,0:T(8,128)S(1)}, u32[]{:S(2)}, u32[]{:S(2)}) collective-permute-start(f32[32,1024]{1,0:T(8,128)S(1)} %get-tuple-element.23), channel_id=1, source_target_pairs={{0,2},{1,3},{2,0},{3,1},{4,6},{5,7},{6,4},{7,5},{8,10},{9,11},{10,... | collective-permute-start | bytes 393224 | tf_op jit(solution)/shard_map/ppermute | solution.py:42
  108.5 9.5 %collective-permute-start.29 = (f32[32,1024]{1,0:T(8,128)S(1)}, f32[32,1024]{1,0:T(8,128)S(1)}, u32[]{:S(2)}, u32[]{:S(2)}) collective-permute-start(f32[32,1024]{1,0:T(8,128)S(1)} %get-tuple-element.24), channel_id=1, source_target_pairs={{0,4},{1,5},{2,6},{3,7},{4,0},{5,1},{6,2},{7,3},{8,12},{9,13},{10,... | collective-permute-start | bytes 393224 | tf_op jit(solution)/shard_map/ppermute | solution.py:42
  111.4 8.6 %collective-permute-start.35 = (f32[32,1024]{1,0:T(8,128)S(1)}, f32[32,1024]{1,0:T(8,128)S(1)}, u32[]{:S(2)}, u32[]{:S(2)}) collective-permute-start(f32[32,1024]{1,0:T(8,128)S(1)} %fusion.2), channel_id=1, source_target_pairs={{0,8},{1,9},{2,10},{3,11},{4,12},{5,13},{6,14},{7,15},{8,0},{9,1},... | collective-permute-start | bytes 393224 | tf_op jit(solution)/shard_map/ppermute | solution.py:42
  (15 other events, 247.3 us)

commit v5 on v4

--- a/solution.py
+++ b/solution.py
@@ -22,13 +22,6 @@
 NEAR = (2, 4)
 
 
-def near_masks(count):
-    masks = [0]
-    for bit in NEAR:
-        masks += [m | bit for m in masks if bit < count]
-    return masks[1:]
-
-
 def far_bits(count):
     return [1 << i for i in range(1, count.bit_length() - 1) if 1 << i not in NEAR]
 
@@ -42,16 +35,22 @@
     return lax.ppermute(x, "col", [(i, i ^ mask) for i in range(count)])
 
 
-def gather(own):
+def gather(own, corner_at_once):
     count = lax.axis_size("col")
+    low, high = NEAR
     pieces = {0: own}
+    far = [0]
     for bit in reversed(far_bits(count)):
-        for p in list(pieces):
+        for p in list(far):
             pieces[p | bit] = swap(pieces[p], bit)
-    for p in sorted(pieces):
-        for mask in near_masks(count):
+            far.append(p | bit)
+    pieces[high] = swap(own, high)
+    pieces[low] = swap(own, low)
+    pieces[low | high] = swap(own, low | high) if corner_at_once else swap(pieces[high], low)
+    for p in sorted(far[1:]):
+        for mask in (high, low, low | high):
             pieces[p | mask] = swap(pieces[p], mask)
-    order = sorted(pieces, key=lambda p: p.bit_count())
+    order = sorted(pieces) if corner_at_once else sorted(pieces, key=lambda p: p.bit_count())
     arrays = [([p], pieces[p][None]) for p in order]
     for start in range(0, len(order), 4):
         some = order[start : start + 4]
@@ -61,13 +60,13 @@
 
 def scatter_sum(sums):
     count = lax.axis_size("col")
+    low, high = NEAR
     held = {}
     for group, kept, sent in zip(sum_groups(count), sums[::2], sums[1::2], strict=True):
         whole = kept + swap(sent, CORE)
         held |= {p: whole[j] for j, p in enumerate(group)}
-    masks = near_masks(count)
-    for p in sorted((p for p in held if not p & sum(NEAR)), reverse=True):
-        for mask in reversed(masks):
+    for p in sorted((p for p in held if not p & (low | high)), reverse=True):
+        for mask in (low | high, high, low):
             held[p] += swap(held.pop(p | mask), mask)
     for bit in far_bits(count):
         for p in sorted((p for p in held if p & bit), reverse=True):
@@ -145,7 +144,7 @@
         split_tile(ring[lax.rem(slot, depth)], ready)
 
     def multiply(slot, ready):
-        add_products(plan[slot, 0], plan[slot, 1], ready, err, acc)
+        add_products(plan[0, slot], plan[1, slot], ready, err, acc)
 
     for slot in range(min(depth, slots)):
         fetch(slot).start()
@@ -211,7 +210,7 @@
     weights = start_weight
     velocity = jnp.zeros(start_weight.shape, jnp.float32)
     for step in range(ITERS):
-        terms = product(tile_plan, hess_tiles, gather(weights - dense_weight))
+        terms = product(tile_plan.T, hess_tiles, gather(weights - dense_weight, step > 0))
         gradient = scatter_sum(terms)
         velocity = momentum * velocity + gradient
         weights = keep * (weights - step_size * velocity)

time: 121 us -> 119 us (0.983)
  waiting for transfers between devices: 44 us -> 35 us
  starting transfers between devices: 37.2 us -> 45.9 us
    ppermute x36, waiting for transfers between devices: 44 us -> 35 us  [swap(): return lax.ppermute(x, 'col', [(i, i ^ mask) for i in range(count)])]
    ppermute x36, starting transfers between devices: 37.2 us -> 45.9 us  [swap(): return lax.ppermute(x, 'col', [(i, i ^ mask) for i in range(count)])]
  transfers between devices with their start and end apart: 36 -> 36, of which waited for: 25 -> 23; matrix products, arithmetic and copies ran while one was open for 2% -> 0% of each run, Pallas kernels for 0% -> 0%
where the time goes in v5:
time: 119 us
  starting transfers between devices  45.9 us (39%)
  waiting for transfers between devices  35 us (29%)
  Pallas kernels  34.1 us (29%)
  other arithmetic  2.32 us (2%)
    ppermute x36, starting transfers between devices, swap(): return lax.ppermute(x, 'col', [(i, i ^ mask) for i in range(count)])  45.9 us
    ppermute x36, waiting for transfers between devices, swap(): return lax.ppermute(x, 'col', [(i, i ^ mask) for i in range(count)])  35 us
    pallas_call x2, Pallas kernels, product(): pl.pallas_call(functools.partial(product_kernel, held, width), in_specs=[...  34.1 us
  transfers between devices with their start and end apart: 36, of which 23 were waited for; matrix products, arithmetic and copies ran while one was open for 0% of the time, Pallas kernels for 0%

profile of v5, /device:TPU:0, one launch (start us, length us, event | category | flops | bytes accessed | tf_op | source)
XLA Modules:
  0.0 119.0 jit_solution(7614378003095651826)
XLA Ops:
  1.7 3.1 %collective-permute-start.1 = (f32[32,1024]{1,0:T(8,128)S(1)}, f32[32,1024]{1,0:T(8,128)S(1)}, u32[]{:S(2)}, u32[]{:S(2)}) collective-permute-start(f32[32,1024]{1,0:T(8,128)S(1)} %sub.12), channel_id=1, source_target_pairs={{0,4},{1,5},{2,6},{3,7},{4,0},{5,1},{6,2},{7,3},{8,12},{9,13},{10,... | collective-permute-start | bytes 393224 | tf_op jit(solution)/shard_map/ppermute | solution.py:35
  4.8 2.6 %collective-permute-start = (f32[32,1024]{1,0:T(8,128)S(1)}, f32[32,1024]{1,0:T(8,128)S(1)}, u32[]{:S(2)}, u32[]{:S(2)}) collective-permute-start(f32[32,1024]{1,0:T(8,128)S(1)} %sub.12), channel_id=1, source_target_pairs={{0,8},{1,9},{2,10},{3,11},{4,12},{5,13},{6,14},{7,15},{8,0},{9,1},... | collective-permute-start | bytes 393224 | tf_op jit(solution)/shard_map/ppermute | solution.py:35
  10.1 1.8 %collective-permute-start.3 = (f32[32,1024]{1,0:T(8,128)S(1)}, f32[32,1024]{1,0:T(8,128)S(1)}, u32[]{:S(2)}, u32[]{:S(2)}) collective-permute-start(f32[32,1024]{1,0:T(8,128)S(1)} %collective-permute-done.1), channel_id=1, source_target_pairs={{0,2},{1,3},{2,0},{3,1},{4,6},{5,7},{6,4},{7,5},{8,10},{9,11},{10,... | collective-permute-start | bytes 393224 | tf_op jit(solution)/shard_map/ppermute | solution.py:35
  17.1 3.0 %collective-permute-done.6 = f32[32,1024]{1,0:T(8,128)S(1)} collective-permute-done((f32[32,1024]{1,0:T(8,128)S(1)}, f32[32,1024]{1,0:T(8,128)S(1)}, u32[]{:S(2)}, u32[]{:S(2)}) %collective-permute-start.6) | collective-permute-done | bytes 131104 | tf_op jit(solution)/shard_map/ppermute | solution.py:35
  21.1 1.9 %collective-permute-done.8.refs_9_ = f32[4,32,1024]{2,1,0:T(8,128)S(1)} collective-permute-done((f32[4,32,1024]{2,1,0:T(8,128)S(1)}, f32[4,32,1024]{2,1,0:T(8,128)S(1)}, u32[]{:S(2)}, u32[]{:S(2)}) %collective-permute-start.8) | collective-permute-done | bytes 524320 | tf_op jit(solution)/shard_map/ppermute | solution.py:35
  23.7 17.0 %product.2 = (f32[4,32,1024]{2,1,0:T(8,128)S(1)}, f32[4,32,1024]{2,1,0:T(8,128)S(1)}, f32[4,32,1024]{2,1,0:T(8,128)S(1)}, f32[4,32,1024]{2,1,0:T(8,128)S(1)}) custom-call(s32[2,33]{1,0:T(2,128)S(1)} %bitcast.113, f32[33,512,512]{2,1,0:T(8,128)} %tiles.3, f32[1,32,1024]{2,1,0:T(8,128)S(1)} %bitcast.84, f32[1,32,1024]{2,1,0:T(8,128)S(1)} %bitcast.90, ...), custom_call_target="tpu_custom_call" | custom-call | flops 3321888768 | bytes 34603008 | tf_op jit(solution)/shard_map/product/pallas_call | solution.py:187
  42.8 2.0 %collective-permute-start.14 = (f32[32,1024]{1,0:T(8,128)S(1)}, f32[32,1024]{1,0:T(8,128)S(1)}, u32[]{:S(2)}, u32[]{:S(2)}) collective-permute-start(f32[32,1024]{1,0:T(8,128)S(1)} %get-tuple-element.31), channel_id=1, source_target_pairs={{0,6},{1,7},{2,4},{3,5},{4,2},{5,3},{6,0},{7,1},{8,14},{9,15},{10,... | collective-permute-start | bytes 393224 | tf_op jit(solution)/shard_map/ppermute | solution.py:35
  46.5 2.0 %collective-permute-start.10 = (f32[32,1024]{1,0:T(8,128)S(1)}, f32[32,1024]{1,0:T(8,128)S(1)}, u32[]{:S(2)}, u32[]{:S(2)}) collective-permute-start(f32[32,1024]{1,0:T(8,128)S(1)} %get-tuple-element.28), channel_id=1, source_target_pairs={{0,6},{1,7},{2,4},{3,5},{4,2},{5,3},{6,0},{7,1},{8,14},{9,15},{10,... | collective-permute-start | bytes 393224 | tf_op jit(solution)/shard_map/ppermute | solution.py:35
  51.2 1.9 %collective-permute-done.16 = f32[32,1024]{1,0:T(8,128)S(1)} collective-permute-done((f32[32,1024]{1,0:T(8,128)S(1)}, f32[32,1024]{1,0:T(8,128)S(1)}, u32[]{:S(2)}, u32[]{:S(2)}) %collective-permute-start.16) | collective-permute-done | bytes 131104 | tf_op jit(solution)/shard_map/ppermute | solution.py:35
  53.1 2.6 %collective-permute-start.17 = (f32[32,1024]{1,0:T(8,128)S(1)}, f32[32,1024]{1,0:T(8,128)S(1)}, u32[]{:S(2)}, u32[]{:S(2)}) collective-permute-start(f32[32,1024]{1,0:T(8,128)S(1)} %fusion.10), channel_id=1, source_target_pairs={{0,8},{1,9},{2,10},{3,11},{4,12},{5,13},{6,14},{7,15},{8,0},{9,1},... | collective-permute-start | bytes 393224 | tf_op jit(solution)/shard_map/ppermute | solution.py:35
  55.8 2.0 %collective-permute-done.12 = f32[32,1024]{1,0:T(8,128)S(1)} collective-permute-done((f32[32,1024]{1,0:T(8,128)S(1)}, f32[32,1024]{1,0:T(8,128)S(1)}, u32[]{:S(2)}, u32[]{:S(2)}) %collective-permute-start.12) | collective-permute-done | bytes 131104 | tf_op jit(solution)/shard_map/ppermute | solution.py:35
  57.8 2.6 %collective-permute-done.11 = f32[32,1024]{1,0:T(8,128)S(1)} collective-permute-done((f32[32,1024]{1,0:T(8,128)S(1)}, f32[32,1024]{1,0:T(8,128)S(1)}, u32[]{:S(2)}, u32[]{:S(2)}) %collective-permute-start.11) | collective-permute-done | bytes 131104 | tf_op jit(solution)/shard_map/ppermute | solution.py:35
  60.4 2.4 %collective-permute-start.21 = (f32[32,1024]{1,0:T(8,128)S(1)}, f32[32,1024]{1,0:T(8,128)S(1)}, u32[]{:S(2)}, u32[]{:S(2)}) collective-permute-start(f32[32,1024]{1,0:T(8,128)S(1)} %get-tuple-element.20), channel_id=1, source_target_pairs={{0,8},{1,9},{2,10},{3,11},{4,12},{5,13},{6,14},{7,15},{8,0},{9,1},... | collective-permute-start | bytes 393224 | tf_op jit(solution)/shard_map/ppermute | solution.py:35
  62.8 2.7 %collective-permute-start.20 = (f32[32,1024]{1,0:T(8,128)S(1)}, f32[32,1024]{1,0:T(8,128)S(1)}, u32[]{:S(2)}, u32[]{:S(2)}) collective-permute-start(f32[32,1024]{1,0:T(8,128)S(1)} %get-tuple-element.20), channel_id=1, source_target_pairs={{0,6},{1,7},{2,4},{3,5},{4,2},{5,3},{6,0},{7,1},{8,14},{9,15},{10,... | collective-permute-start | bytes 393224 | tf_op jit(solution)/shard_map/ppermute | solution.py:35
  73.8 2.9 %collective-permute-done.24 = f32[32,1024]{1,0:T(8,128)S(1)} collective-permute-done((f32[32,1024]{1,0:T(8,128)S(1)}, f32[32,1024]{1,0:T(8,128)S(1)}, u32[]{:S(2)}, u32[]{:S(2)}) %collective-permute-start.24) | collective-permute-done | bytes 131104 | tf_op jit(solution)/shard_map/ppermute | solution.py:35
  77.9 1.9 %collective-permute-done.26.refs_9_ = f32[4,32,1024]{2,1,0:T(8,128)S(1)} collective-permute-done((f32[4,32,1024]{2,1,0:T(8,128)S(1)}, f32[4,32,1024]{2,1,0:T(8,128)S(1)}, u32[]{:S(2)}, u32[]{:S(2)}) %collective-permute-start.26) | collective-permute-done | bytes 524320 | tf_op jit(solution)/shard_map/ppermute | solution.py:35
  79.8 17.0 %product.3 = (f32[4,32,1024]{2,1,0:T(8,128)S(1)}, f32[4,32,1024]{2,1,0:T(8,128)S(1)}, f32[4,32,1024]{2,1,0:T(8,128)S(1)}, f32[4,32,1024]{2,1,0:T(8,128)S(1)}) custom-call(s32[2,33]{1,0:T(2,128)S(1)} %bitcast.114, f32[33,512,512]{2,1,0:T(8,128)} %tiles.3, f32[1,32,1024]{2,1,0:T(8,128)S(1)} %bitcast.82, f32[1,32,1024]{2,1,0:T(8,128)S(1)} %bitcast.98, ...), custom_call_target="tpu_custom_call" | custom-call | flops 3321888768 | bytes 34603008 | tf_op jit(solution)/shard_map/product/pallas_call | solution.py:187
  98.9 2.0 %collective-permute-start.32 = (f32[32,1024]{1,0:T(8,128)S(1)}, f32[32,1024]{1,0:T(8,128)S(1)}, u32[]{:S(2)}, u32[]{:S(2)}) collective-permute-start(f32[32,1024]{1,0:T(8,128)S(1)} %get-tuple-element.25), channel_id=1, source_target_pairs={{0,6},{1,7},{2,4},{3,5},{4,2},{5,3},{6,0},{7,1},{8,14},{9,15},{10,... | collective-permute-start | bytes 393224 | tf_op jit(solution)/shard_map/ppermute | solution.py:35
  102.6 2.0 %collective-permute-start.28 = (f32[32,1024]{1,0:T(8,128)S(1)}, f32[32,1024]{1,0:T(8,128)S(1)}, u32[]{:S(2)}, u32[]{:S(2)}) collective-permute-start(f32[32,1024]{1,0:T(8,128)S(1)} %get-tuple-element.22), channel_id=1, source_target_pairs={{0,6},{1,7},{2,4},{3,5},{4,2},{5,3},{6,0},{7,1},{8,14},{9,15},{10,... | collective-permute-start | bytes 393224 | tf_op jit(solution)/shard_map/ppermute | solution.py:35
  106.2 1.9 %collective-permute-start.29 = (f32[32,1024]{1,0:T(8,128)S(1)}, f32[32,1024]{1,0:T(8,128)S(1)}, u32[]{:S(2)}, u32[]{:S(2)}) collective-permute-start(f32[32,1024]{1,0:T(8,128)S(1)} %get-tuple-element.24), channel_id=1, source_target_pairs={{0,4},{1,5},{2,6},{3,7},{4,0},{5,1},{6,2},{7,3},{8,12},{9,13},{10,... | collective-permute-start | bytes 393224 | tf_op jit(solution)/shard_map/ppermute | solution.py:35
  109.2 2.4 %collective-permute-start.35 = (f32[32,1024]{1,0:T(8,128)S(1)}, f32[32,1024]{1,0:T(8,128)S(1)}, u32[]{:S(2)}, u32[]{:S(2)}) collective-permute-start(f32[32,1024]{1,0:T(8,128)S(1)} %fusion.2), channel_id=1, source_target_pairs={{0,8},{1,9},{2,10},{3,11},{4,12},{5,13},{6,14},{7,15},{8,0},{9,1},... | collective-permute-start | bytes 393224 | tf_op jit(solution)/shard_map/ppermute | solution.py:35
  111.9 2.0 %collective-permute-done.30 = f32[32,1024]{1,0:T(8,128)S(1)} collective-permute-done((f32[32,1024]{1,0:T(8,128)S(1)}, f32[32,1024]{1,0:T(8,128)S(1)}, u32[]{:S(2)}, u32[]{:S(2)}) %collective-permute-start.30) | collective-permute-done | bytes 131104 | tf_op jit(solution)/shard_map/ppermute | solution.py:35
  113.9 2.3 %collective-permute-done.29 = f32[32,1024]{1,0:T(8,128)S(1)} collective-permute-done((f32[32,1024]{1,0:T(8,128)S(1)}, f32[32,1024]{1,0:T(8,128)S(1)}, u32[]{:S(2)}, u32[]{:S(2)}) %collective-permute-start.29) | collective-permute-done | bytes 131104 | tf_op jit(solution)/shard_map/ppermute | solution.py:35
  116.2 2.1 %collective-permute-done.35 = f32[32,1024]{1,0:T(8,128)S(1)} collective-permute-done((f32[32,1024]{1,0:T(8,128)S(1)}, f32[32,1024]{1,0:T(8,128)S(1)}, u32[]{:S(2)}, u32[]{:S(2)}) %collective-permute-start.35) | collective-permute-done | bytes 131104 | tf_op jit(solution)/shard_map/ppermute | solution.py:35
  (75 shorter events, 34.0 us)
Async XLA Ops:
  1.7 8.4 %collective-permute-start.1 = (f32[32,1024]{1,0:T(8,128)S(1)}, f32[32,1024]{1,0:T(8,128)S(1)}, u32[]{:S(2)}, u32[]{:S(2)}) collective-permute-start(f32[32,1024]{1,0:T(8,128)S(1)} %sub.12), channel_id=1, source_target_pairs={{0,4},{1,5},{2,6},{3,7},{4,0},{5,1},{6,2},{7,3},{8,12},{9,13},{10,... | collective-permute-start | bytes 393224 | tf_op jit(solution)/shard_map/ppermute | solution.py:35
  4.8 8.7 %collective-permute-start = (f32[32,1024]{1,0:T(8,128)S(1)}, f32[32,1024]{1,0:T(8,128)S(1)}, u32[]{:S(2)}, u32[]{:S(2)}) collective-permute-start(f32[32,1024]{1,0:T(8,128)S(1)} %sub.12), channel_id=1, source_target_pairs={{0,8},{1,9},{2,10},{3,11},{4,12},{5,13},{6,14},{7,15},{8,0},{9,1},... | collective-permute-start | bytes 393224 | tf_op jit(solution)/shard_map/ppermute | solution.py:35
  7.4 9.6 %collective-permute-start.2 = (f32[32,1024]{1,0:T(8,128)S(1)}, f32[32,1024]{1,0:T(8,128)S(1)}, u32[]{:S(2)}, u32[]{:S(2)}) collective-permute-start(f32[32,1024]{1,0:T(8,128)S(1)} %sub.12), channel_id=1, source_target_pairs={{0,2},{1,3},{2,0},{3,1},{4,6},{5,7},{6,4},{7,5},{8,10},{9,11},{10,... | collective-permute-start | bytes 393224 | tf_op jit(solution)/shard_map/ppermute | solution.py:35
  10.1 7.0 %collective-permute-start.3 = (f32[32,1024]{1,0:T(8,128)S(1)}, f32[32,1024]{1,0:T(8,128)S(1)}, u32[]{:S(2)}, u32[]{:S(2)}) collective-permute-start(f32[32,1024]{1,0:T(8,128)S(1)} %collective-permute-done.1), channel_id=1, source_target_pairs={{0,2},{1,3},{2,0},{3,1},{4,6},{5,7},{6,4},{7,5},{8,10},{9,11},{10,... | collective-permute-start | bytes 393224 | tf_op jit(solution)/shard_map/ppermute | solution.py:35
  42.8 7.3 %collective-permute-start.14 = (f32[32,1024]{1,0:T(8,128)S(1)}, f32[32,1024]{1,0:T(8,128)S(1)}, u32[]{:S(2)}, u32[]{:S(2)}) collective-permute-start(f32[32,1024]{1,0:T(8,128)S(1)} %get-tuple-element.31), channel_id=1, source_target_pairs={{0,6},{1,7},{2,4},{3,5},{4,2},{5,3},{6,0},{7,1},{8,14},{9,15},{10,... | collective-permute-start | bytes 393224 | tf_op jit(solution)/shard_map/ppermute | solution.py:35
  44.8 8.2 %collective-permute-start.16 = (f32[32,1024]{1,0:T(8,128)S(1)}, f32[32,1024]{1,0:T(8,128)S(1)}, u32[]{:S(2)}, u32[]{:S(2)}) collective-permute-start(f32[32,1024]{1,0:T(8,128)S(1)} %get-tuple-element.32), channel_id=1, source_target_pairs={{0,2},{1,3},{2,0},{3,1},{4,6},{5,7},{6,4},{7,5},{8,10},{9,11},{10,... | collective-permute-start | bytes 393224 | tf_op jit(solution)/shard_map/ppermute | solution.py:35
  45.4 7.7 %collective-permute-start.15 = (f32[32,1024]{1,0:T(8,128)S(1)}, f32[32,1024]{1,0:T(8,128)S(1)}, u32[]{:S(2)}, u32[]{:S(2)}) collective-permute-start(f32[32,1024]{1,0:T(8,128)S(1)} %get-tuple-element.33), channel_id=1, source_target_pairs={{0,4},{1,5},{2,6},{3,7},{4,0},{5,1},{6,2},{7,3},{8,12},{9,13},{10,... | collective-permute-start | bytes 393224 | tf_op jit(solution)/shard_map/ppermute | solution.py:35
  46.5 9.3 %collective-permute-start.10 = (f32[32,1024]{1,0:T(8,128)S(1)}, f32[32,1024]{1,0:T(8,128)S(1)}, u32[]{:S(2)}, u32[]{:S(2)}) collective-permute-start(f32[32,1024]{1,0:T(8,128)S(1)} %get-tuple-element.28), channel_id=1, source_target_pairs={{0,6},{1,7},{2,4},{3,5},{4,2},{5,3},{6,0},{7,1},{8,14},{9,15},{10,... | collective-permute-start | bytes 393224 | tf_op jit(solution)/shard_map/ppermute | solution.py:35
  48.5 9.3 %collective-permute-start.12 = (f32[32,1024]{1,0:T(8,128)S(1)}, f32[32,1024]{1,0:T(8,128)S(1)}, u32[]{:S(2)}, u32[]{:S(2)}) collective-permute-start(f32[32,1024]{1,0:T(8,128)S(1)} %get-tuple-element.29), channel_id=1, source_target_pairs={{0,2},{1,3},{2,0},{3,1},{4,6},{5,7},{6,4},{7,5},{8,10},{9,11},{10,... | collective-permute-start | bytes 393224 | tf_op jit(solution)/shard_map/ppermute | solution.py:35
  50.1 10.2 %collective-permute-start.11 = (f32[32,1024]{1,0:T(8,128)S(1)}, f32[32,1024]{1,0:T(8,128)S(1)}, u32[]{:S(2)}, u32[]{:S(2)}) collective-permute-start(f32[32,1024]{1,0:T(8,128)S(1)} %get-tuple-element.30), channel_id=1, source_target_pairs={{0,4},{1,5},{2,6},{3,7},{4,0},{5,1},{6,2},{7,3},{8,12},{9,13},{10,... | collective-permute-start | bytes 393224 | tf_op jit(solution)/shard_map/ppermute | solution.py:35
  53.1 7.2 %collective-permute-start.17 = (f32[32,1024]{1,0:T(8,128)S(1)}, f32[32,1024]{1,0:T(8,128)S(1)}, u32[]{:S(2)}, u32[]{:S(2)}) collective-permute-start(f32[32,1024]{1,0:T(8,128)S(1)} %fusion.10), channel_id=1, source_target_pairs={{0,8},{1,9},{2,10},{3,11},{4,12},{5,13},{6,14},{7,15},{8,0},{9,1},... | collective-permute-start | bytes 393224 | tf_op jit(solution)/shard_map/ppermute | solution.py:35
  60.4 8.1 %collective-permute-start.21 = (f32[32,1024]{1,0:T(8,128)S(1)}, f32[32,1024]{1,0:T(8,128)S(1)}, u32[]{:S(2)}, u32[]{:S(2)}) collective-permute-start(f32[32,1024]{1,0:T(8,128)S(1)} %get-tuple-element.20), channel_id=1, source_target_pairs={{0,8},{1,9},{2,10},{3,11},{4,12},{5,13},{6,14},{7,15},{8,0},{9,1},... | collective-permute-start | bytes 393224 | tf_op jit(solution)/shard_map/ppermute | solution.py:35
  62.8 9.1 %collective-permute-start.20 = (f32[32,1024]{1,0:T(8,128)S(1)}, f32[32,1024]{1,0:T(8,128)S(1)}, u32[]{:S(2)}, u32[]{:S(2)}) collective-permute-start(f32[32,1024]{1,0:T(8,128)S(1)} %get-tuple-element.20), channel_id=1, source_target_pairs={{0,6},{1,7},{2,4},{3,5},{4,2},{5,3},{6,0},{7,1},{8,14},{9,15},{10,... | collective-permute-start | bytes 393224 | tf_op jit(solution)/shard_map/ppermute | solution.py:35
  65.6 8.1 %collective-permute-start.19 = (f32[32,1024]{1,0:T(8,128)S(1)}, f32[32,1024]{1,0:T(8,128)S(1)}, u32[]{:S(2)}, u32[]{:S(2)}) collective-permute-start(f32[32,1024]{1,0:T(8,128)S(1)} %get-tuple-element.20), channel_id=1, source_target_pairs={{0,4},{1,5},{2,6},{3,7},{4,0},{5,1},{6,2},{7,3},{8,12},{9,13},{10,... | collective-permute-start | bytes 393224 | tf_op jit(solution)/shard_map/ppermute | solution.py:35
  65.9 7.8 %collective-permute-start.18 = (f32[32,1024]{1,0:T(8,128)S(1)}, f32[32,1024]{1,0:T(8,128)S(1)}, u32[]{:S(2)}, u32[]{:S(2)}) collective-permute-start(f32[32,1024]{1,0:T(8,128)S(1)} %get-tuple-element.20), channel_id=1, source_target_pairs={{0,2},{1,3},{2,0},{3,1},{4,6},{5,7},{6,4},{7,5},{8,10},{9,11},{10,... | collective-permute-start | bytes 393224 | tf_op jit(solution)/shard_map/ppermute | solution.py:35
  68.6 8.1 %collective-permute-start.24 = (f32[32,1024]{1,0:T(8,128)S(1)}, f32[32,1024]{1,0:T(8,128)S(1)}, u32[]{:S(2)}, u32[]{:S(2)}) collective-permute-start(f32[32,1024]{1,0:T(8,128)S(1)} %collective-permute-done.21), channel_id=1, source_target_pairs={{0,6},{1,7},{2,4},{3,5},{4,2},{5,3},{6,0},{7,1},{8,14},{9,15},{10,... | collective-permute-start | bytes 393224 | tf_op jit(solution)/shard_map/ppermute | solution.py:35
  70.1 7.6 %collective-permute-start.23 = (f32[32,1024]{1,0:T(8,128)S(1)}, f32[32,1024]{1,0:T(8,128)S(1)}, u32[]{:S(2)}, u32[]{:S(2)}) collective-permute-start(f32[32,1024]{1,0:T(8,128)S(1)} %collective-permute-done.21), channel_id=1, source_target_pairs={{0,4},{1,5},{2,6},{3,7},{4,0},{5,1},{6,2},{7,3},{8,12},{9,13},{10,... | collective-permute-start | bytes 393224 | tf_op jit(solution)/shard_map/ppermute | solution.py:35
  98.9 7.3 %collective-permute-start.32 = (f32[32,1024]{1,0:T(8,128)S(1)}, f32[32,1024]{1,0:T(8,128)S(1)}, u32[]{:S(2)}, u32[]{:S(2)}) collective-permute-start(f32[32,1024]{1,0:T(8,128)S(1)} %get-tuple-element.25), channel_id=1, source_target_pairs={{0,6},{1,7},{2,4},{3,5},{4,2},{5,3},{6,0},{7,1},{8,14},{9,15},{10,... | collective-permute-start | bytes 393224 | tf_op jit(solution)/shard_map/ppermute | solution.py:35
  100.9 8.2 %collective-permute-start.34 = (f32[32,1024]{1,0:T(8,128)S(1)}, f32[32,1024]{1,0:T(8,128)S(1)}, u32[]{:S(2)}, u32[]{:S(2)}) collective-permute-start(f32[32,1024]{1,0:T(8,128)S(1)} %get-tuple-element.26), channel_id=1, source_target_pairs={{0,2},{1,3},{2,0},{3,1},{4,6},{5,7},{6,4},{7,5},{8,10},{9,11},{10,... | collective-permute-start | bytes 393224 | tf_op jit(solution)/shard_map/ppermute | solution.py:35
  102.3 6.8 %collective-permute-start.33 = (f32[32,1024]{1,0:T(8,128)S(1)}, f32[32,1024]{1,0:T(8,128)S(1)}, u32[]{:S(2)}, u32[]{:S(2)}) collective-permute-start(f32[32,1024]{1,0:T(8,128)S(1)} %get-tuple-element.27), channel_id=1, source_target_pairs={{0,4},{1,5},{2,6},{3,7},{4,0},{5,1},{6,2},{7,3},{8,12},{9,13},{10,... | collective-permute-start | bytes 393224 | tf_op jit(solution)/shard_map/ppermute | solution.py:35
  102.6 9.3 %collective-permute-start.28 = (f32[32,1024]{1,0:T(8,128)S(1)}, f32[32,1024]{1,0:T(8,128)S(1)}, u32[]{:S(2)}, u32[]{:S(2)}) collective-permute-start(f32[32,1024]{1,0:T(8,128)S(1)} %get-tuple-element.22), channel_id=1, source_target_pairs={{0,6},{1,7},{2,4},{3,5},{4,2},{5,3},{6,0},{7,1},{8,14},{9,15},{10,... | collective-permute-start | bytes 393224 | tf_op jit(solution)/shard_map/ppermute | solution.py:35
  104.6 9.3 %collective-permute-start.30 = (f32[32,1024]{1,0:T(8,128)S(1)}, f32[32,1024]{1,0:T(8,128)S(1)}, u32[]{:S(2)}, u32[]{:S(2)}) collective-permute-start(f32[32,1024]{1,0:T(8,128)S(1)} %get-tuple-element.23), channel_id=1, source_target_pairs={{0,2},{1,3},{2,0},{3,1},{4,6},{5,7},{6,4},{7,5},{8,10},{9,11},{10,... | collective-permute-start | bytes 393224 | tf_op jit(solution)/shard_map/ppermute | solution.py:35
  106.2 9.9 %collective-permute-start.29 = (f32[32,1024]{1,0:T(8,128)S(1)}, f32[32,1024]{1,0:T(8,128)S(1)}, u32[]{:S(2)}, u32[]{:S(2)}) collective-permute-start(f32[32,1024]{1,0:T(8,128)S(1)} %get-tuple-element.24), channel_id=1, source_target_pairs={{0,4},{1,5},{2,6},{3,7},{4,0},{5,1},{6,2},{7,3},{8,12},{9,13},{10,... | collective-permute-start | bytes 393224 | tf_op jit(solution)/shard_map/ppermute | solution.py:35
  109.2 9.0 %collective-permute-start.35 = (f32[32,1024]{1,0:T(8,128)S(1)}, f32[32,1024]{1,0:T(8,128)S(1)}, u32[]{:S(2)}, u32[]{:S(2)}) collective-permute-start(f32[32,1024]{1,0:T(8,128)S(1)} %fusion.2), channel_id=1, source_target_pairs={{0,8},{1,9},{2,10},{3,11},{4,12},{5,13},{6,14},{7,15},{8,0},{9,1},... | collective-permute-start | bytes 393224 | tf_op jit(solution)/shard_map/ppermute | solution.py:35
  (16 other events, 231.0 us)

commit v6 on v5

--- a/solution.py
+++ b/solution.py
@@ -48,7 +48,7 @@
     pieces[low] = swap(own, low)
     pieces[low | high] = swap(own, low | high) if corner_at_once else swap(pieces[high], low)
     for p in sorted(far[1:]):
-        for mask in (high, low, low | high):
+        for mask in (low, high, low | high):
             pieces[p | mask] = swap(pieces[p], mask)
     order = sorted(pieces) if corner_at_once else sorted(pieces, key=lambda p: p.bit_count())
     arrays = [([p], pieces[p][None]) for p in order]
@@ -66,7 +66,7 @@
         whole = kept + swap(sent, CORE)
         held |= {p: whole[j] for j, p in enumerate(group)}
     for p in sorted((p for p in held if not p & (low | high)), reverse=True):
-        for mask in (low | high, high, low):
+        for mask in (low, low | high, high):
             held[p] += swap(held.pop(p | mask), mask)
     for bit in far_bits(count):
         for p in sorted((p for p in held if p & bit), reverse=True):

time: 119 us -> 118 us (level)
  starting transfers between devices: 45.9 us -> 39.4 us
  waiting for transfers between devices: 35 us -> 40.2 us
    ppermute x36, starting transfers between devices: 45.9 us -> 39.4 us  [swap(): return lax.ppermute(x, 'col', [(i, i ^ mask) for i in range(count)])]
    ppermute x36, waiting for transfers between devices: 35 us -> 40.2 us  [swap(): return lax.ppermute(x, 'col', [(i, i ^ mask) for i in range(count)])]
where the time goes in v6:
time: 118 us
  waiting for transfers between devices  40.2 us (34%)
  starting transfers between devices  39.4 us (33%)
  Pallas kernels  34.1 us (29%)
  other arithmetic  2.32 us (2%)
    ppermute x36, waiting for transfers between devices, swap(): return lax.ppermute(x, 'col', [(i, i ^ mask) for i in range(count)])  40.2 us
    ppermute x36, starting transfers between devices, swap(): return lax.ppermute(x, 'col', [(i, i ^ mask) for i in range(count)])  39.4 us
    pallas_call x2, Pallas kernels, product(): pl.pallas_call(functools.partial(product_kernel, held, width), in_specs=[...  34.1 us
  transfers between devices with their start and end apart: 36, of which 23 were waited for; matrix products, arithmetic and copies ran while one was open for 0% of the time, Pallas kernels for 0%

profile of v6, /device:TPU:0, one launch (start us, length us, event | category | flops | bytes accessed | tf_op | source)
XLA Modules:
  0.0 117.6 jit_solution(4355954003748971211)
XLA Ops:
  1.7 3.1 %collective-permute-start.1 = (f32[32,1024]{1,0:T(8,128)S(1)}, f32[32,1024]{1,0:T(8,128)S(1)}, u32[]{:S(2)}, u32[]{:S(2)}) collective-permute-start(f32[32,1024]{1,0:T(8,128)S(1)} %sub.12), channel_id=1, source_target_pairs={{0,4},{1,5},{2,6},{3,7},{4,0},{5,1},{6,2},{7,3},{8,12},{9,13},{10,... | collective-permute-start | bytes 393224 | tf_op jit(solution)/shard_map/ppermute | solution.py:35
  4.8 2.6 %collective-permute-start = (f32[32,1024]{1,0:T(8,128)S(1)}, f32[32,1024]{1,0:T(8,128)S(1)}, u32[]{:S(2)}, u32[]{:S(2)}) collective-permute-start(f32[32,1024]{1,0:T(8,128)S(1)} %sub.12), channel_id=1, source_target_pairs={{0,8},{1,9},{2,10},{3,11},{4,12},{5,13},{6,14},{7,15},{8,0},{9,1},... | collective-permute-start | bytes 393224 | tf_op jit(solution)/shard_map/ppermute | solution.py:35
  7.4 1.5 %collective-permute-start.2 = (f32[32,1024]{1,0:T(8,128)S(1)}, f32[32,1024]{1,0:T(8,128)S(1)}, u32[]{:S(2)}, u32[]{:S(2)}) collective-permute-start(f32[32,1024]{1,0:T(8,128)S(1)} %sub.12), channel_id=1, source_target_pairs={{0,2},{1,3},{2,0},{3,1},{4,6},{5,7},{6,4},{7,5},{8,10},{9,11},{10,... | collective-permute-start | bytes 393224 | tf_op jit(solution)/shard_map/ppermute | solution.py:35
  10.1 1.8 %collective-permute-start.3 = (f32[32,1024]{1,0:T(8,128)S(1)}, f32[32,1024]{1,0:T(8,128)S(1)}, u32[]{:S(2)}, u32[]{:S(2)}) collective-permute-start(f32[32,1024]{1,0:T(8,128)S(1)} %collective-permute-done.1), channel_id=1, source_target_pairs={{0,2},{1,3},{2,0},{3,1},{4,6},{5,7},{6,4},{7,5},{8,10},{9,11},{10,... | collective-permute-start | bytes 393224 | tf_op jit(solution)/shard_map/ppermute | solution.py:35
  12.0 1.5 %collective-permute-done = f32[32,1024]{1,0:T(8,128)S(1)} collective-permute-done((f32[32,1024]{1,0:T(8,128)S(1)}, f32[32,1024]{1,0:T(8,128)S(1)}, u32[]{:S(2)}, u32[]{:S(2)}) %collective-permute-start) | collective-permute-done | bytes 131104 | tf_op jit(solution)/shard_map/ppermute | solution.py:35
  14.9 1.6 %collective-permute-start.5 = (f32[32,1024]{1,0:T(8,128)S(1)}, f32[32,1024]{1,0:T(8,128)S(1)}, u32[]{:S(2)}, u32[]{:S(2)}) collective-permute-start(f32[32,1024]{1,0:T(8,128)S(1)} %collective-permute-done), channel_id=1, source_target_pairs={{0,4},{1,5},{2,6},{3,7},{4,0},{5,1},{6,2},{7,3},{8,12},{9,13},{10,... | collective-permute-start | bytes 393224 | tf_op jit(solution)/shard_map/ppermute | solution.py:35
  17.1 2.2 %collective-permute-done.6 = f32[32,1024]{1,0:T(8,128)S(1)} collective-permute-done((f32[32,1024]{1,0:T(8,128)S(1)}, f32[32,1024]{1,0:T(8,128)S(1)}, u32[]{:S(2)}, u32[]{:S(2)}) %collective-permute-start.6) | collective-permute-done | bytes 131104 | tf_op jit(solution)/shard_map/ppermute | solution.py:35
  21.6 1.9 %collective-permute-done.8.refs_9_ = f32[4,32,1024]{2,1,0:T(8,128)S(1)} collective-permute-done((f32[4,32,1024]{2,1,0:T(8,128)S(1)}, f32[4,32,1024]{2,1,0:T(8,128)S(1)}, u32[]{:S(2)}, u32[]{:S(2)}) %collective-permute-start.8) | collective-permute-done | bytes 524320 | tf_op jit(solution)/shard_map/ppermute | solution.py:35
  24.2 17.0 %product.2 = (f32[4,32,1024]{2,1,0:T(8,128)S(1)}, f32[4,32,1024]{2,1,0:T(8,128)S(1)}, f32[4,32,1024]{2,1,0:T(8,128)S(1)}, f32[4,32,1024]{2,1,0:T(8,128)S(1)}) custom-call(s32[2,33]{1,0:T(2,128)S(1)} %bitcast.113, f32[33,512,512]{2,1,0:T(8,128)} %tiles.3, f32[1,32,1024]{2,1,0:T(8,128)S(1)} %bitcast.84, f32[1,32,1024]{2,1,0:T(8,128)S(1)} %bitcast.90, ...), custom_call_target="tpu_custom_call" | custom-call | flops 3321888768 | bytes 34603008 | tf_op jit(solution)/shard_map/product/pallas_call | solution.py:187
  50.6 3.4 %collective-permute-done.15 = f32[32,1024]{1,0:T(8,128)S(1)} collective-permute-done((f32[32,1024]{1,0:T(8,128)S(1)}, f32[32,1024]{1,0:T(8,128)S(1)}, u32[]{:S(2)}, u32[]{:S(2)}) %collective-permute-start.15) | collective-permute-done | bytes 131104 | tf_op jit(solution)/shard_map/ppermute | solution.py:35
  54.0 1.6 %collective-permute-start.17 = (f32[32,1024]{1,0:T(8,128)S(1)}, f32[32,1024]{1,0:T(8,128)S(1)}, u32[]{:S(2)}, u32[]{:S(2)}) collective-permute-start(f32[32,1024]{1,0:T(8,128)S(1)} %fusion.10), channel_id=1, source_target_pairs={{0,8},{1,9},{2,10},{3,11},{4,12},{5,13},{6,14},{7,15},{8,0},{9,1},... | collective-permute-start | bytes 393224 | tf_op jit(solution)/shard_map/ppermute | solution.py:35
  55.6 1.9 %collective-permute-done.12 = f32[32,1024]{1,0:T(8,128)S(1)} collective-permute-done((f32[32,1024]{1,0:T(8,128)S(1)}, f32[32,1024]{1,0:T(8,128)S(1)}, u32[]{:S(2)}, u32[]{:S(2)}) %collective-permute-start.12) | collective-permute-done | bytes 131104 | tf_op jit(solution)/shard_map/ppermute | solution.py:35
  57.6 3.3 %collective-permute-done.11 = f32[32,1024]{1,0:T(8,128)S(1)} collective-permute-done((f32[32,1024]{1,0:T(8,128)S(1)}, f32[32,1024]{1,0:T(8,128)S(1)}, u32[]{:S(2)}, u32[]{:S(2)}) %collective-permute-start.11) | collective-permute-done | bytes 131104 | tf_op jit(solution)/shard_map/ppermute | solution.py:35
  60.9 1.9 %collective-permute-done.17 = f32[32,1024]{1,0:T(8,128)S(1)} collective-permute-done((f32[32,1024]{1,0:T(8,128)S(1)}, f32[32,1024]{1,0:T(8,128)S(1)}, u32[]{:S(2)}, u32[]{:S(2)}) %collective-permute-start.17) | collective-permute-done | bytes 131104 | tf_op jit(solution)/shard_map/ppermute | solution.py:35
  63.0 2.8 %collective-permute-start.20 = (f32[32,1024]{1,0:T(8,128)S(1)}, f32[32,1024]{1,0:T(8,128)S(1)}, u32[]{:S(2)}, u32[]{:S(2)}) collective-permute-start(f32[32,1024]{1,0:T(8,128)S(1)} %get-tuple-element.20), channel_id=1, source_target_pairs={{0,6},{1,7},{2,4},{3,5},{4,2},{5,3},{6,0},{7,1},{8,14},{9,15},{10,... | collective-permute-start | bytes 393224 | tf_op jit(solution)/shard_map/ppermute | solution.py:35
  66.9 3.3 %collective-permute-done.21 = f32[32,1024]{1,0:T(8,128)S(1)} collective-permute-done((f32[32,1024]{1,0:T(8,128)S(1)}, f32[32,1024]{1,0:T(8,128)S(1)}, u32[]{:S(2)}, u32[]{:S(2)}) %collective-permute-start.21) | collective-permute-done | bytes 131104 | tf_op jit(solution)/shard_map/ppermute | solution.py:35
  70.5 1.7 %collective-permute-start.23 = (f32[32,1024]{1,0:T(8,128)S(1)}, f32[32,1024]{1,0:T(8,128)S(1)}, u32[]{:S(2)}, u32[]{:S(2)}) collective-permute-start(f32[32,1024]{1,0:T(8,128)S(1)} %collective-permute-done.21), channel_id=1, source_target_pairs={{0,4},{1,5},{2,6},{3,7},{4,0},{5,1},{6,2},{7,3},{8,12},{9,13},{10,... | collective-permute-start | bytes 393224 | tf_op jit(solution)/shard_map/ppermute | solution.py:35
  74.5 1.9 %collective-permute-done.24 = f32[32,1024]{1,0:T(8,128)S(1)} collective-permute-done((f32[32,1024]{1,0:T(8,128)S(1)}, f32[32,1024]{1,0:T(8,128)S(1)}, u32[]{:S(2)}, u32[]{:S(2)}) %collective-permute-start.24) | collective-permute-done | bytes 131104 | tf_op jit(solution)/shard_map/ppermute | solution.py:35
  77.8 1.9 %collective-permute-done.26.refs_9_ = f32[4,32,1024]{2,1,0:T(8,128)S(1)} collective-permute-done((f32[4,32,1024]{2,1,0:T(8,128)S(1)}, f32[4,32,1024]{2,1,0:T(8,128)S(1)}, u32[]{:S(2)}, u32[]{:S(2)}) %collective-permute-start.26) | collective-permute-done | bytes 524320 | tf_op jit(solution)/shard_map/ppermute | solution.py:35
  79.7 17.0 %product.3 = (f32[4,32,1024]{2,1,0:T(8,128)S(1)}, f32[4,32,1024]{2,1,0:T(8,128)S(1)}, f32[4,32,1024]{2,1,0:T(8,128)S(1)}, f32[4,32,1024]{2,1,0:T(8,128)S(1)}) custom-call(s32[2,33]{1,0:T(2,128)S(1)} %bitcast.114, f32[33,512,512]{2,1,0:T(8,128)} %tiles.3, f32[1,32,1024]{2,1,0:T(8,128)S(1)} %bitcast.82, f32[1,32,1024]{2,1,0:T(8,128)S(1)} %bitcast.98, ...), custom_call_target="tpu_custom_call" | custom-call | flops 3321888768 | bytes 34603008 | tf_op jit(solution)/shard_map/product/pallas_call | solution.py:187
  106.3 3.3 %collective-permute-done.33 = f32[32,1024]{1,0:T(8,128)S(1)} collective-permute-done((f32[32,1024]{1,0:T(8,128)S(1)}, f32[32,1024]{1,0:T(8,128)S(1)}, u32[]{:S(2)}, u32[]{:S(2)}) %collective-permute-start.33) | collective-permute-done | bytes 131104 | tf_op jit(solution)/shard_map/ppermute | solution.py:35
  109.6 1.9 %collective-permute-start.35 = (f32[32,1024]{1,0:T(8,128)S(1)}, f32[32,1024]{1,0:T(8,128)S(1)}, u32[]{:S(2)}, u32[]{:S(2)}) collective-permute-start(f32[32,1024]{1,0:T(8,128)S(1)} %fusion.2), channel_id=1, source_target_pairs={{0,8},{1,9},{2,10},{3,11},{4,12},{5,13},{6,14},{7,15},{8,0},{9,1},... | collective-permute-start | bytes 393224 | tf_op jit(solution)/shard_map/ppermute | solution.py:35
  111.5 1.7 %collective-permute-done.30 = f32[32,1024]{1,0:T(8,128)S(1)} collective-permute-done((f32[32,1024]{1,0:T(8,128)S(1)}, f32[32,1024]{1,0:T(8,128)S(1)}, u32[]{:S(2)}, u32[]{:S(2)}) %collective-permute-start.30) | collective-permute-done | bytes 131104 | tf_op jit(solution)/shard_map/ppermute | solution.py:35
  113.3 3.6 %collective-permute-done.29 = f32[32,1024]{1,0:T(8,128)S(1)} collective-permute-done((f32[32,1024]{1,0:T(8,128)S(1)}, f32[32,1024]{1,0:T(8,128)S(1)}, u32[]{:S(2)}, u32[]{:S(2)}) %collective-permute-start.29) | collective-permute-done | bytes 131104 | tf_op jit(solution)/shard_map/ppermute | solution.py:35
  (75 shorter events, 32.1 us)
Async XLA Ops:
  1.7 8.4 %collective-permute-start.1 = (f32[32,1024]{1,0:T(8,128)S(1)}, f32[32,1024]{1,0:T(8,128)S(1)}, u32[]{:S(2)}, u32[]{:S(2)}) collective-permute-start(f32[32,1024]{1,0:T(8,128)S(1)} %sub.12), channel_id=1, source_target_pairs={{0,4},{1,5},{2,6},{3,7},{4,0},{5,1},{6,2},{7,3},{8,12},{9,13},{10,... | collective-permute-start | bytes 393224 | tf_op jit(solution)/shard_map/ppermute | solution.py:35
  4.8 8.7 %collective-permute-start = (f32[32,1024]{1,0:T(8,128)S(1)}, f32[32,1024]{1,0:T(8,128)S(1)}, u32[]{:S(2)}, u32[]{:S(2)}) collective-permute-start(f32[32,1024]{1,0:T(8,128)S(1)} %sub.12), channel_id=1, source_target_pairs={{0,8},{1,9},{2,10},{3,11},{4,12},{5,13},{6,14},{7,15},{8,0},{9,1},... | collective-permute-start | bytes 393224 | tf_op jit(solution)/shard_map/ppermute | solution.py:35
  7.4 9.6 %collective-permute-start.2 = (f32[32,1024]{1,0:T(8,128)S(1)}, f32[32,1024]{1,0:T(8,128)S(1)}, u32[]{:S(2)}, u32[]{:S(2)}) collective-permute-start(f32[32,1024]{1,0:T(8,128)S(1)} %sub.12), channel_id=1, source_target_pairs={{0,2},{1,3},{2,0},{3,1},{4,6},{5,7},{6,4},{7,5},{8,10},{9,11},{10,... | collective-permute-start | bytes 393224 | tf_op jit(solution)/shard_map/ppermute | solution.py:35
  10.1 7.0 %collective-permute-start.3 = (f32[32,1024]{1,0:T(8,128)S(1)}, f32[32,1024]{1,0:T(8,128)S(1)}, u32[]{:S(2)}, u32[]{:S(2)}) collective-permute-start(f32[32,1024]{1,0:T(8,128)S(1)} %collective-permute-done.1), channel_id=1, source_target_pairs={{0,2},{1,3},{2,0},{3,1},{4,6},{5,7},{6,4},{7,5},{8,10},{9,11},{10,... | collective-permute-start | bytes 393224 | tf_op jit(solution)/shard_map/ppermute | solution.py:35
  14.9 5.9 %collective-permute-start.5 = (f32[32,1024]{1,0:T(8,128)S(1)}, f32[32,1024]{1,0:T(8,128)S(1)}, u32[]{:S(2)}, u32[]{:S(2)}) collective-permute-start(f32[32,1024]{1,0:T(8,128)S(1)} %collective-permute-done), channel_id=1, source_target_pairs={{0,4},{1,5},{2,6},{3,7},{4,0},{5,1},{6,2},{7,3},{8,12},{9,13},{10,... | collective-permute-start | bytes 393224 | tf_op jit(solution)/shard_map/ppermute | solution.py:35
  44.2 6.4 %collective-permute-start.16 = (f32[32,1024]{1,0:T(8,128)S(1)}, f32[32,1024]{1,0:T(8,128)S(1)}, u32[]{:S(2)}, u32[]{:S(2)}) collective-permute-start(f32[32,1024]{1,0:T(8,128)S(1)} %get-tuple-element.32), channel_id=1, source_target_pairs={{0,4},{1,5},{2,6},{3,7},{4,0},{5,1},{6,2},{7,3},{8,12},{9,13},{10,... | collective-permute-start | bytes 393224 | tf_op jit(solution)/shard_map/ppermute | solution.py:35
  45.3 8.7 %collective-permute-start.15 = (f32[32,1024]{1,0:T(8,128)S(1)}, f32[32,1024]{1,0:T(8,128)S(1)}, u32[]{:S(2)}, u32[]{:S(2)}) collective-permute-start(f32[32,1024]{1,0:T(8,128)S(1)} %get-tuple-element.33), channel_id=1, source_target_pairs={{0,6},{1,7},{2,4},{3,5},{4,2},{5,3},{6,0},{7,1},{8,14},{9,15},{10,... | collective-permute-start | bytes 393224 | tf_op jit(solution)/shard_map/ppermute | solution.py:35
  46.9 8.7 %collective-permute-start.10 = (f32[32,1024]{1,0:T(8,128)S(1)}, f32[32,1024]{1,0:T(8,128)S(1)}, u32[]{:S(2)}, u32[]{:S(2)}) collective-permute-start(f32[32,1024]{1,0:T(8,128)S(1)} %get-tuple-element.28), channel_id=1, source_target_pairs={{0,2},{1,3},{2,0},{3,1},{4,6},{5,7},{6,4},{7,5},{8,10},{9,11},{10,... | collective-permute-start | bytes 393224 | tf_op jit(solution)/shard_map/ppermute | solution.py:35
  47.8 9.7 %collective-permute-start.12 = (f32[32,1024]{1,0:T(8,128)S(1)}, f32[32,1024]{1,0:T(8,128)S(1)}, u32[]{:S(2)}, u32[]{:S(2)}) collective-permute-start(f32[32,1024]{1,0:T(8,128)S(1)} %get-tuple-element.29), channel_id=1, source_target_pairs={{0,4},{1,5},{2,6},{3,7},{4,0},{5,1},{6,2},{7,3},{8,12},{9,13},{10,... | collective-permute-start | bytes 393224 | tf_op jit(solution)/shard_map/ppermute | solution.py:35
  49.0 11.9 %collective-permute-start.11 = (f32[32,1024]{1,0:T(8,128)S(1)}, f32[32,1024]{1,0:T(8,128)S(1)}, u32[]{:S(2)}, u32[]{:S(2)}) collective-permute-start(f32[32,1024]{1,0:T(8,128)S(1)} %get-tuple-element.30), channel_id=1, source_target_pairs={{0,6},{1,7},{2,4},{3,5},{4,2},{5,3},{6,0},{7,1},{8,14},{9,15},{10,... | collective-permute-start | bytes 393224 | tf_op jit(solution)/shard_map/ppermute | solution.py:35
  54.0 8.7 %collective-permute-start.17 = (f32[32,1024]{1,0:T(8,128)S(1)}, f32[32,1024]{1,0:T(8,128)S(1)}, u32[]{:S(2)}, u32[]{:S(2)}) collective-permute-start(f32[32,1024]{1,0:T(8,128)S(1)} %fusion.10), channel_id=1, source_target_pairs={{0,8},{1,9},{2,10},{3,11},{4,12},{5,13},{6,14},{7,15},{8,0},{9,1},... | collective-permute-start | bytes 393224 | tf_op jit(solution)/shard_map/ppermute | solution.py:35
  62.9 7.3 %collective-permute-start.21 = (f32[32,1024]{1,0:T(8,128)S(1)}, f32[32,1024]{1,0:T(8,128)S(1)}, u32[]{:S(2)}, u32[]{:S(2)}) collective-permute-start(f32[32,1024]{1,0:T(8,128)S(1)} %get-tuple-element.20), channel_id=1, source_target_pairs={{0,8},{1,9},{2,10},{3,11},{4,12},{5,13},{6,14},{7,15},{8,0},{9,1},... | collective-permute-start | bytes 393224 | tf_op jit(solution)/shard_map/ppermute | solution.py:35
  63.0 9.3 %collective-permute-start.20 = (f32[32,1024]{1,0:T(8,128)S(1)}, f32[32,1024]{1,0:T(8,128)S(1)}, u32[]{:S(2)}, u32[]{:S(2)}) collective-permute-start(f32[32,1024]{1,0:T(8,128)S(1)} %get-tuple-element.20), channel_id=1, source_target_pairs={{0,6},{1,7},{2,4},{3,5},{4,2},{5,3},{6,0},{7,1},{8,14},{9,15},{10,... | collective-permute-start | bytes 393224 | tf_op jit(solution)/shard_map/ppermute | solution.py:35
  65.8 7.9 %collective-permute-start.19 = (f32[32,1024]{1,0:T(8,128)S(1)}, f32[32,1024]{1,0:T(8,128)S(1)}, u32[]{:S(2)}, u32[]{:S(2)}) collective-permute-start(f32[32,1024]{1,0:T(8,128)S(1)} %get-tuple-element.20), channel_id=1, source_target_pairs={{0,4},{1,5},{2,6},{3,7},{4,0},{5,1},{6,2},{7,3},{8,12},{9,13},{10,... | collective-permute-start | bytes 393224 | tf_op jit(solution)/shard_map/ppermute | solution.py:35
  65.8 8.6 %collective-permute-start.18 = (f32[32,1024]{1,0:T(8,128)S(1)}, f32[32,1024]{1,0:T(8,128)S(1)}, u32[]{:S(2)}, u32[]{:S(2)}) collective-permute-start(f32[32,1024]{1,0:T(8,128)S(1)} %get-tuple-element.20), channel_id=1, source_target_pairs={{0,2},{1,3},{2,0},{3,1},{4,6},{5,7},{6,4},{7,5},{8,10},{9,11},{10,... | collective-permute-start | bytes 393224 | tf_op jit(solution)/shard_map/ppermute | solution.py:35
  70.2 6.2 %collective-permute-start.24 = (f32[32,1024]{1,0:T(8,128)S(1)}, f32[32,1024]{1,0:T(8,128)S(1)}, u32[]{:S(2)}, u32[]{:S(2)}) collective-permute-start(f32[32,1024]{1,0:T(8,128)S(1)} %collective-permute-done.21), channel_id=1, source_target_pairs={{0,6},{1,7},{2,4},{3,5},{4,2},{5,3},{6,0},{7,1},{8,14},{9,15},{10,... | collective-permute-start | bytes 393224 | tf_op jit(solution)/shard_map/ppermute | solution.py:35
  70.5 6.4 %collective-permute-start.23 = (f32[32,1024]{1,0:T(8,128)S(1)}, f32[32,1024]{1,0:T(8,128)S(1)}, u32[]{:S(2)}, u32[]{:S(2)}) collective-permute-start(f32[32,1024]{1,0:T(8,128)S(1)} %collective-permute-done.21), channel_id=1, source_target_pairs={{0,4},{1,5},{2,6},{3,7},{4,0},{5,1},{6,2},{7,3},{8,12},{9,13},{10,... | collective-permute-start | bytes 393224 | tf_op jit(solution)/shard_map/ppermute | solution.py:35
  98.9 6.0 %collective-permute-start.32 = (f32[32,1024]{1,0:T(8,128)S(1)}, f32[32,1024]{1,0:T(8,128)S(1)}, u32[]{:S(2)}, u32[]{:S(2)}) collective-permute-start(f32[32,1024]{1,0:T(8,128)S(1)} %get-tuple-element.25), channel_id=1, source_target_pairs={{0,2},{1,3},{2,0},{3,1},{4,6},{5,7},{6,4},{7,5},{8,10},{9,11},{10,... | collective-permute-start | bytes 393224 | tf_op jit(solution)/shard_map/ppermute | solution.py:35
  99.9 6.4 %collective-permute-start.34 = (f32[32,1024]{1,0:T(8,128)S(1)}, f32[32,1024]{1,0:T(8,128)S(1)}, u32[]{:S(2)}, u32[]{:S(2)}) collective-permute-start(f32[32,1024]{1,0:T(8,128)S(1)} %get-tuple-element.26), channel_id=1, source_target_pairs={{0,4},{1,5},{2,6},{3,7},{4,0},{5,1},{6,2},{7,3},{8,12},{9,13},{10,... | collective-permute-start | bytes 393224 | tf_op jit(solution)/shard_map/ppermute | solution.py:35
  101.2 8.4 %collective-permute-start.33 = (f32[32,1024]{1,0:T(8,128)S(1)}, f32[32,1024]{1,0:T(8,128)S(1)}, u32[]{:S(2)}, u32[]{:S(2)}) collective-permute-start(f32[32,1024]{1,0:T(8,128)S(1)} %get-tuple-element.27), channel_id=1, source_target_pairs={{0,6},{1,7},{2,4},{3,5},{4,2},{5,3},{6,0},{7,1},{8,14},{9,15},{10,... | collective-permute-start | bytes 393224 | tf_op jit(solution)/shard_map/ppermute | solution.py:35
  102.5 9.0 %collective-permute-start.28 = (f32[32,1024]{1,0:T(8,128)S(1)}, f32[32,1024]{1,0:T(8,128)S(1)}, u32[]{:S(2)}, u32[]{:S(2)}) collective-permute-start(f32[32,1024]{1,0:T(8,128)S(1)} %get-tuple-element.22), channel_id=1, source_target_pairs={{0,2},{1,3},{2,0},{3,1},{4,6},{5,7},{6,4},{7,5},{8,10},{9,11},{10,... | collective-permute-start | bytes 393224 | tf_op jit(solution)/shard_map/ppermute | solution.py:35
  103.5 9.7 %collective-permute-start.30 = (f32[32,1024]{1,0:T(8,128)S(1)}, f32[32,1024]{1,0:T(8,128)S(1)}, u32[]{:S(2)}, u32[]{:S(2)}) collective-permute-start(f32[32,1024]{1,0:T(8,128)S(1)} %get-tuple-element.23), channel_id=1, source_target_pairs={{0,4},{1,5},{2,6},{3,7},{4,0},{5,1},{6,2},{7,3},{8,12},{9,13},{10,... | collective-permute-start | bytes 393224 | tf_op jit(solution)/shard_map/ppermute | solution.py:35
  104.9 12.0 %collective-permute-start.29 = (f32[32,1024]{1,0:T(8,128)S(1)}, f32[32,1024]{1,0:T(8,128)S(1)}, u32[]{:S(2)}, u32[]{:S(2)}) collective-permute-start(f32[32,1024]{1,0:T(8,128)S(1)} %get-tuple-element.24), channel_id=1, source_target_pairs={{0,6},{1,7},{2,4},{3,5},{4,2},{5,3},{6,0},{7,1},{8,14},{9,15},{10,... | collective-permute-start | bytes 393224 | tf_op jit(solution)/shard_map/ppermute | solution.py:35
  109.6 7.2 %collective-permute-start.35 = (f32[32,1024]{1,0:T(8,128)S(1)}, f32[32,1024]{1,0:T(8,128)S(1)}, u32[]{:S(2)}, u32[]{:S(2)}) collective-permute-start(f32[32,1024]{1,0:T(8,128)S(1)} %fusion.2), channel_id=1, source_target_pairs={{0,8},{1,9},{2,10},{3,11},{4,12},{5,13},{6,14},{7,15},{8,0},{9,1},... | collective-permute-start | bytes 393224 | tf_op jit(solution)/shard_map/ppermute | solution.py:35
  (16 other events, 235.8 us)

commit v7 on v6

--- a/solution.py
+++ b/solution.py
@@ -44,8 +44,8 @@
         for p in list(far):
             pieces[p | bit] = swap(pieces[p], bit)
             far.append(p | bit)
+    pieces[low] = swap(own, low)
     pieces[high] = swap(own, high)
-    pieces[low] = swap(own, low)
     pieces[low | high] = swap(own, low | high) if corner_at_once else swap(pieces[high], low)
     for p in sorted(far[1:]):
         for mask in (low, high, low | high):

time: 118 us -> 118 us (level)
  no operation moved by 1% of the time
where the time goes in v7:
time: 118 us
  waiting for transfers between devices  40.2 us (34%)
  starting transfers between devices  39.4 us (33%)
  Pallas kernels  34.1 us (29%)
  other arithmetic  2.32 us (2%)
    ppermute x36, waiting for transfers between devices, swap(): return lax.ppermute(x, 'col', [(i, i ^ mask) for i in range(count)])  40.2 us
    ppermute x36, starting transfers between devices, swap(): return lax.ppermute(x, 'col', [(i, i ^ mask) for i in range(count)])  39.4 us
    pallas_call x2, Pallas kernels, product(): pl.pallas_call(functools.partial(product_kernel, held, width), in_specs=[...  34.1 us
  transfers between devices with their start and end apart: 36, of which 23 were waited for; matrix products, arithmetic and copies ran while one was open for 0% of the time, Pallas kernels for 0%

profile of v7, /device:TPU:0, one launch (start us, length us, event | category | flops | bytes accessed | tf_op | source)
XLA Modules:
  0.0 117.6 jit_solution(17978694735624970542)
XLA Ops:
  1.7 3.1 %collective-permute-start.2 = (f32[32,1024]{1,0:T(8,128)S(1)}, f32[32,1024]{1,0:T(8,128)S(1)}, u32[]{:S(2)}, u32[]{:S(2)}) collective-permute-start(f32[32,1024]{1,0:T(8,128)S(1)} %sub.12), channel_id=1, source_target_pairs={{0,4},{1,5},{2,6},{3,7},{4,0},{5,1},{6,2},{7,3},{8,12},{9,13},{10,... | collective-permute-start | bytes 393224 | tf_op jit(solution)/shard_map/ppermute | solution.py:35
  4.8 2.6 %collective-permute-start = (f32[32,1024]{1,0:T(8,128)S(1)}, f32[32,1024]{1,0:T(8,128)S(1)}, u32[]{:S(2)}, u32[]{:S(2)}) collective-permute-start(f32[32,1024]{1,0:T(8,128)S(1)} %sub.12), channel_id=1, source_target_pairs={{0,8},{1,9},{2,10},{3,11},{4,12},{5,13},{6,14},{7,15},{8,0},{9,1},... | collective-permute-start | bytes 393224 | tf_op jit(solution)/shard_map/ppermute | solution.py:35
  7.4 1.5 %collective-permute-start.1 = (f32[32,1024]{1,0:T(8,128)S(1)}, f32[32,1024]{1,0:T(8,128)S(1)}, u32[]{:S(2)}, u32[]{:S(2)}) collective-permute-start(f32[32,1024]{1,0:T(8,128)S(1)} %sub.12), channel_id=1, source_target_pairs={{0,2},{1,3},{2,0},{3,1},{4,6},{5,7},{6,4},{7,5},{8,10},{9,11},{10,... | collective-permute-start | bytes 393224 | tf_op jit(solution)/shard_map/ppermute | solution.py:35
  10.1 1.8 %collective-permute-start.3 = (f32[32,1024]{1,0:T(8,128)S(1)}, f32[32,1024]{1,0:T(8,128)S(1)}, u32[]{:S(2)}, u32[]{:S(2)}) collective-permute-start(f32[32,1024]{1,0:T(8,128)S(1)} %collective-permute-done.2), channel_id=1, source_target_pairs={{0,2},{1,3},{2,0},{3,1},{4,6},{5,7},{6,4},{7,5},{8,10},{9,11},{10,... | collective-permute-start | bytes 393224 | tf_op jit(solution)/shard_map/ppermute | solution.py:35
  12.0 1.5 %collective-permute-done = f32[32,1024]{1,0:T(8,128)S(1)} collective-permute-done((f32[32,1024]{1,0:T(8,128)S(1)}, f32[32,1024]{1,0:T(8,128)S(1)}, u32[]{:S(2)}, u32[]{:S(2)}) %collective-permute-start) | collective-permute-done | bytes 131104 | tf_op jit(solution)/shard_map/ppermute | solution.py:35
  14.9 1.6 %collective-permute-start.5 = (f32[32,1024]{1,0:T(8,128)S(1)}, f32[32,1024]{1,0:T(8,128)S(1)}, u32[]{:S(2)}, u32[]{:S(2)}) collective-permute-start(f32[32,1024]{1,0:T(8,128)S(1)} %collective-permute-done), channel_id=1, source_target_pairs={{0,4},{1,5},{2,6},{3,7},{4,0},{5,1},{6,2},{7,3},{8,12},{9,13},{10,... | collective-permute-start | bytes 393224 | tf_op jit(solution)/shard_map/ppermute | solution.py:35
  17.1 2.2 %collective-permute-done.6 = f32[32,1024]{1,0:T(8,128)S(1)} collective-permute-done((f32[32,1024]{1,0:T(8,128)S(1)}, f32[32,1024]{1,0:T(8,128)S(1)}, u32[]{:S(2)}, u32[]{:S(2)}) %collective-permute-start.6) | collective-permute-done | bytes 131104 | tf_op jit(solution)/shard_map/ppermute | solution.py:35
  21.6 1.9 %collective-permute-done.8.refs_9_ = f32[4,32,1024]{2,1,0:T(8,128)S(1)} collective-permute-done((f32[4,32,1024]{2,1,0:T(8,128)S(1)}, f32[4,32,1024]{2,1,0:T(8,128)S(1)}, u32[]{:S(2)}, u32[]{:S(2)}) %collective-permute-start.8) | collective-permute-done | bytes 524320 | tf_op jit(solution)/shard_map/ppermute | solution.py:35
  24.2 17.0 %product.2 = (f32[4,32,1024]{2,1,0:T(8,128)S(1)}, f32[4,32,1024]{2,1,0:T(8,128)S(1)}, f32[4,32,1024]{2,1,0:T(8,128)S(1)}, f32[4,32,1024]{2,1,0:T(8,128)S(1)}) custom-call(s32[2,33]{1,0:T(2,128)S(1)} %bitcast.113, f32[33,512,512]{2,1,0:T(8,128)} %tiles.3, f32[1,32,1024]{2,1,0:T(8,128)S(1)} %bitcast.84, f32[1,32,1024]{2,1,0:T(8,128)S(1)} %bitcast.90, ...), custom_call_target="tpu_custom_call" | custom-call | flops 3321888768 | bytes 34603008 | tf_op jit(solution)/shard_map/product/pallas_call | solution.py:187
  50.6 3.4 %collective-permute-done.15 = f32[32,1024]{1,0:T(8,128)S(1)} collective-permute-done((f32[32,1024]{1,0:T(8,128)S(1)}, f32[32,1024]{1,0:T(8,128)S(1)}, u32[]{:S(2)}, u32[]{:S(2)}) %collective-permute-start.15) | collective-permute-done | bytes 131104 | tf_op jit(solution)/shard_map/ppermute | solution.py:35
  54.0 1.6 %collective-permute-start.17 = (f32[32,1024]{1,0:T(8,128)S(1)}, f32[32,1024]{1,0:T(8,128)S(1)}, u32[]{:S(2)}, u32[]{:S(2)}) collective-permute-start(f32[32,1024]{1,0:T(8,128)S(1)} %fusion.10), channel_id=1, source_target_pairs={{0,8},{1,9},{2,10},{3,11},{4,12},{5,13},{6,14},{7,15},{8,0},{9,1},... | collective-permute-start | bytes 393224 | tf_op jit(solution)/shard_map/ppermute | solution.py:35
  55.6 1.9 %collective-permute-done.12 = f32[32,1024]{1,0:T(8,128)S(1)} collective-permute-done((f32[32,1024]{1,0:T(8,128)S(1)}, f32[32,1024]{1,0:T(8,128)S(1)}, u32[]{:S(2)}, u32[]{:S(2)}) %collective-permute-start.12) | collective-permute-done | bytes 131104 | tf_op jit(solution)/shard_map/ppermute | solution.py:35
  57.6 3.3 %collective-permute-done.11 = f32[32,1024]{1,0:T(8,128)S(1)} collective-permute-done((f32[32,1024]{1,0:T(8,128)S(1)}, f32[32,1024]{1,0:T(8,128)S(1)}, u32[]{:S(2)}, u32[]{:S(2)}) %collective-permute-start.11) | collective-permute-done | bytes 131104 | tf_op jit(solution)/shard_map/ppermute | solution.py:35
  60.9 1.9 %collective-permute-done.17 = f32[32,1024]{1,0:T(8,128)S(1)} collective-permute-done((f32[32,1024]{1,0:T(8,128)S(1)}, f32[32,1024]{1,0:T(8,128)S(1)}, u32[]{:S(2)}, u32[]{:S(2)}) %collective-permute-start.17) | collective-permute-done | bytes 131104 | tf_op jit(solution)/shard_map/ppermute | solution.py:35
  63.0 2.8 %collective-permute-start.20 = (f32[32,1024]{1,0:T(8,128)S(1)}, f32[32,1024]{1,0:T(8,128)S(1)}, u32[]{:S(2)}, u32[]{:S(2)}) collective-permute-start(f32[32,1024]{1,0:T(8,128)S(1)} %get-tuple-element.20), channel_id=1, source_target_pairs={{0,6},{1,7},{2,4},{3,5},{4,2},{5,3},{6,0},{7,1},{8,14},{9,15},{10,... | collective-permute-start | bytes 393224 | tf_op jit(solution)/shard_map/ppermute | solution.py:35
  66.9 3.3 %collective-permute-done.21 = f32[32,1024]{1,0:T(8,128)S(1)} collective-permute-done((f32[32,1024]{1,0:T(8,128)S(1)}, f32[32,1024]{1,0:T(8,128)S(1)}, u32[]{:S(2)}, u32[]{:S(2)}) %collective-permute-start.21) | collective-permute-done | bytes 131104 | tf_op jit(solution)/shard_map/ppermute | solution.py:35
  70.5 1.7 %collective-permute-start.23 = (f32[32,1024]{1,0:T(8,128)S(1)}, f32[32,1024]{1,0:T(8,128)S(1)}, u32[]{:S(2)}, u32[]{:S(2)}) collective-permute-start(f32[32,1024]{1,0:T(8,128)S(1)} %collective-permute-done.21), channel_id=1, source_target_pairs={{0,4},{1,5},{2,6},{3,7},{4,0},{5,1},{6,2},{7,3},{8,12},{9,13},{10,... | collective-permute-start | bytes 393224 | tf_op jit(solution)/shard_map/ppermute | solution.py:35
  74.5 1.9 %collective-permute-done.24 = f32[32,1024]{1,0:T(8,128)S(1)} collective-permute-done((f32[32,1024]{1,0:T(8,128)S(1)}, f32[32,1024]{1,0:T(8,128)S(1)}, u32[]{:S(2)}, u32[]{:S(2)}) %collective-permute-start.24) | collective-permute-done | bytes 131104 | tf_op jit(solution)/shard_map/ppermute | solution.py:35
  77.8 1.9 %collective-permute-done.26.refs_9_ = f32[4,32,1024]{2,1,0:T(8,128)S(1)} collective-permute-done((f32[4,32,1024]{2,1,0:T(8,128)S(1)}, f32[4,32,1024]{2,1,0:T(8,128)S(1)}, u32[]{:S(2)}, u32[]{:S(2)}) %collective-permute-start.26) | collective-permute-done | bytes 524320 | tf_op jit(solution)/shard_map/ppermute | solution.py:35
  79.7 17.0 %product.3 = (f32[4,32,1024]{2,1,0:T(8,128)S(1)}, f32[4,32,1024]{2,1,0:T(8,128)S(1)}, f32[4,32,1024]{2,1,0:T(8,128)S(1)}, f32[4,32,1024]{2,1,0:T(8,128)S(1)}) custom-call(s32[2,33]{1,0:T(2,128)S(1)} %bitcast.114, f32[33,512,512]{2,1,0:T(8,128)} %tiles.3, f32[1,32,1024]{2,1,0:T(8,128)S(1)} %bitcast.82, f32[1,32,1024]{2,1,0:T(8,128)S(1)} %bitcast.98, ...), custom_call_target="tpu_custom_call" | custom-call | flops 3321888768 | bytes 34603008 | tf_op jit(solution)/shard_map/product/pallas_call | solution.py:187
  106.3 3.3 %collective-permute-done.33 = f32[32,1024]{1,0:T(8,128)S(1)} collective-permute-done((f32[32,1024]{1,0:T(8,128)S(1)}, f32[32,1024]{1,0:T(8,128)S(1)}, u32[]{:S(2)}, u32[]{:S(2)}) %collective-permute-start.33) | collective-permute-done | bytes 131104 | tf_op jit(solution)/shard_map/ppermute | solution.py:35
  109.6 1.9 %collective-permute-start.35 = (f32[32,1024]{1,0:T(8,128)S(1)}, f32[32,1024]{1,0:T(8,128)S(1)}, u32[]{:S(2)}, u32[]{:S(2)}) collective-permute-start(f32[32,1024]{1,0:T(8,128)S(1)} %fusion.2), channel_id=1, source_target_pairs={{0,8},{1,9},{2,10},{3,11},{4,12},{5,13},{6,14},{7,15},{8,0},{9,1},... | collective-permute-start | bytes 393224 | tf_op jit(solution)/shard_map/ppermute | solution.py:35
  111.5 1.7 %collective-permute-done.30 = f32[32,1024]{1,0:T(8,128)S(1)} collective-permute-done((f32[32,1024]{1,0:T(8,128)S(1)}, f32[32,1024]{1,0:T(8,128)S(1)}, u32[]{:S(2)}, u32[]{:S(2)}) %collective-permute-start.30) | collective-permute-done | bytes 131104 | tf_op jit(solution)/shard_map/ppermute | solution.py:35
  113.3 3.6 %collective-permute-done.29 = f32[32,1024]{1,0:T(8,128)S(1)} collective-permute-done((f32[32,1024]{1,0:T(8,128)S(1)}, f32[32,1024]{1,0:T(8,128)S(1)}, u32[]{:S(2)}, u32[]{:S(2)}) %collective-permute-start.29) | collective-permute-done | bytes 131104 | tf_op jit(solution)/shard_map/ppermute | solution.py:35
  (75 shorter events, 32.1 us)
Async XLA Ops:
  1.7 8.4 %collective-permute-start.2 = (f32[32,1024]{1,0:T(8,128)S(1)}, f32[32,1024]{1,0:T(8,128)S(1)}, u32[]{:S(2)}, u32[]{:S(2)}) collective-permute-start(f32[32,1024]{1,0:T(8,128)S(1)} %sub.12), channel_id=1, source_target_pairs={{0,4},{1,5},{2,6},{3,7},{4,0},{5,1},{6,2},{7,3},{8,12},{9,13},{10,... | collective-permute-start | bytes 393224 | tf_op jit(solution)/shard_map/ppermute | solution.py:35
  4.8 8.7 %collective-permute-start = (f32[32,1024]{1,0:T(8,128)S(1)}, f32[32,1024]{1,0:T(8,128)S(1)}, u32[]{:S(2)}, u32[]{:S(2)}) collective-permute-start(f32[32,1024]{1,0:T(8,128)S(1)} %sub.12), channel_id=1, source_target_pairs={{0,8},{1,9},{2,10},{3,11},{4,12},{5,13},{6,14},{7,15},{8,0},{9,1},... | collective-permute-start | bytes 393224 | tf_op jit(solution)/shard_map/ppermute | solution.py:35
  7.4 9.6 %collective-permute-start.1 = (f32[32,1024]{1,0:T(8,128)S(1)}, f32[32,1024]{1,0:T(8,128)S(1)}, u32[]{:S(2)}, u32[]{:S(2)}) collective-permute-start(f32[32,1024]{1,0:T(8,128)S(1)} %sub.12), channel_id=1, source_target_pairs={{0,2},{1,3},{2,0},{3,1},{4,6},{5,7},{6,4},{7,5},{8,10},{9,11},{10,... | collective-permute-start | bytes 393224 | tf_op jit(solution)/shard_map/ppermute | solution.py:35
  10.1 7.0 %collective-permute-start.3 = (f32[32,1024]{1,0:T(8,128)S(1)}, f32[32,1024]{1,0:T(8,128)S(1)}, u32[]{:S(2)}, u32[]{:S(2)}) collective-permute-start(f32[32,1024]{1,0:T(8,128)S(1)} %collective-permute-done.2), channel_id=1, source_target_pairs={{0,2},{1,3},{2,0},{3,1},{4,6},{5,7},{6,4},{7,5},{8,10},{9,11},{10,... | collective-permute-start | bytes 393224 | tf_op jit(solution)/shard_map/ppermute | solution.py:35
  14.9 5.9 %collective-permute-start.5 = (f32[32,1024]{1,0:T(8,128)S(1)}, f32[32,1024]{1,0:T(8,128)S(1)}, u32[]{:S(2)}, u32[]{:S(2)}) collective-permute-start(f32[32,1024]{1,0:T(8,128)S(1)} %collective-permute-done), channel_id=1, source_target_pairs={{0,4},{1,5},{2,6},{3,7},{4,0},{5,1},{6,2},{7,3},{8,12},{9,13},{10,... | collective-permute-start | bytes 393224 | tf_op jit(solution)/shard_map/ppermute | solution.py:35
  44.2 6.4 %collective-permute-start.16 = (f32[32,1024]{1,0:T(8,128)S(1)}, f32[32,1024]{1,0:T(8,128)S(1)}, u32[]{:S(2)}, u32[]{:S(2)}) collective-permute-start(f32[32,1024]{1,0:T(8,128)S(1)} %get-tuple-element.32), channel_id=1, source_target_pairs={{0,4},{1,5},{2,6},{3,7},{4,0},{5,1},{6,2},{7,3},{8,12},{9,13},{10,... | collective-permute-start | bytes 393224 | tf_op jit(solution)/shard_map/ppermute | solution.py:35
  45.3 8.7 %collective-permute-start.15 = (f32[32,1024]{1,0:T(8,128)S(1)}, f32[32,1024]{1,0:T(8,128)S(1)}, u32[]{:S(2)}, u32[]{:S(2)}) collective-permute-start(f32[32,1024]{1,0:T(8,128)S(1)} %get-tuple-element.33), channel_id=1, source_target_pairs={{0,6},{1,7},{2,4},{3,5},{4,2},{5,3},{6,0},{7,1},{8,14},{9,15},{10,... | collective-permute-start | bytes 393224 | tf_op jit(solution)/shard_map/ppermute | solution.py:35
  46.9 8.7 %collective-permute-start.10 = (f32[32,1024]{1,0:T(8,128)S(1)}, f32[32,1024]{1,0:T(8,128)S(1)}, u32[]{:S(2)}, u32[]{:S(2)}) collective-permute-start(f32[32,1024]{1,0:T(8,128)S(1)} %get-tuple-element.28), channel_id=1, source_target_pairs={{0,2},{1,3},{2,0},{3,1},{4,6},{5,7},{6,4},{7,5},{8,10},{9,11},{10,... | collective-permute-start | bytes 393224 | tf_op jit(solution)/shard_map/ppermute | solution.py:35
  47.8 9.7 %collective-permute-start.12 = (f32[32,1024]{1,0:T(8,128)S(1)}, f32[32,1024]{1,0:T(8,128)S(1)}, u32[]{:S(2)}, u32[]{:S(2)}) collective-permute-start(f32[32,1024]{1,0:T(8,128)S(1)} %get-tuple-element.29), channel_id=1, source_target_pairs={{0,4},{1,5},{2,6},{3,7},{4,0},{5,1},{6,2},{7,3},{8,12},{9,13},{10,... | collective-permute-start | bytes 393224 | tf_op jit(solution)/shard_map/ppermute | solution.py:35
  49.0 11.9 %collective-permute-start.11 = (f32[32,1024]{1,0:T(8,128)S(1)}, f32[32,1024]{1,0:T(8,128)S(1)}, u32[]{:S(2)}, u32[]{:S(2)}) collective-permute-start(f32[32,1024]{1,0:T(8,128)S(1)} %get-tuple-element.30), channel_id=1, source_target_pairs={{0,6},{1,7},{2,4},{3,5},{4,2},{5,3},{6,0},{7,1},{8,14},{9,15},{10,... | collective-permute-start | bytes 393224 | tf_op jit(solution)/shard_map/ppermute | solution.py:35
  54.0 8.7 %collective-permute-start.17 = (f32[32,1024]{1,0:T(8,128)S(1)}, f32[32,1024]{1,0:T(8,128)S(1)}, u32[]{:S(2)}, u32[]{:S(2)}) collective-permute-start(f32[32,1024]{1,0:T(8,128)S(1)} %fusion.10), channel_id=1, source_target_pairs={{0,8},{1,9},{2,10},{3,11},{4,12},{5,13},{6,14},{7,15},{8,0},{9,1},... | collective-permute-start | bytes 393224 | tf_op jit(solution)/shard_map/ppermute | solution.py:35
  62.9 7.3 %collective-permute-start.21 = (f32[32,1024]{1,0:T(8,128)S(1)}, f32[32,1024]{1,0:T(8,128)S(1)}, u32[]{:S(2)}, u32[]{:S(2)}) collective-permute-start(f32[32,1024]{1,0:T(8,128)S(1)} %get-tuple-element.20), channel_id=1, source_target_pairs={{0,8},{1,9},{2,10},{3,11},{4,12},{5,13},{6,14},{7,15},{8,0},{9,1},... | collective-permute-start | bytes 393224 | tf_op jit(solution)/shard_map/ppermute | solution.py:35
  63.0 9.3 %collective-permute-start.20 = (f32[32,1024]{1,0:T(8,128)S(1)}, f32[32,1024]{1,0:T(8,128)S(1)}, u32[]{:S(2)}, u32[]{:S(2)}) collective-permute-start(f32[32,1024]{1,0:T(8,128)S(1)} %get-tuple-element.20), channel_id=1, source_target_pairs={{0,6},{1,7},{2,4},{3,5},{4,2},{5,3},{6,0},{7,1},{8,14},{9,15},{10,... | collective-permute-start | bytes 393224 | tf_op jit(solution)/shard_map/ppermute | solution.py:35
  65.8 7.9 %collective-permute-start.19 = (f32[32,1024]{1,0:T(8,128)S(1)}, f32[32,1024]{1,0:T(8,128)S(1)}, u32[]{:S(2)}, u32[]{:S(2)}) collective-permute-start(f32[32,1024]{1,0:T(8,128)S(1)} %get-tuple-element.20), channel_id=1, source_target_pairs={{0,4},{1,5},{2,6},{3,7},{4,0},{5,1},{6,2},{7,3},{8,12},{9,13},{10,... | collective-permute-start | bytes 393224 | tf_op jit(solution)/shard_map/ppermute | solution.py:35
  65.8 8.6 %collective-permute-start.18 = (f32[32,1024]{1,0:T(8,128)S(1)}, f32[32,1024]{1,0:T(8,128)S(1)}, u32[]{:S(2)}, u32[]{:S(2)}) collective-permute-start(f32[32,1024]{1,0:T(8,128)S(1)} %get-tuple-element.20), channel_id=1, source_target_pairs={{0,2},{1,3},{2,0},{3,1},{4,6},{5,7},{6,4},{7,5},{8,10},{9,11},{10,... | collective-permute-start | bytes 393224 | tf_op jit(solution)/shard_map/ppermute | solution.py:35
  70.2 6.2 %collective-permute-start.24 = (f32[32,1024]{1,0:T(8,128)S(1)}, f32[32,1024]{1,0:T(8,128)S(1)}, u32[]{:S(2)}, u32[]{:S(2)}) collective-permute-start(f32[32,1024]{1,0:T(8,128)S(1)} %collective-permute-done.21), channel_id=1, source_target_pairs={{0,6},{1,7},{2,4},{3,5},{4,2},{5,3},{6,0},{7,1},{8,14},{9,15},{10,... | collective-permute-start | bytes 393224 | tf_op jit(solution)/shard_map/ppermute | solution.py:35
  70.5 6.4 %collective-permute-start.23 = (f32[32,1024]{1,0:T(8,128)S(1)}, f32[32,1024]{1,0:T(8,128)S(1)}, u32[]{:S(2)}, u32[]{:S(2)}) collective-permute-start(f32[32,1024]{1,0:T(8,128)S(1)} %collective-permute-done.21), channel_id=1, source_target_pairs={{0,4},{1,5},{2,6},{3,7},{4,0},{5,1},{6,2},{7,3},{8,12},{9,13},{10,... | collective-permute-start | bytes 393224 | tf_op jit(solution)/shard_map/ppermute | solution.py:35
  98.9 6.0 %collective-permute-start.32 = (f32[32,1024]{1,0:T(8,128)S(1)}, f32[32,1024]{1,0:T(8,128)S(1)}, u32[]{:S(2)}, u32[]{:S(2)}) collective-permute-start(f32[32,1024]{1,0:T(8,128)S(1)} %get-tuple-element.25), channel_id=1, source_target_pairs={{0,2},{1,3},{2,0},{3,1},{4,6},{5,7},{6,4},{7,5},{8,10},{9,11},{10,... | collective-permute-start | bytes 393224 | tf_op jit(solution)/shard_map/ppermute | solution.py:35
  99.9 6.4 %collective-permute-start.34 = (f32[32,1024]{1,0:T(8,128)S(1)}, f32[32,1024]{1,0:T(8,128)S(1)}, u32[]{:S(2)}, u32[]{:S(2)}) collective-permute-start(f32[32,1024]{1,0:T(8,128)S(1)} %get-tuple-element.26), channel_id=1, source_target_pairs={{0,4},{1,5},{2,6},{3,7},{4,0},{5,1},{6,2},{7,3},{8,12},{9,13},{10,... | collective-permute-start | bytes 393224 | tf_op jit(solution)/shard_map/ppermute | solution.py:35
  101.2 8.4 %collective-permute-start.33 = (f32[32,1024]{1,0:T(8,128)S(1)}, f32[32,1024]{1,0:T(8,128)S(1)}, u32[]{:S(2)}, u32[]{:S(2)}) collective-permute-start(f32[32,1024]{1,0:T(8,128)S(1)} %get-tuple-element.27), channel_id=1, source_target_pairs={{0,6},{1,7},{2,4},{3,5},{4,2},{5,3},{6,0},{7,1},{8,14},{9,15},{10,... | collective-permute-start | bytes 393224 | tf_op jit(solution)/shard_map/ppermute | solution.py:35
  102.5 9.0 %collective-permute-start.28 = (f32[32,1024]{1,0:T(8,128)S(1)}, f32[32,1024]{1,0:T(8,128)S(1)}, u32[]{:S(2)}, u32[]{:S(2)}) collective-permute-start(f32[32,1024]{1,0:T(8,128)S(1)} %get-tuple-element.22), channel_id=1, source_target_pairs={{0,2},{1,3},{2,0},{3,1},{4,6},{5,7},{6,4},{7,5},{8,10},{9,11},{10,... | collective-permute-start | bytes 393224 | tf_op jit(solution)/shard_map/ppermute | solution.py:35
  103.5 9.7 %collective-permute-start.30 = (f32[32,1024]{1,0:T(8,128)S(1)}, f32[32,1024]{1,0:T(8,128)S(1)}, u32[]{:S(2)}, u32[]{:S(2)}) collective-permute-start(f32[32,1024]{1,0:T(8,128)S(1)} %get-tuple-element.23), channel_id=1, source_target_pairs={{0,4},{1,5},{2,6},{3,7},{4,0},{5,1},{6,2},{7,3},{8,12},{9,13},{10,... | collective-permute-start | bytes 393224 | tf_op jit(solution)/shard_map/ppermute | solution.py:35
  104.9 12.0 %collective-permute-start.29 = (f32[32,1024]{1,0:T(8,128)S(1)}, f32[32,1024]{1,0:T(8,128)S(1)}, u32[]{:S(2)}, u32[]{:S(2)}) collective-permute-start(f32[32,1024]{1,0:T(8,128)S(1)} %get-tuple-element.24), channel_id=1, source_target_pairs={{0,6},{1,7},{2,4},{3,5},{4,2},{5,3},{6,0},{7,1},{8,14},{9,15},{10,... | collective-permute-start | bytes 393224 | tf_op jit(solution)/shard_map/ppermute | solution.py:35
  109.6 7.2 %collective-permute-start.35 = (f32[32,1024]{1,0:T(8,128)S(1)}, f32[32,1024]{1,0:T(8,128)S(1)}, u32[]{:S(2)}, u32[]{:S(2)}) collective-permute-start(f32[32,1024]{1,0:T(8,128)S(1)} %fusion.2), channel_id=1, source_target_pairs={{0,8},{1,9},{2,10},{3,11},{4,12},{5,13},{6,14},{7,15},{8,0},{9,1},... | collective-permute-start | bytes 393224 | tf_op jit(solution)/shard_map/ppermute | solution.py:35
  (16 other events, 235.8 us)
